TPU v7x, 128 devices: a whole 4x4x4 slice. The times are simulated.
128 devices in a mesh: blk: 32 (over y_lo, x, z), dp: 4 (over y_hi, core).
Axes of the slice: x: 4, y: 4 (y_hi: 2, y_lo: 2; y = y_hi * 2 + y_lo), z: 4, core: 2. Of those that a mesh axis runs over, the one named last changes fastest.
Arguments:
- embeddings: bfloat16 [20480, 4096], P(('dp', 'blk')), parts along dimension 0, may hold values from -1 to 1
- partner: int32 [20480], P(('dp', 'blk')), parts along dimension 0, may hold values from 0 to 5119, as said below
- logit_scale: float32 [1], replicated, may hold values from 10 to 320
Outputs:
- grad: bfloat16 [20480, 4096], P(('dp', 'blk')), parts along dimension 0
- loss: float32 [4], P('dp'), parts along dimension 0
There are 4 independent parts, one for each index of `dp`. A program takes and returns all parts, laid end to end along the dimension named above; an argument that names none is the same for every part. Nothing has to cross between parts.
Inputs may be any that keep to these rules, and one draw needn't show every extreme that they name: partner pairs the rows: partner[partner[i]] = i and partner[i] != i.
All inputs are finite; a program needn't handle non-finite values.
Results may differ from a plain program's by a relative error of at most 0.0019.
The roundings to bfloat16 on the way count: a program that leaves them out, or rounds other values in their place, can miss the bound.
Values may be sent and summed in bfloat16 or wider, within the bound.
No kernel may reach another device: no remote copies, remote signals or barrier semaphores. Data moves between devices by JAX's collectives and lax.ppermute only.
A program may use at most 128 MiB of HBM per device.

v0:
```python
import jax
import jax.numpy as jnp
from jax import lax
from jax.sharding import PartitionSpec as P


def scores_of(left, right, multiplier):
    return multiplier * lax.dot_general(
        left, right, (((1,), (1,)), ((), ())), preferred_element_type=jnp.float32
    )


def local(embeddings, partner, logit_scale):
    rows = embeddings.shape[0]
    total = rows * lax.axis_size("blk")
    wide = embeddings.astype(jnp.float32)
    factor = lax.rsqrt(jnp.sum(wide * wide, axis=1, keepdims=True) + 1e-06)
    unit = (wide * factor).astype(jnp.bfloat16)
    multiplier = logit_scale[0]
    gathered = lax.all_gather(unit, "blk", axis=0, tiled=True)
    slab = scores_of(unit, gathered, multiplier)
    first = lax.axis_index("blk") * rows
    row_ids = first + lax.broadcasted_iota(jnp.int32, (rows, 1), 0)
    col_ids = lax.broadcasted_iota(jnp.int32, (1, total), 1)
    diagonal = row_ids == col_ids
    masked = jnp.where(diagonal, jnp.float32(-1e30), slab)
    highest = jnp.max(masked, axis=1)
    lse = highest + jnp.log(jnp.sum(jnp.exp(masked - highest[:, None]), axis=1))
    onehot = col_ids == partner[:, None]
    positive = jnp.sum(jnp.where(onehot, slab, jnp.float32(0.0)), axis=1)
    lse_all = lax.all_gather(lse, "blk", axis=0, tiled=True)
    summed = lax.psum(jnp.sum(lse - positive), "blk")
    loss = (summed / total).reshape(1)
    own = jnp.exp(masked - lse[:, None])
    other = jnp.exp(masked - lse_all[None, :])
    weights = (own + other - 2.0 * onehot.astype(jnp.float32)).astype(jnp.bfloat16)
    grad_unit = multiplier * jnp.dot(weights, gathered, preferred_element_type=jnp.float32)
    inner = jnp.sum(wide * grad_unit, axis=1, keepdims=True)
    grad = (factor * grad_unit - factor * factor * factor * inner * wide).astype(jnp.bfloat16)
    return (grad, loss)


def solution(mesh):
    return jax.shard_map(
        local,
        mesh=mesh,
        in_specs=(P(("dp", "blk"), None), P(("dp", "blk")), P()),
        out_specs=(P(("dp", "blk"), None), P("dp")),
        check_vma=False,
    )
```

profile of v0, /device:TPU:0, one launch (start us, length us, event | category | flops | bytes accessed | tf_op | source)
XLA Modules:
  0.0 677.4 jit_solution(13987993018097458942)
XLA Ops:
  7.2 0.0 copy-start.2
  7.2 0.0 all-gather.2.cloned.1.call-start
  7.2 1.7 fusion.1
  8.9 2.7 fusion.2
  11.6 0.0 all-gather.2.cloned.1.call-update
  12.3 0.0 copy-done.2
  12.3 0.6 dynamic-slice
  13.6 452.6 %all-gather.2.cloned.1.call-done = bf16[5120,4096]{1,0:T(8,128)(2,1)} async-done(((bf16[160,4096]{1,0:T(8,128)(2,1)}), bf16[5120,4096]{1,0:T(8,128)(2,1)}) %all-gather.2.cloned.1.call-update) | async-done | bytes 41943056 | tf_op jit(solution)/shard_map/all_gather | solution.py:20
  466.2 0.0 copy-start.1
  466.2 21.8 %fusion.6 = (f32[160]{0:T(256)S(1)}, f32[160,5120]{1,0:T(8,128)}) fusion(s32[160]{0:T(256)S(1)} %iota_add_fusion, bf16[160,4096]{1,0:T(8,128)(2,1)} %fusion.2, bf16[5120,4096]{1,0:T(8,128)(2,1)} %all-gather.2.cloned.1.call-done, f32[]{:T(128)} %bitcast.7), kind=kOutput, calls=%fused_computation.17 | convolution fusion | flops 6714163200 | bytes 46531844 | tf_op jit(solution)/shard_map/dot_general | solution.py:8
  488.0 0.0 copy-start
  488.0 0.0 copy-done.1
  488.0 3.8 select_reduce_fusion
  491.8 0.6 subtract_reduce_fusion
  492.5 0.2 dynamic-update-slice
  492.6 152.8 %all-reduce.1 = (f32[5120]{0:T(1024)S(1)}, f32[]{:T(128)}) all-reduce(f32[5120]{0:T(1024)S(1)} %dynamic-update-slice, f32[]{:T(128)} %get-tuple-element.6), channel_id=1, replica_groups=mesh['blk'=32,'dp'=4] {'blk'}, use_global_device_ids=true, to_apply=%add | all-reduce | flops 5121 | bytes 40968
  645.5 0.0 copy-done
  645.5 19.9 %fusion.3 = (f32[160]{0:T(256)S(1)}, f32[160,4096]{1,0:T(8,128)}) fusion(bf16[160,4096]{1,0:T(8,128)(2,1)S(1)} %copy-done, bf16[5120,4096]{1,0:T(8,128)(2,1)} %all-gather.2.cloned.1.call-done, f32[160,5120]{1,0:T(8,128)} %get-tuple-element.9, s32[160]{0:T(256)S(1)} %copy-done.1, f32[5120]{0:T(1024)S(1)} %get-tuple-element.4, f32[160]{0:T(256)S(1)} %get-tuple-element.7, ...), kind=kOutput, calls=%fused_computation.14 | convolution fusion | flops 6720880640 | bytes 49175044 | tf_op jit(solution)/shard_map/dot_general | solution.py:37
  666.0 3.4 fusion.5
  (4 shorter events, 0.0 us)
Async XLA Ops:
  7.2 5.1 copy-start.2
  7.2 459.0 %all-gather.2.cloned.1.call-start = ((), (), s32[]{:S(2)}) async-start(), calls=%async_computation | async-start | bytes 43253760 | tf_op jit(solution)/shard_map/all_gather | solution.py:20
  466.2 21.8 %copy-start.1 = (s32[160]{0:T(256)S(1)}, s32[160]{0:T(256)}, u32[]{:S(2)}) copy-start(s32[160]{0:T(256)} %param.4) | copy-start | bytes 1924
  488.0 157.4 %copy-start = (bf16[160,4096]{1,0:T(8,128)(2,1)S(1)}, bf16[160,4096]{1,0:T(8,128)(2,1)}, u32[]{:S(2)}) copy-start(bf16[160,4096]{1,0:T(8,128)(2,1)} %param.3) | copy-start | bytes 3932164
Sparse Core Ops, SparseCore 0:
  11.7 454.4 all-gather.1
where the time goes:
time: 678 us; the launch traced here: 677 us
  waiting for transfers between devices  453 us (67%)
  blocking collectives  153 us (23%)
  matrix products  41.7 us (6%)
  between operations  17.1 us (3%)
  other arithmetic  12.2 us (2%)
    all_gather x1, waiting for transfers between devices, local(): gathered = lax.all_gather(unit, 'blk', axis=0, tiled=True)  453 us
    unnamed x1, blocking collectives  153 us
    dot_general x1, matrix products, scores_of(): lax.dot_general(left, right, (((1,), (1,)), ((), ())), preferred_element_...  21.8 us
    dot_general x1, matrix products, local(): jnp.dot(weights, gathered, preferred_element_type=jnp.float32)  19.9 us
  transfers between devices with their start and end apart: 1, of which 1 were waited for; matrix products, arithmetic and copies ran while one was open for 0% of the time, Pallas kernels for 0%

commit v1 on v0

v1 whole, which is shorter than its diff:
```python
import jax
import jax.numpy as jnp
from jax import lax
from jax.sharding import Mesh, PartitionSpec as P

X, Z = 4, 4


def ring(n, step):
    return [(i, (i + step) % n) for i in range(n)]


SWAP = [(0, 0), (1, 2), (2, 1), (3, 3)]
SWAP_OTHER = [(1, 0), (3, 1), (0, 2), (2, 3)]


def swap(v):
    return lax.ppermute(v, ("yl", "c"), SWAP)


def other_core(v):
    return lax.ppermute(v, "c", ring(2, 1))


def gather_ring(u, axis):
    half = u.shape[0] // 2
    down = lax.ppermute(u, axis, ring(4, 1))
    up = lax.ppermute(u, axis, ring(4, -1))
    first = lax.ppermute(down[:half], axis, ring(4, 1))
    second = lax.ppermute(up[half:], axis, ring(4, -1))
    return [u, up, jnp.concatenate([first, second], 0), down]


def gather_small(v, axis):
    return [v] + [lax.ppermute(v, axis, ring(4, -k)) for k in (1, 2, 3)]


def scatter_ring(parts, axis):
    half = parts[0].shape[0] // 2
    t1 = lax.ppermute(parts[2][:half], axis, ring(4, 1))
    t2 = lax.ppermute(parts[2][half:], axis, ring(4, -1))
    d1 = lax.ppermute(parts[1][half:], axis, ring(4, 1))
    d3 = lax.ppermute(parts[3][:half], axis, ring(4, -1))
    s1 = lax.ppermute(t1 + parts[1][:half], axis, ring(4, 1))
    s3 = lax.ppermute(t2 + parts[3][half:], axis, ring(4, -1))
    return jnp.concatenate([parts[0][:half] + s1 + d3, parts[0][half:] + s3 + d1], 0)


def local(embeddings, partner, logit_scale):
    rows, width = embeddings.shape
    half = width // 2
    total = rows * 2 * X * Z
    multiplier = logit_scale[0]
    c, x, z = lax.axis_index("c"), lax.axis_index("x"), lax.axis_index("z")

    emb = swap(embeddings)
    mate = swap(partner.reshape(1, rows))
    wide = emb.astype(jnp.float32)
    factor = lax.rsqrt(jnp.sum(wide * wide, axis=1, keepdims=True) + 1e-06)
    unit = (wide * factor).astype(jnp.bfloat16)

    a_own = gather_ring(unit, "z")
    b_own = gather_ring(unit, "x")
    b_other = [other_core(v) for v in b_own]
    a_other = [other_core(v[:, half:]) for v in a_own]
    mates = jnp.concatenate(gather_small(mate, "z"), 1).reshape(-1, 1)

    a_rows = jnp.concatenate(a_own, 0)
    b_rows = jnp.concatenate(b_own + b_other, 0)
    scores = multiplier * lax.dot_general(
        a_rows, b_rows, (((1,), (1,)), ((), ())), preferred_element_type=jnp.float32
    )
    within = jnp.arange(rows, dtype=jnp.int32)
    row_ids = jnp.concatenate(
        [((c * X + x) * Z + (z + k) % Z) * rows + within for k in range(4)]
    ).reshape(-1, 1)
    col_ids = jnp.concatenate(
        [((cc * X + (x + k) % X) * Z + z) * rows + within for cc in (c, 1 - c) for k in range(4)]
    ).reshape(1, -1)
    onehot = col_ids == mates
    masked = jnp.where(row_ids == col_ids, jnp.float32(-1e30), scores)
    top = jnp.max(masked, axis=1)
    low = jnp.sum(jnp.exp(masked - top[:, None]), axis=1)
    pos = jnp.sum(jnp.where(onehot, scores, jnp.float32(0.0)), axis=1)
    stats = jnp.stack(gather_small(jnp.stack([top, low, pos]), "z"))
    stats = stats.reshape(4, 3, 4, rows)
    stats = jnp.stack([jnp.roll(stats[s], s, axis=1) for s in range(4)]).reshape(4, 3, -1)
    highest = jnp.max(stats[:, 0], axis=0)
    lse = highest + jnp.log(jnp.sum(stats[:, 1] * jnp.exp(stats[:, 0] - highest), axis=0))
    positive = jnp.sum(stats[:, 2], axis=0)

    own = lse[:rows].reshape(1, rows)
    lse_own = gather_small(own, "x")
    lse_cols = jnp.concatenate(lse_own + [other_core(v) for v in lse_own], 1)
    weights = (
        jnp.exp(masked - lse[:, None])
        + jnp.exp(masked - lse_cols)
        - 2.0 * onehot.astype(jnp.float32)
    ).astype(jnp.bfloat16)

    near, far = weights[:, : 4 * rows], weights[:, 4 * rows :]
    far = other_core(far)
    g_z = jnp.dot(weights, b_rows[:, :half], preferred_element_type=jnp.float32)
    a_half = jnp.concatenate([v[:, half:] for v in a_own] + a_other, 0)
    g_x = lax.dot_general(
        jnp.concatenate([near, far], 0), a_half, (((0,), (0,)), ((), ())),
        preferred_element_type=jnp.float32,
    )
    cut = lambda g: [g[k * rows : (k + 1) * rows] for k in range(4)]
    sum_z = scatter_ring(cut(g_z), "z")
    sum_x = scatter_ring(cut(g_x), "x")
    grad_unit = multiplier * jnp.concatenate([sum_z, sum_x], 1)
    inner = jnp.sum(wide * grad_unit, axis=1, keepdims=True)
    grad = (factor * grad_unit - factor * factor * factor * inner * wide).astype(jnp.bfloat16)

    part = jnp.sum(lse - positive).reshape(1, 1)
    part = sum(gather_small(part, "x"))
    both = swap(part) + lax.ppermute(part, ("yl", "c"), SWAP_OTHER)
    return swap(grad), (both / total).reshape(1)


def solution(mesh):
    fine = Mesh(
        mesh.devices.reshape(2, X, Z, 2, 2), ("yl", "x", "z", "yh", "c")
    )
    rows = ("yh", "c", "yl", "x", "z")
    return jax.shard_map(
        local,
        mesh=fine,
        in_specs=(P(rows, None), P(rows), P()),
        out_specs=(P(rows, None), P(("yh", "c"))),
        check_vma=False,
    )
```

time: 678 us -> 244 us (0.36)
  the two profiles are of different devices: /device:TPU:0 before, /device:TPU:1 now
where the time goes in v1:
time: 244 us; the launch traced here: 243 us
  waiting for transfers between devices  107 us (44%)
  starting transfers between devices  72.2 us (30%)
  local copies, waits for them, and re-layouts  26.9 us (11%)
  matrix products  20.6 us (8%)
  other arithmetic  9.49 us (4%)
  between operations  6.78 us (3%)
    ppermute x4, starting transfers between devices, swap(): return lax.ppermute(v, ('yl', 'c'), SWAP)  24.7 us
    ppermute x12, waiting for transfers between devices, gather_small(): return [v] + [lax.ppermute(v, axis, ring(4, -k)) for k in (1, 2, 3)]  21.6 us
    unnamed x29, local copies, waits for them, and re-layouts  14.8 us
    ppermute x2, waiting for transfers between devices, scatter_ring(): t1 = lax.ppermute(parts[2][:half], axis, ring(4, 1))  14.4 us
    ppermute x4, waiting for transfers between devices, swap(): return lax.ppermute(v, ('yl', 'c'), SWAP)  13.8 us
    ppermute x2, waiting for transfers between devices, scatter_ring(): t2 = lax.ppermute(parts[2][half:], axis, ring(4, -1))  12.8 us
    ppermute x12, starting transfers between devices, gather_small(): return [v] + [lax.ppermute(v, axis, ring(4, -k)) for k in (1, 2, 3)]  12.4 us
    dot_general x1, matrix products, local(): lax.dot_general(a_rows, b_rows, (((1,), (1,)), ((), ())), preferred_eleme...  11.3 us
  transfers between devices with their start and end apart: 50, of which 24 were waited for; matrix products, arithmetic and copies ran while one was open for 18% of the time, Pallas kernels for 0%

profile of v1, /device:TPU:1, one launch (start us, length us, event | category | flops | bytes accessed | tf_op | source)
XLA Modules:
  0.0 243.0 jit_solution(1577313630664963774)
XLA Ops:
  0.6 4.6 %collective-permute-start = (bf16[160,4096]{1,0:T(8,128)(2,1)}, bf16[160,4096]{1,0:T(8,128)(2,1)S(1)}, u32[]{:S(2)}, u32[]{:S(2)}) collective-permute-start(bf16[160,4096]{1,0:T(8,128)(2,1)} %param.3), channel_id=1, source_target_pairs={{0,0},{1,64},{64,1},{65,65},{2,2},{3,66},{66,3},{67,67},{4,4},{5,6... | collective-permute-start | bytes 3932168 | tf_op jit(solution)/shard_map/ppermute | solution.py:18
  7.4 13.8 %collective-permute-done = bf16[160,4096]{1,0:T(8,128)(2,1)S(1)} collective-permute-done((bf16[160,4096]{1,0:T(8,128)(2,1)}, bf16[160,4096]{1,0:T(8,128)(2,1)S(1)}, u32[]{:S(2)}, u32[]{:S(2)}) %collective-permute-start) | collective-permute-done | bytes 1310752 | tf_op jit(solution)/shard_map/ppermute | solution.py:18
  25.5 3.8 %collective-permute-start.1 = (bf16[160,4096]{1,0:T(8,128)(2,1)S(1)}, bf16[160,4096]{1,0:T(8,128)(2,1)}, u32[]{:S(2)}, u32[]{:S(2)}) collective-permute-start(bf16[160,4096]{1,0:T(8,128)(2,1)S(1)} %get-tuple-element.9), channel_id=1, source_target_pairs={{0,12},{4,0},{8,4},{12,8},{1,13},{5,1},{9,5},{13,9},{2,14},{6,2},{... | collective-permute-start | bytes 3932168 | tf_op jit(solution)/shard_map/ppermute | solution.py:28
  32.0 11.9 %collective-permute-done.14 = s32[1,160]{1,0:T(1,128)S(1)} collective-permute-done((s32[1,160]{1,0:T(1,128)S(1)}, s32[1,160]{1,0:T(1,128)S(1)}, u32[]{:S(2)}, u32[]{:S(2)}) %collective-permute-start.14) | collective-permute-done | bytes 672 | tf_op jit(solution)/shard_map/ppermute | solution.py:35
  65.2 7.0 %collective-permute-done.7 = bf16[80,4096]{1,0:T(8,128)(2,1)S(1)} collective-permute-done((bf16[80,4096]{1,0:T(8,128)(2,1)S(1)}, bf16[80,4096]{1,0:T(8,128)(2,1)S(1)}, u32[]{:S(2)}, u32[]{:S(2)}) %collective-permute-start.7) | collective-permute-done | bytes 655392 | tf_op jit(solution)/shard_map/ppermute | solution.py:29
  78.4 9.3 %collective-permute-done.4 = bf16[80,4096]{1,0:T(8,128)(2,1)S(1)} collective-permute-done((bf16[80,4096]{1,0:T(8,128)(2,1)S(1)}, bf16[80,4096]{1,0:T(8,128)(2,1)S(1)}, u32[]{:S(2)}, u32[]{:S(2)}) %collective-permute-start.4) | collective-permute-done | bytes 655392 | tf_op jit(solution)/shard_map/ppermute | solution.py:30
  96.9 3.8 %copy-done.3 = bf16[1280,4096]{1,0:T(8,128)(2,1)} copy-done((bf16[1280,4096]{1,0:T(8,128)(2,1)}, bf16[1280,4096]{1,0:T(8,128)(2,1)S(1)}, u32[]{:S(2)}) %copy-start.3) | copy-done | bytes 10485784
  100.7 11.3 %fusion.10 = (f32[640]{0:T(1024)S(1)}, f32[640,1280]{1,0:T(8,128)S(1)}) fusion(s32[1280]{0:T(1024)S(1)} %concatenate.55, s32[640]{0:T(1024)S(1)} %pad_add_fusion, bf16[640,4096]{1,0:T(8,128)(2,1)} %copy-done.1, bf16[1280,4096]{1,0:T(8,128)(2,1)} %copy-done.3, f32[]{:T(128)} %bitcast.25), kind=kOutput, calls=%fused_computation.20 | convolution fusion | flops 6714162688 | bytes 19015684 | tf_op jit(solution)/shard_map/dot_general | solution.py:70
  114.9 2.9 %collective-permute-start.17 = (f32[3,640]{1,0:T(4,128)S(1)}, f32[3,640]{1,0:T(4,128)S(1)}, u32[]{:S(2)}, u32[]{:S(2)}) collective-permute-start(f32[3,640]{1,0:T(4,128)S(1)} %get-tuple-element.37), channel_id=1, source_target_pairs={{0,12},{4,0},{8,4},{12,8},{1,13},{5,1},{9,5},{13,9},{2,14},{6,2},{... | collective-permute-start | bytes 23048 | tf_op jit(solution)/shard_map/ppermute | solution.py:35
  119.4 3.0 %collective-permute-done.19 = f32[3,640]{1,0:T(4,128)S(1)} collective-permute-done((f32[3,640]{1,0:T(4,128)S(1)}, f32[3,640]{1,0:T(4,128)S(1)}, u32[]{:S(2)}, u32[]{:S(2)}) %collective-permute-start.19) | collective-permute-done | bytes 7712 | tf_op jit(solution)/shard_map/ppermute | solution.py:35
  129.1 2.9 %collective-permute-start.25 = (f32[1,160]{1,0:T(1,128)S(1)}, f32[1,160]{1,0:T(1,128)S(1)}, u32[]{:S(2)}, u32[]{:S(2)}) collective-permute-start(f32[1,160]{1,0:T(1,128)S(1)} %collective-permute-done.21), channel_id=1, source_target_pairs={{0,1},{1,0},{2,3},{3,2},{4,5},{5,4},{6,7},{7,6},{8,9},{9,8},{10,11... | collective-permute-start | bytes 1928 | tf_op jit(solution)/shard_map/ppermute | solution.py:22
  133.3 3.0 %fusion.4 = bf16[640,1280]{1,0:T(8,128)(2,1)S(1)} fusion(f32[640,1280]{1,0:T(8,128)} %copy-done, f32[1280]{0:T(1024)S(1)} %reduce.3, f32[640]{0:T(1024)S(1)} %get-tuple-element.5, s32[1280]{0:T(1024)S(1)} %concatenate.55, s32[640]{0:T(1024)S(1)} %add_reduce_fusion, s32[640]{0:T(1024)S(1)} %pad_add_fusion), kind=kLoop, calls=%fused_computation.11 | loop fusion | flops 7372800 | bytes 4933120 | tf_op jit(solution)/shard_map/convert_element_type | solution.py:99
  136.9 5.7 %fusion = f32[640,2048]{1,0:T(8,128)S(1)} fusion(bf16[640,1280]{1,0:T(8,128)(2,1)S(1)} %fusion.4, bf16[1280,4096]{1,0:T(8,128)(2,1)} %copy-done.3), kind=kOutput, calls=%fused_computation | convolution fusion | flops 3355443200 | bytes 12124160 | tf_op jit(solution)/shard_map/dot_general | solution.py:103
  142.7 3.6 %fusion.11 = f32[640,2048]{1,0:T(8,128)S(1)} fusion(bf16[1280,2048]{1,0:T(8,128)(2,1)S(1)} %bitcast.28, bf16[640,640]{1,0:T(8,128)(2,1)S(1)} %collective-permute-done.33, bf16[640,640]{1,0:T(8,128)(2,1)S(1)} %get-tuple-element.24), kind=kOutput, calls=%fused_computation.21 | convolution fusion | flops 3358720000 | bytes 12124160 | tf_op jit(solution)/shard_map/dot_general | solution.py:105
  146.5 13.6 %collective-permute-done.27 = f32[80,2048]{1,0:T(8,128)S(1)} collective-permute-done((f32[80,2048]{1,0:T(8,128)S(1)}, f32[80,2048]{1,0:T(8,128)S(1)}, u32[]{:S(2)}, u32[]{:S(2)}) %collective-permute-start.27) | collective-permute-done | bytes 655392 | tf_op jit(solution)/shard_map/ppermute | solution.py:40
  166.8 10.0 %collective-permute-done.28 = f32[80,2048]{1,0:T(8,128)S(1)} collective-permute-done((f32[80,2048]{1,0:T(8,128)S(1)}, f32[80,2048]{1,0:T(8,128)S(1)}, u32[]{:S(2)}, u32[]{:S(2)}) %collective-permute-start.28) | collective-permute-done | bytes 655392 | tf_op jit(solution)/shard_map/ppermute | solution.py:44
  177.1 12.7 %collective-permute-done.30 = f32[80,2048]{1,0:T(8,128)S(1)} collective-permute-done((f32[80,2048]{1,0:T(8,128)S(1)}, f32[80,2048]{1,0:T(8,128)S(1)}, u32[]{:S(2)}, u32[]{:S(2)}) %collective-permute-start.30) | collective-permute-done | bytes 655392 | tf_op jit(solution)/shard_map/ppermute | solution.py:41
  190.1 3.5 %collective-permute-start.31 = (f32[80,2048]{1,0:T(8,128)S(1)}, f32[80,2048]{1,0:T(8,128)S(1)}, u32[]{:S(2)}, u32[]{:S(2)}) collective-permute-start(f32[80,2048]{1,0:T(8,128)S(1)} %get-tuple-element.14), channel_id=1, source_target_pairs={{0,12},{4,0},{8,4},{12,8},{1,13},{5,1},{9,5},{13,9},{2,14},{6,2},{... | collective-permute-start | bytes 1966088 | tf_op jit(solution)/shard_map/ppermute | solution.py:45
  194.0 3.4 %collective-permute-start.42 = (f32[80,2048]{1,0:T(8,128)S(1)}, f32[80,2048]{1,0:T(8,128)S(1)}, u32[]{:S(2)}, u32[]{:S(2)}) collective-permute-start(f32[80,2048]{1,0:T(8,128)S(1)} %get-tuple-element.20), channel_id=1, source_target_pairs={{0,48},{16,0},{32,16},{48,32},{1,49},{17,1},{33,17},{49,33},{2,50}... | collective-permute-start | bytes 1966088 | tf_op jit(solution)/shard_map/ppermute | solution.py:45
  197.4 8.1 %collective-permute-done.31 = f32[80,2048]{1,0:T(8,128)S(1)} collective-permute-done((f32[80,2048]{1,0:T(8,128)S(1)}, f32[80,2048]{1,0:T(8,128)S(1)}, u32[]{:S(2)}, u32[]{:S(2)}) %collective-permute-start.31) | collective-permute-done | bytes 655392 | tf_op jit(solution)/shard_map/ppermute | solution.py:45
  205.4 3.1 %collective-permute-done.32 = f32[80,2048]{1,0:T(8,128)S(1)} collective-permute-done((f32[80,2048]{1,0:T(8,128)S(1)}, f32[80,2048]{1,0:T(8,128)S(1)}, u32[]{:S(2)}, u32[]{:S(2)}) %collective-permute-start.32) | collective-permute-done | bytes 655392 | tf_op jit(solution)/shard_map/ppermute | solution.py:42
  209.2 3.1 %collective-permute-done.43 = f32[80,2048]{1,0:T(8,128)S(1)} collective-permute-done((f32[80,2048]{1,0:T(8,128)S(1)}, f32[80,2048]{1,0:T(8,128)S(1)}, u32[]{:S(2)}, u32[]{:S(2)}) %collective-permute-start.43) | collective-permute-done | bytes 655392 | tf_op jit(solution)/shard_map/ppermute | solution.py:42
  213.6 9.1 %collective-permute-start.44 = (bf16[160,4096]{1,0:T(8,128)(2,1)S(1)}, bf16[160,4096]{1,0:T(8,128)(2,1)S(1)}, u32[]{:S(2)}, u32[]{:S(2)}) collective-permute-start(bf16[160,4096]{1,0:T(8,128)(2,1)S(1)} %fusion.9), channel_id=1, source_target_pairs={{0,0},{1,64},{64,1},{65,65},{2,2},{3,66},{66,3},{67,67},{4,4},{5,6... | collective-permute-start | bytes 3932168 | tf_op jit(solution)/shard_map/ppermute | solution.py:18
  228.2 9.1 %collective-permute-start.48 = (f32[1,1]{1,0:T(1,128)}, f32[1,1]{1,0:T(1,128)}, u32[]{:S(2)}, u32[]{:S(2)}) collective-permute-start(f32[1,1]{1,0:T(1,128)} %add.337), channel_id=1, source_target_pairs={{0,0},{1,64},{64,1},{65,65},{2,2},{3,66},{66,3},{67,67},{4,4},{5,6... | collective-permute-start | bytes 20 | tf_op jit(solution)/shard_map/ppermute | solution.py:18
  (170 shorter events, 74.0 us)
Async XLA Ops:
  0.6 20.5 %collective-permute-start = (bf16[160,4096]{1,0:T(8,128)(2,1)}, bf16[160,4096]{1,0:T(8,128)(2,1)S(1)}, u32[]{:S(2)}, u32[]{:S(2)}) collective-permute-start(bf16[160,4096]{1,0:T(8,128)(2,1)} %param.3), channel_id=1, source_target_pairs={{0,0},{1,64},{64,1},{65,65},{2,2},{3,66},{66,3},{67,67},{4,4},{5,6... | collective-permute-start | bytes 3932168 | tf_op jit(solution)/shard_map/ppermute | solution.py:18
  5.2 24.1 %collective-permute-start.13 = (s32[1,160]{1,0:T(1,128)}, s32[1,160]{1,0:T(1,128)S(1)}, u32[]{:S(2)}, u32[]{:S(2)}) collective-permute-start(s32[1,160]{1,0:T(1,128)} %bitcast.35), channel_id=1, source_target_pairs={{0,0},{1,64},{64,1},{65,65},{2,2},{3,66},{66,3},{67,67},{4,4},{5,6... | collective-permute-start | bytes 1928 | tf_op jit(solution)/shard_map/ppermute | solution.py:18
  23.1 31.4 %collective-permute-start.5 = (bf16[160,4096]{1,0:T(8,128)(2,1)S(1)}, bf16[160,4096]{1,0:T(8,128)(2,1)}, u32[]{:S(2)}, u32[]{:S(2)}) collective-permute-start(bf16[160,4096]{1,0:T(8,128)(2,1)S(1)} %get-tuple-element.9), channel_id=1, source_target_pairs={{0,48},{16,0},{32,16},{48,32},{1,49},{17,1},{33,17},{49,33},{2,50}... | collective-permute-start | bytes 3932168 | tf_op jit(solution)/shard_map/ppermute | solution.py:28
  25.5 26.8 %collective-permute-start.6 = (bf16[160,4096]{1,0:T(8,128)(2,1)S(1)}, bf16[160,4096]{1,0:T(8,128)(2,1)}, u32[]{:S(2)}, u32[]{:S(2)}) collective-permute-start(bf16[160,4096]{1,0:T(8,128)(2,1)S(1)} %get-tuple-element.9), channel_id=1, source_target_pairs={{0,16},{16,32},{32,48},{48,0},{1,17},{17,33},{33,49},{49,1},{2,18}... | collective-permute-start | bytes 3932168 | tf_op jit(solution)/shard_map/ppermute | solution.py:27
  25.5 34.4 %collective-permute-start.1 = (bf16[160,4096]{1,0:T(8,128)(2,1)S(1)}, bf16[160,4096]{1,0:T(8,128)(2,1)}, u32[]{:S(2)}, u32[]{:S(2)}) collective-permute-start(bf16[160,4096]{1,0:T(8,128)(2,1)S(1)} %get-tuple-element.9), channel_id=1, source_target_pairs={{0,12},{4,0},{8,4},{12,8},{1,13},{5,1},{9,5},{13,9},{2,14},{6,2},{... | collective-permute-start | bytes 3932168 | tf_op jit(solution)/shard_map/ppermute | solution.py:28
  29.3 27.0 %collective-permute-start.2 = (bf16[160,4096]{1,0:T(8,128)(2,1)S(1)}, bf16[160,4096]{1,0:T(8,128)(2,1)}, u32[]{:S(2)}, u32[]{:S(2)}) collective-permute-start(bf16[160,4096]{1,0:T(8,128)(2,1)S(1)} %get-tuple-element.9), channel_id=1, source_target_pairs={{0,4},{4,8},{8,12},{12,0},{1,5},{5,9},{9,13},{13,1},{2,6},{6,10},{... | collective-permute-start | bytes 3932168 | tf_op jit(solution)/shard_map/ppermute | solution.py:27
  52.0 40.9 %collective-permute-start.9 = (bf16[160,4096]{1,0:T(8,128)(2,1)S(1)}, bf16[160,4096]{1,0:T(8,128)(2,1)S(1)}, u32[]{:S(2)}, u32[]{:S(2)}) collective-permute-start(bf16[160,4096]{1,0:T(8,128)(2,1)S(1)} %get-tuple-element.9), channel_id=1, source_target_pairs={{0,1},{1,0},{2,3},{3,2},{4,5},{5,4},{6,7},{7,6},{8,9},{9,8},{10,11... | collective-permute-start | bytes 3932168 | tf_op jit(solution)/shard_map/ppermute | solution.py:22
  52.4 40.8 %collective-permute-start.34 = (bf16[160,2048]{1,0:T(8,128)(2,1)S(1)}, bf16[160,2048]{1,0:T(8,128)(2,1)S(1)}, u32[]{:S(2)}, u32[]{:S(2)}) collective-permute-start(bf16[160,2048]{1,0:T(8,128)(2,1)S(1)} %get-tuple-element.30), channel_id=1, source_target_pairs={{0,1},{1,0},{2,3},{3,2},{4,5},{5,4},{6,7},{7,6},{8,9},{9,8},{10,11... | collective-permute-start | bytes 1966088 | tf_op jit(solution)/shard_map/ppermute | solution.py:22
  54.4 17.7 %collective-permute-start.7 = (bf16[80,4096]{1,0:T(8,128)(2,1)S(1)}, bf16[80,4096]{1,0:T(8,128)(2,1)S(1)}, u32[]{:S(2)}, u32[]{:S(2)}) collective-permute-start(bf16[80,4096]{1,0:T(8,128)(2,1)S(1)} %slice.193), channel_id=1, source_target_pairs={{0,16},{16,32},{32,48},{48,0},{1,17},{17,33},{33,49},{49,1},{2,18}... | collective-permute-start | bytes 1966088 | tf_op jit(solution)/shard_map/ppermute | solution.py:29
  56.3 17.4 %collective-permute-start.8 = (bf16[80,4096]{1,0:T(8,128)(2,1)S(1)}, bf16[80,4096]{1,0:T(8,128)(2,1)S(1)}, u32[]{:S(2)}, u32[]{:S(2)}) collective-permute-start(bf16[80,4096]{1,0:T(8,128)(2,1)S(1)} %slice.194), channel_id=1, source_target_pairs={{0,48},{16,0},{32,16},{48,32},{1,49},{17,1},{33,17},{49,33},{2,50}... | collective-permute-start | bytes 1966088 | tf_op jit(solution)/shard_map/ppermute | solution.py:30
  60.0 17.1 %collective-permute-start.3 = (bf16[80,4096]{1,0:T(8,128)(2,1)S(1)}, bf16[80,4096]{1,0:T(8,128)(2,1)S(1)}, u32[]{:S(2)}, u32[]{:S(2)}) collective-permute-start(bf16[80,4096]{1,0:T(8,128)(2,1)S(1)} %slice.191), channel_id=1, source_target_pairs={{0,4},{4,8},{8,12},{12,0},{1,5},{5,9},{9,13},{13,1},{2,6},{6,10},{... | collective-permute-start | bytes 1966088 | tf_op jit(solution)/shard_map/ppermute | solution.py:29
  73.7 44.1 %collective-permute-start.35 = (bf16[160,2048]{1,0:T(8,128)(2,1)S(1)}, bf16[160,2048]{1,0:T(8,128)(2,1)S(1)}, u32[]{:S(2)}, u32[]{:S(2)}) collective-permute-start(bf16[160,2048]{1,0:T(8,128)(2,1)S(1)} %get-tuple-element.28), channel_id=1, source_target_pairs={{0,1},{1,0},{2,3},{3,2},{4,5},{5,4},{6,7},{7,6},{8,9},{9,8},{10,11... | collective-permute-start | bytes 1966088 | tf_op jit(solution)/shard_map/ppermute | solution.py:22
  77.1 16.8 %collective-permute-start.10 = (bf16[160,4096]{1,0:T(8,128)(2,1)}, bf16[160,4096]{1,0:T(8,128)(2,1)S(1)}, u32[]{:S(2)}, u32[]{:S(2)}) collective-permute-start(bf16[160,4096]{1,0:T(8,128)(2,1)} %collective-permute-done.5), channel_id=1, source_target_pairs={{0,1},{1,0},{2,3},{3,2},{4,5},{5,4},{6,7},{7,6},{8,9},{9,8},{10,11... | collective-permute-start | bytes 3932168 | tf_op jit(solution)/shard_map/ppermute | solution.py:22
  93.2 32.6 %collective-permute-start.36 = (bf16[160,2048]{1,0:T(8,128)(2,1)S(1)}, bf16[160,2048]{1,0:T(8,128)(2,1)S(1)}, u32[]{:S(2)}, u32[]{:S(2)}) collective-permute-start(bf16[160,2048]{1,0:T(8,128)(2,1)S(1)} %get-tuple-element.11), channel_id=1, source_target_pairs={{0,1},{1,0},{2,3},{3,2},{4,5},{5,4},{6,7},{7,6},{8,9},{9,8},{10,11... | collective-permute-start | bytes 1966088 | tf_op jit(solution)/shard_map/ppermute | solution.py:22
  93.9 38.2 %collective-permute-start.37 = (bf16[160,2048]{1,0:T(8,128)(2,1)}, bf16[160,2048]{1,0:T(8,128)(2,1)S(1)}, u32[]{:S(2)}, u32[]{:S(2)}) collective-permute-start(bf16[160,2048]{1,0:T(8,128)(2,1)} %get-tuple-element.26), channel_id=1, source_target_pairs={{0,1},{1,0},{2,3},{3,2},{4,5},{5,4},{6,7},{7,6},{8,9},{9,8},{10,11... | collective-permute-start | bytes 1966088 | tf_op jit(solution)/shard_map/ppermute | solution.py:22
  142.6 17.5 %collective-permute-start.27 = (f32[80,2048]{1,0:T(8,128)S(1)}, f32[80,2048]{1,0:T(8,128)S(1)}, u32[]{:S(2)}, u32[]{:S(2)}) collective-permute-start(f32[80,2048]{1,0:T(8,128)S(1)} %slice.203), channel_id=1, source_target_pairs={{0,4},{4,8},{8,12},{12,0},{1,5},{5,9},{9,13},{13,1},{2,6},{6,10},{... | collective-permute-start | bytes 1966088 | tf_op jit(solution)/shard_map/ppermute | solution.py:40
  146.4 17.5 %collective-permute-start.38 = (f32[80,2048]{1,0:T(8,128)S(1)}, f32[80,2048]{1,0:T(8,128)S(1)}, u32[]{:S(2)}, u32[]{:S(2)}) collective-permute-start(f32[80,2048]{1,0:T(8,128)S(1)} %slice.216), channel_id=1, source_target_pairs={{0,16},{16,32},{32,48},{48,0},{1,17},{17,33},{33,49},{49,1},{2,18}... | collective-permute-start | bytes 1966088 | tf_op jit(solution)/shard_map/ppermute | solution.py:40
  160.2 16.5 %collective-permute-start.28 = (f32[80,2048]{1,0:T(8,128)S(1)}, f32[80,2048]{1,0:T(8,128)S(1)}, u32[]{:S(2)}, u32[]{:S(2)}) collective-permute-start(f32[80,2048]{1,0:T(8,128)S(1)} %get-tuple-element.15), channel_id=1, source_target_pairs={{0,4},{4,8},{8,12},{12,0},{1,5},{5,9},{9,13},{13,1},{2,6},{6,10},{... | collective-permute-start | bytes 1966088 | tf_op jit(solution)/shard_map/ppermute | solution.py:44
  160.3 16.8 %collective-permute-start.29 = (f32[80,2048]{1,0:T(8,128)S(1)}, f32[80,2048]{1,0:T(8,128)S(1)}, u32[]{:S(2)}, u32[]{:S(2)}) collective-permute-start(f32[80,2048]{1,0:T(8,128)S(1)} %get-tuple-element.17), channel_id=1, source_target_pairs={{0,12},{4,0},{8,4},{12,8},{1,13},{5,1},{9,5},{13,9},{2,14},{6,2},{... | collective-permute-start | bytes 1966088 | tf_op jit(solution)/shard_map/ppermute | solution.py:43
  163.0 26.8 %collective-permute-start.30 = (f32[80,2048]{1,0:T(8,128)S(1)}, f32[80,2048]{1,0:T(8,128)S(1)}, u32[]{:S(2)}, u32[]{:S(2)}) collective-permute-start(f32[80,2048]{1,0:T(8,128)S(1)} %get-tuple-element.16), channel_id=1, source_target_pairs={{0,12},{4,0},{8,4},{12,8},{1,13},{5,1},{9,5},{13,9},{2,14},{6,2},{... | collective-permute-start | bytes 1966088 | tf_op jit(solution)/shard_map/ppermute | solution.py:41
  164.0 29.5 %collective-permute-start.39 = (f32[80,2048]{1,0:T(8,128)S(1)}, f32[80,2048]{1,0:T(8,128)S(1)}, u32[]{:S(2)}, u32[]{:S(2)}) collective-permute-start(f32[80,2048]{1,0:T(8,128)S(1)} %get-tuple-element.21), channel_id=1, source_target_pairs={{0,16},{16,32},{32,48},{48,0},{1,17},{17,33},{33,49},{49,1},{2,18}... | collective-permute-start | bytes 1966088 | tf_op jit(solution)/shard_map/ppermute | solution.py:44
  164.1 29.4 %collective-permute-start.40 = (f32[80,2048]{1,0:T(8,128)S(1)}, f32[80,2048]{1,0:T(8,128)S(1)}, u32[]{:S(2)}, u32[]{:S(2)}) collective-permute-start(f32[80,2048]{1,0:T(8,128)S(1)} %get-tuple-element.23), channel_id=1, source_target_pairs={{0,48},{16,0},{32,16},{48,32},{1,49},{17,1},{33,17},{49,33},{2,50}... | collective-permute-start | bytes 1966088 | tf_op jit(solution)/shard_map/ppermute | solution.py:43
  176.8 16.9 %collective-permute-start.41 = (f32[80,2048]{1,0:T(8,128)S(1)}, f32[80,2048]{1,0:T(8,128)S(1)}, u32[]{:S(2)}, u32[]{:S(2)}) collective-permute-start(f32[80,2048]{1,0:T(8,128)S(1)} %get-tuple-element.22), channel_id=1, source_target_pairs={{0,48},{16,0},{32,16},{48,32},{1,49},{17,1},{33,17},{49,33},{2,50}... | collective-permute-start | bytes 1966088 | tf_op jit(solution)/shard_map/ppermute | solution.py:41
  213.6 27.2 %collective-permute-start.44 = (bf16[160,4096]{1,0:T(8,128)(2,1)S(1)}, bf16[160,4096]{1,0:T(8,128)(2,1)S(1)}, u32[]{:S(2)}, u32[]{:S(2)}) collective-permute-start(bf16[160,4096]{1,0:T(8,128)(2,1)S(1)} %fusion.9), channel_id=1, source_target_pairs={{0,0},{1,64},{64,1},{65,65},{2,2},{3,66},{66,3},{67,67},{4,4},{5,6... | collective-permute-start | bytes 3932168 | tf_op jit(solution)/shard_map/ppermute | solution.py:18
  (33 other events, 214.8 us)

commit v2 on v0

v2 whole, which is shorter than its diff:
```python
import math

import jax
import jax.numpy as jnp
from jax import lax
from jax.experimental import pallas as pl
from jax.experimental.pallas import tpu as pltpu
from jax.sharding import Mesh, PartitionSpec as P

X, Z = 4, 4
ORDER = (0, 1, 3, 2)
LANES = 128
LEVELS = 32000.0
STEPS = 64 / math.log(2.0)
NN = (((1,), (0,)), ((), ()))
NT = (((1,), (1,)), ((), ()))
TN = (((0,), (0,)), ((), ()))
F32, BF16, I16 = jnp.float32, jnp.bfloat16, jnp.int16


def ring(n, step):
    return [(i, (i + step) % n) for i in range(n)]


SWAP = [(0, 0), (1, 2), (2, 1), (3, 3)]
SWAP_OTHER = [(1, 0), (3, 1), (0, 2), (2, 3)]


def swap(v):
    return lax.ppermute(v, ("yl", "c"), SWAP)


def other_core(v):
    return lax.ppermute(v, "c", ring(2, 1))


def up(v, axis):
    return lax.ppermute(v, axis, ring(4, 1))


def down(v, axis):
    return lax.ppermute(v, axis, ring(4, -1))


def after(v, *others):
    return lax.optimization_barrier((v, *others))[0]


def gather_small(v, axis):
    return [v] + [lax.ppermute(v, axis, ring(4, -k)) for k in ORDER[1:]]


def dot(a, b, dims):
    return lax.dot_general(a, b, dims, preferred_element_type=F32)


def call(kernel, name, args, outs, scratch=(), flops=0):
    vmem = pl.BlockSpec(memory_space=pltpu.VMEM)
    smem = pl.BlockSpec(memory_space=pltpu.SMEM)
    size = sum(a.size * a.dtype.itemsize for a in list(args) + list(outs))
    return pl.pallas_call(
        kernel,
        name=name,
        out_shape=tuple(jax.ShapeDtypeStruct(o.shape, o.dtype) for o in outs),
        in_specs=[smem if a.shape == (1,) else vmem for a in args],
        out_specs=tuple(vmem for _ in outs),
        scratch_shapes=list(scratch),
        cost_estimate=pl.CostEstimate(flops=flops, bytes_accessed=size, transcendentals=0),
        compiler_params=pltpu.CompilerParams(vmem_limit_bytes=16 << 20),
    )(*args)


def shape(*dims, dtype=F32):
    return jax.ShapeDtypeStruct(dims, dtype)


def split_kernel(xu, xd, zu, zd, xa, xb, za, zb):
    cut = xa.shape[0]
    xa[...] = xu[0:cut, :]
    za[...] = zu[0:cut, :]
    xb[...] = xd[cut:, :]
    zb[...] = zd[cut:, :]


def stack_kernel(u, xd, xu, zd, zu, be, ae):
    rows = u.shape[0]
    for dst, d, w in ((be, xd, xu), (ae, zd, zu)):
        dst[0:rows, :] = u[...]
        dst[rows : 2 * rows, :] = d[...]
        dst[2 * rows :, :] = w[...]


def early_kernel(ae, b, s):
    s[...] = dot(ae[...], b[...], NT)


def column(row, n):
    return jnp.transpose(jnp.broadcast_to(row, (LANES, n)))[:, :1]


def tail_kernel(mult, ae, za, zb, bo, xa, xb, bs, ya, yb, s1, s2, mate, s, rstat, cstat, at, bt):
    n, side = bo.shape[0], s.shape[1] // 2
    cut, rows = za.shape[0], 2 * za.shape[0]
    for i, v in enumerate((za, zb)):
        at[i * cut : (i + 1) * cut, :] = v[...]
    for i, v in enumerate((xa, xb, ya, yb)):
        bt[i * cut : (i + 1) * cut, :] = v[...]
    s[0:n, 0:n] = s1[...]
    s[0:n, side : side + n] = s2[...]
    s[n:, 0:n] = dot(at[...], bo[...], NT)
    s[n:, side : side + n] = dot(at[...], bs[...], NT)
    e = dot(ae[...], bt[...], NT)
    s[0:n, n:side] = e[:, :rows]
    s[0:n, side + n :] = e[:, rows:]
    e = dot(at[...], bt[...], NT)
    s[n:, n:side] = e[:, :rows]
    s[n:, side + n :] = e[:, rows:]
    multiplier = mult[0]
    tall, wide = s.shape
    rstat[...] = jnp.zeros(rstat.shape, F32)
    rstat[2:3, 0:rows] = mate[...]

    def first(i, top):
        r = pl.ds(pl.multiple_of(i * LANES, LANES), LANES)
        v = s[r, :] * multiplier
        row_ids = i * LANES + lax.broadcasted_iota(jnp.int32, (LANES, wide), 0)
        col_ids = lax.broadcasted_iota(jnp.int32, (LANES, wide), 1)
        v = jnp.where((row_ids == col_ids) & (row_ids < rows), F32(-1e30), v)
        s[r, :] = v
        m = jnp.max(v, axis=1, keepdims=True)
        l = jnp.sum(jnp.exp(v - m), axis=1, keepdims=True)
        rstat[0:1, r] = jnp.transpose(jnp.broadcast_to(m, (LANES, LANES)))[0:1, :]
        rstat[1:2, r] = jnp.transpose(jnp.broadcast_to(l, (LANES, LANES)))[0:1, :]
        return jnp.maximum(top, jnp.max(v, axis=0, keepdims=True))

    top = lax.fori_loop(0, tall // LANES, first, jnp.full((1, wide), -1e30, F32))

    def second(i, low):
        r = pl.ds(pl.multiple_of(i * LANES, LANES), LANES)
        return low + jnp.sum(jnp.exp(s[r, :] - top), axis=0, keepdims=True)

    low = lax.fori_loop(0, tall // LANES, second, jnp.zeros((1, wide), F32))
    cstat[...] = jnp.zeros(cstat.shape, F32)
    cstat[0:1, :] = top
    cstat[1:2, :] = low


def merge_kernel(mine, other, s, r0, r1, r2, r3, cols, out, known):
    side = mine.shape[1] // 2
    tall, wide = s.shape
    rows = tall // 4
    theirs = jnp.concatenate([other[:, side:], other[:, :side]], 1)
    m1, m2 = mine[0:1, :], theirs[0:1, :]
    m = jnp.maximum(m1, m2)
    out[0:1, :] = m
    out[1:2, :] = mine[1:2, :] * jnp.exp(m1 - m) + theirs[1:2, :] * jnp.exp(m2 - m)
    lse_r = combine((r0, r1, r2, r3), rows)
    known[...] = jnp.zeros(known.shape, F32)
    known[0:1, :] = lse_r
    known[1:2, :] = jnp.concatenate([r[2:3, 0:rows] for r in (r0, r1, r2, r3)], 1)
    ids = cols[...]

    def step(i, pos):
        r = pl.ds(pl.multiple_of(i * LANES, LANES), LANES)
        hit = ids == column(known[1:2, r], LANES)
        return pos + jnp.sum(jnp.where(hit, s[r, :], F32(0.0)), axis=0, keepdims=True)

    pos = lax.fori_loop(0, tall // LANES, step, jnp.zeros((1, wide), F32))
    share = jnp.sum(lse_r[:, 0:rows]) - jnp.sum(pos)
    out[2:3, :] = jnp.full((1, wide), share, F32)
    out[3:, :] = jnp.zeros((out.shape[0] - 3, wide), F32)


def combine(messages, rows):
    groups = messages[0].shape[1] // (4 * rows)
    tops, lows = [], []
    for step, message in zip(ORDER, messages):
        at = [(g * 4 + ORDER.index((k - step) % 4)) * rows for g in range(groups) for k in ORDER]
        tops.append(jnp.concatenate([message[0:1, p : p + rows] for p in at], 1))
        lows.append(jnp.concatenate([message[1:2, p : p + rows] for p in at], 1))
    top = jnp.maximum(jnp.maximum(tops[0], tops[1]), jnp.maximum(tops[2], tops[3]))
    low = sum(l * jnp.exp(t - top) for t, l in zip(tops, lows))
    return top + jnp.log(low)


def weights_kernel(s, known, c0, c1, c2, c3, cols, near, far, part):
    tall, wide = s.shape
    side = wide // 2
    lse_c = combine((c0, c1, c2, c3), tall // 4)
    ids = cols[...]

    @pl.loop(0, tall // LANES)
    def _(i):
        r = pl.ds(pl.multiple_of(i * LANES, LANES), LANES)
        v = s[r, :]
        hit = ids == column(known[1:2, r], LANES)
        w = jnp.exp(v - column(known[0:1, r], LANES)) + jnp.exp(v - lse_c)
        w = (w - jnp.where(hit, F32(2.0), F32(0.0))).astype(BF16)
        near[r, :] = w[:, :side]
        far[r, :] = w[:, side:]

    part[...] = c0[2:3, 0:LANES] + c1[2:3, 0:LANES] + c2[2:3, 0:LANES] + c3[2:3, 0:LANES]


def pack(dst, at, g):
    n, w = g.shape
    m = jnp.maximum(jnp.max(jnp.abs(g), axis=1, keepdims=True), F32(1e-30))
    k = jnp.ceil(jnp.log(m) * STEPS)
    q = (g * (LEVELS * jnp.exp(k * (-1.0 / STEPS))) + F32(12582912.0)) - F32(12582912.0)
    dst[at : at + n, 0:w] = q.astype(jnp.int32).astype(I16)
    dst[at : at + n, w : w + LANES] = jnp.broadcast_to(k, (n, LANES)).astype(jnp.int32).astype(I16)


def unpack(src, at, n):
    w = src.shape[1] - LANES
    k = src[at : at + n, w : w + LANES].astype(jnp.int32).astype(F32)[:, :1]
    q = src[at : at + n, 0:w].astype(jnp.int32).astype(F32)
    return q * (jnp.exp(k * (1.0 / STEPS)) * (1.0 / LEVELS))


def hand_out(acc, fwd, bwd, keep1, keep3, own):
    rows = own.shape[0]
    cut = rows // 2
    pack(fwd, 0, acc[3 * rows : 3 * rows + cut, :])
    pack(fwd, cut, acc[rows + cut : 2 * rows, :])
    pack(bwd, 0, acc[3 * rows + cut : 4 * rows, :])
    pack(bwd, cut, acc[2 * rows : 2 * rows + cut, :])
    keep1[...] = acc[rows : rows + cut, :]
    keep3[...] = acc[2 * rows + cut : 3 * rows, :]
    own[...] = acc[0:rows, :]


def rows_z_kernel(bo, xa, xb, bs, ya, yb, out):
    n, cut, half = bo.shape[0], xa.shape[0], out.shape[1]
    at = 0
    for v in (bo, xa, xb, bs, ya, yb):
        out[at : at + v.shape[0], :] = v[:, :half]
        at += v.shape[0]


def rows_x_kernel(ae, za, zb, oe, oa, ob, out):
    half = out.shape[1]
    at = 0
    for v in (ae, za, zb, oe, oa, ob):
        out[at : at + v.shape[0], :] = v[:, v.shape[1] - half :]
        at += v.shape[0]


def z_kernel(near, far, b, fwd, bwd, keep1, keep3, own, acc):
    side = near.shape[1]
    acc[...] = dot(near[...], b[0:side, :], NN) + dot(far[...], b[side:, :], NN)
    hand_out(acc, fwd, bwd, keep1, keep3, own)


def x_kernel(near, far, a, fwd, bwd, keep1, keep3, own, acc):
    side = near.shape[0]
    acc[...] = dot(near[...], a[0:side, :], TN) + dot(far[...], a[side:, :], TN)
    hand_out(acc, fwd, bwd, keep1, keep3, own)


def forward_kernel(fwd, bwd, keep1, keep3, to_up, to_down):
    cut = keep1.shape[0]
    pack(to_up, 0, unpack(fwd, 0, cut) + keep1[...])
    pack(to_down, 0, unpack(bwd, 0, cut) + keep3[...])


def finish_kernel(mult, e, oz, fz, bz, uz, dz, ox, fx, bx, ux, dx, grad):
    cut, half = e.shape[0] // 2, oz.shape[1]
    for h in (0, 1):
        r = slice(h * cut, (h + 1) * cut)
        terms = []
        for own, f, b, u, d in ((oz, fz, bz, uz, dz), (ox, fx, bx, ux, dx)):
            step, straight = (u, b) if h == 0 else (d, f)
            terms.append(own[r, :] + unpack(step, 0, cut) + unpack(straight, cut, cut))
        g0, g1 = mult[0] * terms[0], mult[0] * terms[1]
        e0, e1 = e[r, :half].astype(F32), e[r, half:].astype(F32)
        square = jnp.sum(e0 * e0, axis=1, keepdims=True) + jnp.sum(e1 * e1, axis=1, keepdims=True)
        factor = lax.rsqrt(square + 1e-06)
        inner = jnp.sum(e0 * g0, axis=1, keepdims=True) + jnp.sum(e1 * g1, axis=1, keepdims=True)
        scale = factor * factor * factor * inner
        grad[r, :half] = (factor * g0 - scale * e0).astype(BF16)
        grad[r, half:] = (factor * g1 - scale * e1).astype(BF16)


def normalize(e):
    wide = e.astype(F32)
    return (wide * lax.rsqrt(jnp.sum(wide * wide, axis=1, keepdims=True) + 1e-06)).astype(BF16)


def local(embeddings, partner, logit_scale):
    rows, width = embeddings.shape
    half, cut = width // 2, rows // 2
    side, n = 4 * rows, 3 * rows
    total = rows * 2 * X * Z
    c, x, z = lax.axis_index("c"), lax.axis_index("x"), lax.axis_index("z")

    emb = swap(embeddings)
    u = normalize(emb)

    xu, xd, zu, zd = lax.optimization_barrier((up(u, "x"), down(u, "x"), up(u, "z"), down(u, "z")))
    piece = shape(cut, width, dtype=BF16)
    xa, xb, za, zb = call(split_kernel, "halves", (xu, xd, zu, zd), (piece,) * 4)
    xa, za, xb, zb = up(xa, "x"), up(za, "z"), down(xb, "x"), down(zb, "z")
    stack = shape(n, width, dtype=BF16)
    be, ae = call(stack_kernel, "stack", (u, xd, xu, zd, zu), (stack, stack))
    flops = 2 * n * n * width
    scores1, = call(early_kernel, "early", (ae, be), (shape(n, n),), flops=flops)
    be, scores1 = lax.optimization_barrier((be, scores1))
    bs = other_core(be)
    mate = swap(after(partner.reshape(1, rows), scores1)).astype(F32)
    xa, xb, za, zb = lax.optimization_barrier((xa, xb, za, zb))
    ya, yb = other_core(xa), other_core(xb)
    scores2, = call(early_kernel, "other", (ae, bs), (shape(n, n),), flops=flops)
    oe = other_core(after(ae, ya, yb))
    oa, ob = other_core(after(za, oe)), other_core(after(zb, oe))

    scores, rstat, cstat = call(
        tail_kernel, "tail", (logit_scale, ae, za, zb, be, xa, xb, bs, ya, yb, scores1, scores2, mate),
        (shape(side, 2 * side), shape(8, side), shape(8, 2 * side)),
        scratch=[pltpu.VMEM((rows, width), BF16), pltpu.VMEM((2 * rows, width), BF16)],
        flops=2 * 7 * rows * 2 * rows * width,
    )
    within = jnp.arange(rows, dtype=jnp.int32)
    cols = jnp.concatenate(
        [((cc * X + (x + k) % X) * Z + z) * rows + within for cc in (c, 1 - c) for k in ORDER]
    ).reshape(1, -1).astype(F32)
    cstat_other = other_core(cstat)
    rstats = gather_small(rstat, "z")
    merged, known = call(
        merge_kernel, "merge", (cstat, cstat_other, scores, *rstats, cols), (cstat, rstat)
    )
    cstats = gather_small(merged, "x")
    near, far, part = call(
        weights_kernel, "weights", (scores, known, *cstats, cols),
        (shape(side, side, dtype=BF16), shape(side, side, dtype=BF16), shape(1, LANES)),
    )
    far_other = other_core(far)

    stack = shape(2 * side, half, dtype=BF16)
    rows_z, = call(rows_z_kernel, "rows_z", (be, xa, xb, bs, ya, yb), (stack,))
    rows_x, = call(rows_x_kernel, "rows_x", (ae, za, zb, oe, oa, ob), (stack,))
    message = shape(rows, half + LANES, dtype=I16)
    kept = shape(cut, half)
    outs = (message, message, kept, kept, shape(rows, half))
    flops = 2 * side * 2 * side * half
    acc = [pltpu.VMEM((side, half), F32)]
    fz, bz, k1z, k3z, oz = call(
        z_kernel, "along_z", (near, far, rows_z), outs, scratch=acc, flops=flops
    )
    fz, bz = up(fz, "z"), down(bz, "z")
    fx, bx, k1x, k3x, ox = call(
        x_kernel, "along_x", (near, far_other, rows_x), outs, scratch=acc, flops=flops
    )
    fx, bx = up(fx, "x"), down(bx, "x")
    fz, bz, part = lax.optimization_barrier((fz, bz, sum(gather_small(part, "z"))))
    both = swap(part) + lax.ppermute(part, ("yl", "c"), SWAP_OTHER)
    short = shape(cut, half + LANES, dtype=I16)
    uz, dz = call(forward_kernel, "forward_z", (fz, bz, k1z, k3z), (short, short))
    uz, dz = up(uz, "z"), down(dz, "z")
    fx, bx, both = lax.optimization_barrier((fx, bx, both))
    ux, dx = call(forward_kernel, "forward_x", (fx, bx, k1x, k3x), (short, short))
    ux, dx = up(ux, "x"), down(dx, "x")
    grad, = call(
        finish_kernel, "finish",
        (logit_scale, emb, oz, fz, bz, uz, dz, ox, fx, bx, ux, dx),
        (shape(rows, width, dtype=BF16),),
    )
    return swap(grad), (both[0, :1] / total)


def solution(mesh):
    fine = Mesh(
        mesh.devices.reshape(2, X, Z, 2, 2), ("yl", "x", "z", "yh", "c")
    )
    rows = ("yh", "c", "yl", "x", "z")
    return jax.shard_map(
        local,
        mesh=fine,
        in_specs=(P(rows, None), P(rows), P()),
        out_specs=(P(rows, None), P(("yh", "c"))),
        check_vma=False,
    )
```

time: 678 us -> 200 us (0.29)
  the two profiles are of different devices: /device:TPU:0 before, /device:TPU:1 now
where the time goes in v2:
time: 200 us
  waiting for transfers between devices  81.6 us (41%)
  starting transfers between devices  56.6 us (28%)
  Pallas kernels  50.5 us (25%)
  local copies, waits for them, and re-layouts  7.59 us (4%)
  between operations  2.88 us (1%)
    pallas_call x14, Pallas kernels, call(): pl.pallas_call(kernel, name=name, out_shape=tuple((jax.ShapeDtypeStruct(o...  50.5 us
    ppermute x4, waiting for transfers between devices, swap(): return lax.ppermute(v, ('yl', 'c'), SWAP)  31.9 us
    ppermute x8, waiting for transfers between devices, up(): return lax.ppermute(v, axis, ring(4, 1))  29.2 us
    ppermute x4, starting transfers between devices, swap(): return lax.ppermute(v, ('yl', 'c'), SWAP)  25.1 us
    ppermute x8, starting transfers between devices, down(): return lax.ppermute(v, axis, ring(4, -1))  16.9 us
    ppermute x9, waiting for transfers between devices, gather_small(): return [v] + [lax.ppermute(v, axis, ring(4, -k)) for k in ORDER[1:]]  16.5 us
    unnamed x47, local copies, waits for them, and re-layouts  7.48 us
    ppermute x9, starting transfers between devices, gather_small(): return [v] + [lax.ppermute(v, axis, ring(4, -k)) for k in ORDER[1:]]  7.44 us
  transfers between devices with their start and end apart: 38, of which 18 were waited for; matrix products, arithmetic and copies ran while one was open for 0% of the time, Pallas kernels for 24%

profile of v2, /device:TPU:1, one launch (start us, length us, event | category | flops | bytes accessed | tf_op | source)
XLA Modules:
  0.0 199.9 jit_solution(3543260315058102617)
XLA Ops:
  0.6 4.6 %collective-permute-start = (bf16[160,4096]{1,0:T(8,128)(2,1)}, bf16[160,4096]{1,0:T(8,128)(2,1)S(1)}, u32[]{:S(2)}, u32[]{:S(2)}) collective-permute-start(bf16[160,4096]{1,0:T(8,128)(2,1)} %param.3), channel_id=1, source_target_pairs={{0,0},{1,64},{64,1},{65,65},{2,2},{3,66},{66,3},{67,67},{4,4},{5,6... | collective-permute-start | bytes 3932168 | tf_op jit(solution)/shard_map/ppermute | solution.py:30
  5.2 15.8 %collective-permute-done.e = bf16[160,4096]{1,0:T(8,128)(2,1)S(1)} collective-permute-done((bf16[160,4096]{1,0:T(8,128)(2,1)}, bf16[160,4096]{1,0:T(8,128)(2,1)S(1)}, u32[]{:S(2)}, u32[]{:S(2)}) %collective-permute-start) | collective-permute-done | bytes 1310752 | tf_op jit(solution)/shard_map/ppermute | solution.py:30
  28.5 18.5 %collective-permute-done.1.xu = bf16[160,4096]{1,0:T(8,128)(2,1)S(1)} collective-permute-done((bf16[160,4096]{1,0:T(8,128)(2,1)S(1)}, bf16[160,4096]{1,0:T(8,128)(2,1)S(1)}, u32[]{:S(2)}, u32[]{:S(2)}) %collective-permute-start.1) | collective-permute-done | bytes 1310752 | tf_op jit(solution)/shard_map/ppermute | solution.py:38
  47.1 3.5 %collective-permute-done.3.zu = bf16[160,4096]{1,0:T(8,128)(2,1)S(1)} collective-permute-done((bf16[160,4096]{1,0:T(8,128)(2,1)S(1)}, bf16[160,4096]{1,0:T(8,128)(2,1)S(1)}, u32[]{:S(2)}, u32[]{:S(2)}) %collective-permute-start.3) | collective-permute-done | bytes 1310752 | tf_op jit(solution)/shard_map/ppermute | solution.py:38
  50.8 2.7 %collective-permute-start.6 = (bf16[80,4096]{1,0:T(8,128)(2,1)S(1)}, bf16[80,4096]{1,0:T(8,128)(2,1)S(1)}, u32[]{:S(2)}, u32[]{:S(2)}) collective-permute-start(bf16[80,4096]{1,0:T(8,128)(2,1)S(1)} %get-tuple-element.56), channel_id=1, source_target_pairs={{0,48},{16,0},{32,16},{48,32},{1,49},{17,1},{33,17},{49,33},{2,50}... | collective-permute-start | bytes 1966088 | tf_op jit(solution)/shard_map/ppermute | solution.py:42
  56.1 3.7 %stack.1 = (bf16[480,4096]{1,0:T(8,128)(2,1)}, bf16[480,4096]{1,0:T(8,128)(2,1)}) custom-call(bf16[160,4096]{1,0:T(8,128)(2,1)S(1)} %fusion.1.u, bf16[160,4096]{1,0:T(8,128)(2,1)S(1)} %collective-permute-done.2.xd, bf16[160,4096]{1,0:T(8,128)(2,1)S(1)} %collective-permute-done.1.xu, bf16[160,4096]{1,0:T(8,128)(2,1)S(1)} %collective-permute-done.4.zd, ...), custom_call_target="tpu_custom_call" | custom-call | bytes 14417920 | tf_op jit(solution)/shard_map/stack/pallas_call | solution.py:61
  59.8 5.5 %early.1.s1 = f32[480,480]{1,0:T(8,128)S(1)} custom-call(bf16[480,4096]{1,0:T(8,128)(2,1)} %get-tuple-element.84.ae, bf16[480,4096]{1,0:T(8,128)(2,1)} %get-tuple-element.62.b.bo), custom_call_target="tpu_custom_call" | custom-call | flops 1887436800 | bytes 8785920 | tf_op jit(solution)/shard_map/early/pallas_call | solution.py:61
  70.2 3.8 %collective-permute-done.10.ya = bf16[80,4096]{1,0:T(8,128)(2,1)S(1)} collective-permute-done((bf16[80,4096]{1,0:T(8,128)(2,1)S(1)}, bf16[80,4096]{1,0:T(8,128)(2,1)S(1)}, u32[]{:S(2)}, u32[]{:S(2)}) %collective-permute-start.10) | collective-permute-done | bytes 655392 | tf_op jit(solution)/shard_map/ppermute | solution.py:34
  76.0 6.1 %collective-permute-start.12 = (s32[1,160]{1,0:T(1,128)S(1)}, s32[1,160]{1,0:T(1,128)S(1)}, u32[]{:S(2)}, u32[]{:S(2)}) collective-permute-start(s32[1,160]{1,0:T(1,128)S(1)} %bitcast.19), channel_id=1, source_target_pairs={{0,0},{1,64},{64,1},{65,65},{2,2},{3,66},{66,3},{67,67},{4,4},{5,6... | collective-permute-start | bytes 1928 | tf_op jit(solution)/shard_map/ppermute | solution.py:30
  83.2 5.7 %other.1.s2 = f32[480,480]{1,0:T(8,128)S(1)} custom-call(bf16[480,4096]{1,0:T(8,128)(2,1)} %get-tuple-element.84.ae, bf16[480,4096]{1,0:T(8,128)(2,1)} %collective-permute-done.9.b.bs), custom_call_target="tpu_custom_call" | custom-call | flops 1887436800 | bytes 8785920 | tf_op jit(solution)/shard_map/other/pallas_call | solution.py:61
  88.9 12.4 %tail.1 = (f32[640,1280]{1,0:T(8,128)S(1)}, f32[8,640]{1,0:T(8,128)S(1)}, f32[8,1280]{1,0:T(8,128)S(1)}) custom-call(f32[1]{0:T(128)S(6)} %copy.6.mult, bf16[480,4096]{1,0:T(8,128)(2,1)} %get-tuple-element.84.ae, bf16[80,4096]{1,0:T(8,128)(2,1)S(1)} %copy-done.5, bf16[80,4096]{1,0:T(8,128)(2,1)S(1)} %copy-done.8, bf16[480,4096]{1,0:T(8,128)(2,1)} %get-tuple-element.62.b.bo, ...), custom_call_target="tpu_custom_call" | custom-call | flops 2936012800 | bytes 20910724 | tf_op jit(solution)/shard_map/tail/pallas_call | solution.py:61
  118.2 3.7 %rows_z.1.b = bf16[1280,2048]{1,0:T(8,128)(2,1)S(1)} custom-call(bf16[480,4096]{1,0:T(8,128)(2,1)} %get-tuple-element.62.b.bo, bf16[80,4096]{1,0:T(8,128)(2,1)S(1)} %copy-done.12, bf16[80,4096]{1,0:T(8,128)(2,1)S(1)} %copy-done.15, bf16[480,4096]{1,0:T(8,128)(2,1)} %collective-permute-done.9.b.bs, bf16[80,4096]{1,0:T(8,128)(2,1)S(1)} %copy-done.18, ...), custom_call_target="tpu_custom_call" | custom-call | bytes 15728640 | tf_op jit(solution)/shard_map/rows_z/pallas_call | solution.py:61
  121.9 4.9 %along_z.1 = (s16[160,2176]{1,0:T(8,128)(2,1)S(1)}, s16[160,2176]{1,0:T(8,128)(2,1)S(1)}, f32[80,2048]{1,0:T(8,128)S(1)}, f32[80,2048]{1,0:T(8,128)S(1)}, f32[160,2048]{1,0:T(8,128)S(1)}) custom-call(bf16[640,640]{1,0:T(8,128)(2,1)S(1)} %get-tuple-element.72.near, bf16[640,640]{1,0:T(8,128)(2,1)S(1)} %get-tuple-element.73.far, bf16[1280,2048]{1,0:T(8,128)(2,1)S(1)} %rows_z.1.b), custom_call_target="tpu_custom_call" | custom-call | flops 3355443200 | bytes 10895360 | tf_op jit(solution)/shard_map/along_z/pallas_call | solution.py:61
  129.5 3.7 %rows_x.1.a = bf16[1280,2048]{1,0:T(8,128)(2,1)S(1)} custom-call(bf16[480,4096]{1,0:T(8,128)(2,1)} %get-tuple-element.84.ae, bf16[80,4096]{1,0:T(8,128)(2,1)S(1)} %copy-done.6, bf16[80,4096]{1,0:T(8,128)(2,1)S(1)} %copy-done.9, bf16[480,4096]{1,0:T(8,128)(2,1)} %collective-permute-done.28.oe, bf16[80,4096]{1,0:T(8,128)(2,1)S(1)} %collective-permute-done.29.oa, ...), custom_call_target="tpu_custom_call" | custom-call | bytes 15728640 | tf_op jit(solution)/shard_map/rows_x/pallas_call | solution.py:61
  133.2 4.9 %along_x.1 = (s16[160,2176]{1,0:T(8,128)(2,1)S(1)}, s16[160,2176]{1,0:T(8,128)(2,1)S(1)}, f32[80,2048]{1,0:T(8,128)S(1)}, f32[80,2048]{1,0:T(8,128)S(1)}, f32[160,2048]{1,0:T(8,128)S(1)}) custom-call(bf16[640,640]{1,0:T(8,128)(2,1)S(1)} %get-tuple-element.72.near, bf16[640,640]{1,0:T(8,128)(2,1)S(1)} %collective-permute-done.27.far, ...), custom_call_target="tpu_custom_call" | custom-call | flops 3355443200 | bytes 10895360 | tf_op jit(solution)/shard_map/along_x/pallas_call | solution.py:61
  138.2 2.7 %collective-permute-start.32 = (s16[160,2176]{1,0:T(8,128)(2,1)S(1)}, s16[160,2176]{1,0:T(8,128)(2,1)S(1)}, u32[]{:S(2)}, u32[]{:S(2)}) collective-permute-start(s16[160,2176]{1,0:T(8,128)(2,1)S(1)} %get-tuple-element.89), channel_id=1, source_target_pairs={{0,48},{16,0},{32,16},{48,32},{1,49},{17,1},{33,17},{49,33},{2,50}... | collective-permute-start | bytes 2088968 | tf_op jit(solution)/shard_map/ppermute | solution.py:42
  141.5 3.0 %collective-permute-done.22 = f32[1,128]{1,0:T(1,128)S(1)} collective-permute-done((f32[1,128]{1,0:T(1,128)S(1)}, f32[1,128]{1,0:T(1,128)S(1)}, u32[]{:S(2)}, u32[]{:S(2)}) %collective-permute-start.22) | collective-permute-done | bytes 544 | tf_op jit(solution)/shard_map/ppermute | solution.py:50
  145.1 3.4 %collective-permute-done.23 = f32[1,128]{1,0:T(1,128)S(1)} collective-permute-done((f32[1,128]{1,0:T(1,128)S(1)}, f32[1,128]{1,0:T(1,128)S(1)}, u32[]{:S(2)}, u32[]{:S(2)}) %collective-permute-start.23) | collective-permute-done | bytes 544 | tf_op jit(solution)/shard_map/ppermute | solution.py:50
  149.3 3.1 %collective-permute-done.24 = f32[1,128]{1,0:T(1,128)S(1)} collective-permute-done((f32[1,128]{1,0:T(1,128)S(1)}, f32[1,128]{1,0:T(1,128)S(1)}, u32[]{:S(2)}, u32[]{:S(2)}) %collective-permute-start.24) | collective-permute-done | bytes 544 | tf_op jit(solution)/shard_map/ppermute | solution.py:50
  152.4 9.3 %collective-permute-start.33 = (f32[1,128]{1,0:T(1,128)S(1)}, f32[1,128]{1,0:T(1,128)S(1)}, u32[]{:S(2)}, u32[]{:S(2)}) collective-permute-start(f32[1,128]{1,0:T(1,128)S(1)} %add_add_fusion), channel_id=1, source_target_pairs={{0,0},{1,64},{64,1},{65,65},{2,2},{3,66},{66,3},{67,67},{4,4},{5,6... | collective-permute-start | bytes 1544 | tf_op jit(solution)/shard_map/ppermute | solution.py:30
  168.4 4.5 %collective-permute-done.25.uz = s16[80,2176]{1,0:T(8,128)(2,1)S(1)} collective-permute-done((s16[80,2176]{1,0:T(8,128)(2,1)S(1)}, s16[80,2176]{1,0:T(8,128)(2,1)S(1)}, u32[]{:S(2)}, u32[]{:S(2)}) %collective-permute-start.25) | collective-permute-done | bytes 348192 | tf_op jit(solution)/shard_map/ppermute | solution.py:38
  173.0 2.7 %collective-permute-done.35.ux = s16[80,2176]{1,0:T(8,128)(2,1)S(1)} collective-permute-done((s16[80,2176]{1,0:T(8,128)(2,1)S(1)}, s16[80,2176]{1,0:T(8,128)(2,1)S(1)}, u32[]{:S(2)}, u32[]{:S(2)}) %collective-permute-start.35) | collective-permute-done | bytes 348192 | tf_op jit(solution)/shard_map/ppermute | solution.py:38
  177.3 5.1 %collective-permute-start.37 = (bf16[160,4096]{1,0:T(8,128)(2,1)S(1)}, bf16[160,4096]{1,0:T(8,128)(2,1)S(1)}, u32[]{:S(2)}, u32[]{:S(2)}) collective-permute-start(bf16[160,4096]{1,0:T(8,128)(2,1)S(1)} %finish.1), channel_id=1, source_target_pairs={{0,0},{1,64},{64,1},{65,65},{2,2},{3,66},{66,3},{67,67},{4,4},{5,6... | collective-permute-start | bytes 3932168 | tf_op jit(solution)/shard_map/ppermute | solution.py:30
  182.5 15.2 %collective-permute-done.37 = bf16[160,4096]{1,0:T(8,128)(2,1)S(1)} collective-permute-done((bf16[160,4096]{1,0:T(8,128)(2,1)S(1)}, bf16[160,4096]{1,0:T(8,128)(2,1)S(1)}, u32[]{:S(2)}, u32[]{:S(2)}) %collective-permute-start.37) | collective-permute-done | bytes 1310752 | tf_op jit(solution)/shard_map/ppermute | solution.py:30
  (129 shorter events, 48.6 us)
Async XLA Ops:
  0.6 20.4 %collective-permute-start = (bf16[160,4096]{1,0:T(8,128)(2,1)}, bf16[160,4096]{1,0:T(8,128)(2,1)S(1)}, u32[]{:S(2)}, u32[]{:S(2)}) collective-permute-start(bf16[160,4096]{1,0:T(8,128)(2,1)} %param.3), channel_id=1, source_target_pairs={{0,0},{1,64},{64,1},{65,65},{2,2},{3,66},{66,3},{67,67},{4,4},{5,6... | collective-permute-start | bytes 3932168 | tf_op jit(solution)/shard_map/ppermute | solution.py:30
  22.1 25.0 %collective-permute-start.1 = (bf16[160,4096]{1,0:T(8,128)(2,1)S(1)}, bf16[160,4096]{1,0:T(8,128)(2,1)S(1)}, u32[]{:S(2)}, u32[]{:S(2)}) collective-permute-start(bf16[160,4096]{1,0:T(8,128)(2,1)S(1)} %fusion.1.u), channel_id=1, source_target_pairs={{0,16},{16,32},{32,48},{48,0},{1,17},{17,33},{33,49},{49,1},{2,18}... | collective-permute-start | bytes 3932168 | tf_op jit(solution)/shard_map/ppermute | solution.py:38
  23.3 23.8 %collective-permute-start.2 = (bf16[160,4096]{1,0:T(8,128)(2,1)S(1)}, bf16[160,4096]{1,0:T(8,128)(2,1)S(1)}, u32[]{:S(2)}, u32[]{:S(2)}) collective-permute-start(bf16[160,4096]{1,0:T(8,128)(2,1)S(1)} %fusion.1.u), channel_id=1, source_target_pairs={{0,48},{16,0},{32,16},{48,32},{1,49},{17,1},{33,17},{49,33},{2,50}... | collective-permute-start | bytes 3932168 | tf_op jit(solution)/shard_map/ppermute | solution.py:42
  24.7 25.8 %collective-permute-start.3 = (bf16[160,4096]{1,0:T(8,128)(2,1)S(1)}, bf16[160,4096]{1,0:T(8,128)(2,1)S(1)}, u32[]{:S(2)}, u32[]{:S(2)}) collective-permute-start(bf16[160,4096]{1,0:T(8,128)(2,1)S(1)} %fusion.1.u), channel_id=1, source_target_pairs={{0,4},{4,8},{8,12},{12,0},{1,5},{5,9},{9,13},{13,1},{2,6},{6,10},{... | collective-permute-start | bytes 3932168 | tf_op jit(solution)/shard_map/ppermute | solution.py:38
  26.4 24.1 %collective-permute-start.4 = (bf16[160,4096]{1,0:T(8,128)(2,1)S(1)}, bf16[160,4096]{1,0:T(8,128)(2,1)S(1)}, u32[]{:S(2)}, u32[]{:S(2)}) collective-permute-start(bf16[160,4096]{1,0:T(8,128)(2,1)S(1)} %fusion.1.u), channel_id=1, source_target_pairs={{0,12},{4,0},{8,4},{12,8},{1,13},{5,1},{9,5},{13,9},{2,14},{6,2},{... | collective-permute-start | bytes 3932168 | tf_op jit(solution)/shard_map/ppermute | solution.py:42
  50.7 15.6 %collective-permute-start.5 = (bf16[80,4096]{1,0:T(8,128)(2,1)S(1)}, bf16[80,4096]{1,0:T(8,128)(2,1)S(1)}, u32[]{:S(2)}, u32[]{:S(2)}) collective-permute-start(bf16[80,4096]{1,0:T(8,128)(2,1)S(1)} %get-tuple-element.55), channel_id=1, source_target_pairs={{0,16},{16,32},{32,48},{48,0},{1,17},{17,33},{33,49},{49,1},{2,18}... | collective-permute-start | bytes 1966088 | tf_op jit(solution)/shard_map/ppermute | solution.py:38
  50.8 15.5 %collective-permute-start.6 = (bf16[80,4096]{1,0:T(8,128)(2,1)S(1)}, bf16[80,4096]{1,0:T(8,128)(2,1)S(1)}, u32[]{:S(2)}, u32[]{:S(2)}) collective-permute-start(bf16[80,4096]{1,0:T(8,128)(2,1)S(1)} %get-tuple-element.56), channel_id=1, source_target_pairs={{0,48},{16,0},{32,16},{48,32},{1,49},{17,1},{33,17},{49,33},{2,50}... | collective-permute-start | bytes 1966088 | tf_op jit(solution)/shard_map/ppermute | solution.py:42
  53.4 12.9 %collective-permute-start.7 = (bf16[80,4096]{1,0:T(8,128)(2,1)S(1)}, bf16[80,4096]{1,0:T(8,128)(2,1)S(1)}, u32[]{:S(2)}, u32[]{:S(2)}) collective-permute-start(bf16[80,4096]{1,0:T(8,128)(2,1)S(1)} %get-tuple-element.57), channel_id=1, source_target_pairs={{0,4},{4,8},{8,12},{12,0},{1,5},{5,9},{9,13},{13,1},{2,6},{6,10},{... | collective-permute-start | bytes 1966088 | tf_op jit(solution)/shard_map/ppermute | solution.py:38
  54.6 12.6 %collective-permute-start.8 = (bf16[80,4096]{1,0:T(8,128)(2,1)S(1)}, bf16[80,4096]{1,0:T(8,128)(2,1)S(1)}, u32[]{:S(2)}, u32[]{:S(2)}) collective-permute-start(bf16[80,4096]{1,0:T(8,128)(2,1)S(1)} %get-tuple-element.58), channel_id=1, source_target_pairs={{0,12},{4,0},{8,4},{12,8},{1,13},{5,1},{9,5},{13,9},{2,14},{6,2},{... | collective-permute-start | bytes 1966088 | tf_op jit(solution)/shard_map/ppermute | solution.py:42
  66.3 16.9 %collective-permute-start.9 = (bf16[480,4096]{1,0:T(8,128)(2,1)}, bf16[480,4096]{1,0:T(8,128)(2,1)}, u32[]{:S(2)}, u32[]{:S(2)}) collective-permute-start(bf16[480,4096]{1,0:T(8,128)(2,1)} %get-tuple-element.62.b.bo), channel_id=1, source_target_pairs={{0,1},{1,0},{2,3},{3,2},{4,5},{5,4},{6,7},{7,6},{8,9},{9,8},{10,11... | collective-permute-start | bytes 11796488 | tf_op jit(solution)/shard_map/ppermute | solution.py:34
  75.8 41.9 %collective-permute-start.28 = (bf16[480,4096]{1,0:T(8,128)(2,1)}, bf16[480,4096]{1,0:T(8,128)(2,1)}, u32[]{:S(2)}, u32[]{:S(2)}) collective-permute-start(bf16[480,4096]{1,0:T(8,128)(2,1)} %get-tuple-element.84.ae), channel_id=1, source_target_pairs={{0,1},{1,0},{2,3},{3,2},{4,5},{5,4},{6,7},{7,6},{8,9},{9,8},{10,11... | collective-permute-start | bytes 11796488 | tf_op jit(solution)/shard_map/ppermute | solution.py:34
  117.2 16.0 %collective-permute-start.27 = (bf16[640,640]{1,0:T(8,128)(2,1)S(1)}, bf16[640,640]{1,0:T(8,128)(2,1)S(1)}, u32[]{:S(2)}, u32[]{:S(2)}) collective-permute-start(bf16[640,640]{1,0:T(8,128)(2,1)S(1)} %get-tuple-element.73.far), channel_id=1, source_target_pairs={{0,1},{1,0},{2,3},{3,2},{4,5},{5,4},{6,7},{7,6},{8,9},{9,8},{10,11... | collective-permute-start | bytes 2457608 | tf_op jit(solution)/shard_map/ppermute | solution.py:34
  117.7 11.8 %collective-permute-start.30 = (bf16[80,4096]{1,0:T(8,128)(2,1)S(1)}, bf16[80,4096]{1,0:T(8,128)(2,1)S(1)}, u32[]{:S(2)}, u32[]{:S(2)}) collective-permute-start(bf16[80,4096]{1,0:T(8,128)(2,1)S(1)} %copy-done.9), channel_id=1, source_target_pairs={{0,1},{1,0},{2,3},{3,2},{4,5},{5,4},{6,7},{7,6},{8,9},{9,8},{10,11... | collective-permute-start | bytes 1966088 | tf_op jit(solution)/shard_map/ppermute | solution.py:34
  117.8 11.7 %collective-permute-start.29 = (bf16[80,4096]{1,0:T(8,128)(2,1)S(1)}, bf16[80,4096]{1,0:T(8,128)(2,1)S(1)}, u32[]{:S(2)}, u32[]{:S(2)}) collective-permute-start(bf16[80,4096]{1,0:T(8,128)(2,1)S(1)} %copy-done.6), channel_id=1, source_target_pairs={{0,1},{1,0},{2,3},{3,2},{4,5},{5,4},{6,7},{7,6},{8,9},{9,8},{10,11... | collective-permute-start | bytes 1966088 | tf_op jit(solution)/shard_map/ppermute | solution.py:34
  126.8 25.7 %collective-permute-start.20 = (s16[160,2176]{1,0:T(8,128)(2,1)S(1)}, s16[160,2176]{1,0:T(8,128)(2,1)S(1)}, u32[]{:S(2)}, u32[]{:S(2)}) collective-permute-start(s16[160,2176]{1,0:T(8,128)(2,1)S(1)} %get-tuple-element.75), channel_id=1, source_target_pairs={{0,4},{4,8},{8,12},{12,0},{1,5},{5,9},{9,13},{13,1},{2,6},{6,10},{... | collective-permute-start | bytes 2088968 | tf_op jit(solution)/shard_map/ppermute | solution.py:38
  127.9 24.5 %collective-permute-start.21 = (s16[160,2176]{1,0:T(8,128)(2,1)S(1)}, s16[160,2176]{1,0:T(8,128)(2,1)S(1)}, u32[]{:S(2)}, u32[]{:S(2)}) collective-permute-start(s16[160,2176]{1,0:T(8,128)(2,1)S(1)} %get-tuple-element.76), channel_id=1, source_target_pairs={{0,12},{4,0},{8,4},{12,8},{1,13},{5,1},{9,5},{13,9},{2,14},{6,2},{... | collective-permute-start | bytes 2088968 | tf_op jit(solution)/shard_map/ppermute | solution.py:42
  138.1 27.0 %collective-permute-start.31 = (s16[160,2176]{1,0:T(8,128)(2,1)S(1)}, s16[160,2176]{1,0:T(8,128)(2,1)S(1)}, u32[]{:S(2)}, u32[]{:S(2)}) collective-permute-start(s16[160,2176]{1,0:T(8,128)(2,1)S(1)} %get-tuple-element.88), channel_id=1, source_target_pairs={{0,16},{16,32},{32,48},{48,0},{1,17},{17,33},{33,49},{49,1},{2,18}... | collective-permute-start | bytes 2088968 | tf_op jit(solution)/shard_map/ppermute | solution.py:38
  138.2 27.0 %collective-permute-start.32 = (s16[160,2176]{1,0:T(8,128)(2,1)S(1)}, s16[160,2176]{1,0:T(8,128)(2,1)S(1)}, u32[]{:S(2)}, u32[]{:S(2)}) collective-permute-start(s16[160,2176]{1,0:T(8,128)(2,1)S(1)} %get-tuple-element.89), channel_id=1, source_target_pairs={{0,48},{16,0},{32,16},{48,32},{1,49},{17,1},{33,17},{49,33},{2,50}... | collective-permute-start | bytes 2088968 | tf_op jit(solution)/shard_map/ppermute | solution.py:42
  152.4 10.5 %collective-permute-start.33 = (f32[1,128]{1,0:T(1,128)S(1)}, f32[1,128]{1,0:T(1,128)S(1)}, u32[]{:S(2)}, u32[]{:S(2)}) collective-permute-start(f32[1,128]{1,0:T(1,128)S(1)} %add_add_fusion), channel_id=1, source_target_pairs={{0,0},{1,64},{64,1},{65,65},{2,2},{3,66},{66,3},{67,67},{4,4},{5,6... | collective-permute-start | bytes 1544 | tf_op jit(solution)/shard_map/ppermute | solution.py:30
  162.4 10.6 %collective-permute-start.25 = (s16[80,2176]{1,0:T(8,128)(2,1)S(1)}, s16[80,2176]{1,0:T(8,128)(2,1)S(1)}, u32[]{:S(2)}, u32[]{:S(2)}) collective-permute-start(s16[80,2176]{1,0:T(8,128)(2,1)S(1)} %get-tuple-element.82), channel_id=1, source_target_pairs={{0,4},{4,8},{8,12},{12,0},{1,5},{5,9},{9,13},{13,1},{2,6},{6,10},{... | collective-permute-start | bytes 1044488 | tf_op jit(solution)/shard_map/ppermute | solution.py:38
  162.9 10.0 %collective-permute-start.26 = (s16[80,2176]{1,0:T(8,128)(2,1)S(1)}, s16[80,2176]{1,0:T(8,128)(2,1)S(1)}, u32[]{:S(2)}, u32[]{:S(2)}) collective-permute-start(s16[80,2176]{1,0:T(8,128)(2,1)S(1)} %get-tuple-element.83), channel_id=1, source_target_pairs={{0,12},{4,0},{8,4},{12,8},{1,13},{5,1},{9,5},{13,9},{2,14},{6,2},{... | collective-permute-start | bytes 1044488 | tf_op jit(solution)/shard_map/ppermute | solution.py:42
  165.7 10.0 %collective-permute-start.35 = (s16[80,2176]{1,0:T(8,128)(2,1)S(1)}, s16[80,2176]{1,0:T(8,128)(2,1)S(1)}, u32[]{:S(2)}, u32[]{:S(2)}) collective-permute-start(s16[80,2176]{1,0:T(8,128)(2,1)S(1)} %get-tuple-element.95), channel_id=1, source_target_pairs={{0,16},{16,32},{32,48},{48,0},{1,17},{17,33},{33,49},{49,1},{2,18}... | collective-permute-start | bytes 1044488 | tf_op jit(solution)/shard_map/ppermute | solution.py:38
  165.8 9.9 %collective-permute-start.36 = (s16[80,2176]{1,0:T(8,128)(2,1)S(1)}, s16[80,2176]{1,0:T(8,128)(2,1)S(1)}, u32[]{:S(2)}, u32[]{:S(2)}) collective-permute-start(s16[80,2176]{1,0:T(8,128)(2,1)S(1)} %get-tuple-element.96), channel_id=1, source_target_pairs={{0,48},{16,0},{32,16},{48,32},{1,49},{17,1},{33,17},{49,33},{2,50}... | collective-permute-start | bytes 1044488 | tf_op jit(solution)/shard_map/ppermute | solution.py:42
  177.3 20.4 %collective-permute-start.37 = (bf16[160,4096]{1,0:T(8,128)(2,1)S(1)}, bf16[160,4096]{1,0:T(8,128)(2,1)S(1)}, u32[]{:S(2)}, u32[]{:S(2)}) collective-permute-start(bf16[160,4096]{1,0:T(8,128)(2,1)S(1)} %finish.1), channel_id=1, source_target_pairs={{0,0},{1,64},{64,1},{65,65},{2,2},{3,66},{66,3},{67,67},{4,4},{5,6... | collective-permute-start | bytes 3932168 | tf_op jit(solution)/shard_map/ppermute | solution.py:30
  (37 other events, 158.5 us)

commit v3 on v2

v3 whole, which is shorter than its diff:
```python
import math

import jax
import jax.numpy as jnp
from jax import lax
from jax.experimental import pallas as pl
from jax.experimental.pallas import tpu as pltpu
from jax.sharding import Mesh, PartitionSpec as P

X, Z = 4, 4
ORDER = (0, 1, 3, 2)
LANES = 128
LEVELS = 32000.0
STEPS = 64 / math.log(2.0)
NN = (((1,), (0,)), ((), ()))
NT = (((1,), (1,)), ((), ()))
TN = (((0,), (0,)), ((), ()))
F32, BF16, I16 = jnp.float32, jnp.bfloat16, jnp.int16


def ring(n, step):
    return [(i, (i + step) % n) for i in range(n)]


SWAP = [(0, 0), (1, 2), (2, 1), (3, 3)]
SWAP_OTHER = [(1, 0), (3, 1), (0, 2), (2, 3)]


def swap(v):
    return lax.ppermute(v, ("yl", "c"), SWAP)


def other_core(v):
    return lax.ppermute(v, "c", ring(2, 1))


def up(v, axis):
    return lax.ppermute(v, axis, ring(4, 1))


def down(v, axis):
    return lax.ppermute(v, axis, ring(4, -1))


def after(v, *others):
    return lax.optimization_barrier((v, *others))[0]


def gather_small(v, axis):
    return [v] + [lax.ppermute(v, axis, ring(4, -k)) for k in ORDER[1:]]


def dot(a, b, dims):
    return lax.dot_general(a, b, dims, preferred_element_type=F32)


def call(kernel, name, args, outs, scratch=(), flops=0, mib=14):
    args = [
        pltpu.with_memory_space_constraint(a, pltpu.VMEM) if a.size * a.dtype.itemsize >= 1 << 19 else a
        for a in args
    ]
    vmem = pl.BlockSpec(memory_space=pltpu.VMEM)
    smem = pl.BlockSpec(memory_space=pltpu.SMEM)
    size = sum(a.size * a.dtype.itemsize for a in list(args) + list(outs))
    return pl.pallas_call(
        kernel,
        name=name,
        out_shape=tuple(jax.ShapeDtypeStruct(o.shape, o.dtype) for o in outs),
        in_specs=[smem if a.shape == (1,) else vmem for a in args],
        out_specs=tuple(vmem for _ in outs),
        scratch_shapes=list(scratch),
        cost_estimate=pl.CostEstimate(flops=flops, bytes_accessed=size, transcendentals=0),
        compiler_params=pltpu.CompilerParams(vmem_limit_bytes=mib << 20),
    )(*args)


def shape(*dims, dtype=F32):
    return jax.ShapeDtypeStruct(dims, dtype)


def halves_kernel(xu, xd, zu, zd, xa, xb, za, zb):
    cut = xa.shape[0]
    xa[...] = xu[0:cut, :]
    za[...] = zu[0:cut, :]
    xb[...] = xd[cut:, :]
    zb[...] = zd[cut:, :]


def stack_kernel(*refs):
    at = 0
    for v in refs[:-1]:
        refs[-1][at : at + v.shape[0], :] = v[...]
        at += v.shape[0]


def stack(name, *refs):
    out = shape(sum(r.shape[0] for r in refs), refs[0].shape[1], dtype=BF16)
    return call(stack_kernel, name, refs, (out,))[0]


def unit_kernel(e, digits, u, v):
    wide = e[...].astype(F32)
    unit = wide * lax.rsqrt(jnp.sum(wide * wide, axis=1, keepdims=True) + 1e-06)
    u[...] = unit.astype(BF16)
    v[:, : e.shape[1]] = unit.astype(BF16)
    v[:, e.shape[1] :] = digits[...]


def early_kernel(v, zd, zu, za, zb, b, a, last, mates, s):
    width, w = a.shape[1], last.shape[1]
    at = 0
    for r in (v, zd, zu, za, zb):
        n = r.shape[0]
        a[at : at + n, :] = r[:, :width]
        last[at : at + n, :] = r[:, width - w : width]
        two = r[:, width:].astype(F32)
        mates[at : at + n, :] = jnp.broadcast_to(two[:, 0:1] * F32(64.0) + two[:, 1:2], (n, LANES))
        at += n
    s[...] = dot(a[...], b[...], NT)


def column(row, n):
    return jnp.transpose(jnp.broadcast_to(row, (LANES, n)))[:, :1]


def tail_kernel(mult, a, b, early, mates, cols, s, rstat, cstat):
    side, rows = early.shape[0], early.shape[0] // 4
    s[:, 0:side] = early[...]
    s[:, side:] = dot(a[...], b[...], NT)
    multiplier = mult[0]
    tall, wide = s.shape
    rstat[...] = jnp.zeros(rstat.shape, F32)
    ids = cols[...]

    def first(i, carry):
        top, pos = carry
        r = pl.ds(pl.multiple_of(i * LANES, LANES), LANES)
        v = s[r, :] * multiplier
        pos += jnp.sum(jnp.where(ids == mates[r, 0:1], v, F32(0.0)), axis=0, keepdims=True)
        row_ids = i * LANES + lax.broadcasted_iota(jnp.int32, (LANES, wide), 0)
        col_ids = lax.broadcasted_iota(jnp.int32, (LANES, wide), 1)
        v = jnp.where((row_ids == col_ids) & (row_ids < rows), F32(-1e30), v)
        s[r, :] = v
        m = jnp.max(v, axis=1, keepdims=True)
        l = jnp.sum(jnp.exp(v - m), axis=1, keepdims=True)
        rstat[0:1, r] = jnp.transpose(jnp.broadcast_to(m, (LANES, LANES)))[0:1, :]
        rstat[1:2, r] = jnp.transpose(jnp.broadcast_to(l, (LANES, LANES)))[0:1, :]
        return jnp.maximum(top, jnp.max(v, axis=0, keepdims=True)), pos

    start = jnp.full((1, wide), -1e30, F32), jnp.zeros((1, wide), F32)
    top, pos = lax.fori_loop(0, tall // LANES, first, start)
    rstat[2:3, :] = jnp.full((1, tall), jnp.sum(pos), F32)

    def second(i, low):
        r = pl.ds(pl.multiple_of(i * LANES, LANES), LANES)
        return low + jnp.sum(jnp.exp(s[r, :] - top), axis=0, keepdims=True)

    low = lax.fori_loop(0, tall // LANES, second, jnp.zeros((1, wide), F32))
    cstat[...] = jnp.zeros(cstat.shape, F32)
    cstat[0:1, :] = top
    cstat[1:2, :] = low


def merge_kernel(mine, other, r0, r1, r2, r3, out, lse_r):
    wide, rows = out.shape[1], lse_r.shape[1] // 4
    side = wide // 2
    theirs = jnp.concatenate([other[:, side:], other[:, :side]], 1)
    m1, m2 = mine[0:1, :], theirs[0:1, :]
    m = jnp.maximum(m1, m2)
    lse = combine((r0, r1, r2, r3), rows)
    lse_r[...] = jnp.broadcast_to(lse, lse_r.shape)
    positive = r0[2:3, 0:1] + r1[2:3, 0:1] + r2[2:3, 0:1] + r3[2:3, 0:1]
    out[...] = jnp.broadcast_to(jnp.sum(lse, axis=1, keepdims=True) - positive, out.shape)
    out[0:1, :] = m
    out[1:2, :] = mine[1:2, :] * jnp.exp(m1 - m) + theirs[1:2, :] * jnp.exp(m2 - m)


def combine(messages, rows):
    groups = messages[0].shape[1] // (4 * rows)
    tops, lows = [], []
    for step, message in zip(ORDER, messages):
        at = [(g * 4 + ORDER.index((k - step) % 4)) * rows for g in range(groups) for k in ORDER]
        tops.append(jnp.concatenate([message[0:1, p : p + rows] for p in at], 1))
        lows.append(jnp.concatenate([message[1:2, p : p + rows] for p in at], 1))
    top = jnp.maximum(jnp.maximum(tops[0], tops[1]), jnp.maximum(tops[2], tops[3]))
    low = sum(l * jnp.exp(t - top) for t, l in zip(tops, lows))
    return top + jnp.log(low)


def weights_kernel(s, mates, lse_r, c0, c1, c2, c3, cols, near, far, part):
    tall, wide = s.shape
    side = wide // 2
    lse_c = combine((c0, c1, c2, c3), tall // 4)
    ids = cols[...]

    @pl.loop(0, tall // LANES)
    def _(i):
        r = pl.ds(pl.multiple_of(i * LANES, LANES), LANES)
        v = s[r, :]
        hit = ids == mates[r, 0:1]
        w = jnp.exp(v - column(lse_r[0:1, r], LANES)) + jnp.exp(v - lse_c)
        w = (w - jnp.where(hit, F32(2.0), F32(0.0))).astype(BF16)
        near[r, :] = w[:, :side]
        far[r, :] = w[:, side:]

    part[...] = c0[2:3, 0:LANES] + c1[2:3, 0:LANES] + c2[2:3, 0:LANES] + c3[2:3, 0:LANES]


def pack(dst, at, g):
    n, w = g.shape
    m = jnp.maximum(jnp.max(jnp.abs(g), axis=1, keepdims=True), F32(1e-30))
    k = jnp.ceil(jnp.log(m) * STEPS)
    q = (g * (LEVELS * jnp.exp(k * (-1.0 / STEPS))) + F32(12582912.0)) - F32(12582912.0)
    dst[at : at + n, 0:w] = q.astype(jnp.int32).astype(I16)
    dst[at : at + n, w : w + LANES] = jnp.broadcast_to(k, (n, LANES)).astype(jnp.int32).astype(I16)


def unpack(src, at, n):
    w = src.shape[1] - LANES
    k = src[at : at + n, w : w + LANES].astype(jnp.int32).astype(F32)[:, :1]
    q = src[at : at + n, 0:w].astype(jnp.int32).astype(F32)
    return q * (jnp.exp(k * (1.0 / STEPS)) * (1.0 / LEVELS))


def hand_out(acc, fwd, bwd, keep1, keep3, own):
    rows = own.shape[0]
    cut = rows // 2
    pack(fwd, 0, acc[3 * rows : 3 * rows + cut, :])
    pack(fwd, cut, acc[rows + cut : 2 * rows, :])
    pack(bwd, 0, acc[3 * rows + cut : 4 * rows, :])
    pack(bwd, cut, acc[2 * rows : 2 * rows + cut, :])
    keep1[...] = acc[rows : rows + cut, :]
    keep3[...] = acc[2 * rows + cut : 3 * rows, :]
    own[...] = acc[0:rows, :]


def z_kernel(near, far, b, o, fwd, bwd, keep1, keep3, own, acc):
    w = acc.shape[1]
    acc[...] = dot(near[...], b[:, :w], NN) + dot(far[...], o[:, :w], NN)
    hand_out(acc, fwd, bwd, keep1, keep3, own)


def x_kernel(near, far, a, o, fwd, bwd, keep1, keep3, own, acc):
    w = a.shape[1] - acc.shape[1]
    acc[...] = dot(near[...], a[:, w:], TN) + dot(far[...], o[...], TN)
    hand_out(acc, fwd, bwd, keep1, keep3, own)


def forward_kernel(fwd, bwd, keep1, keep3, to_up, to_down):
    cut = keep1.shape[0]
    pack(to_up, 0, unpack(fwd, 0, cut) + keep1[...])
    pack(to_down, 0, unpack(bwd, 0, cut) + keep3[...])


def finish_kernel(mult, e, oz, fz, bz, uz, dz, ox, fx, bx, ux, dx, grad):
    cut, half = e.shape[0] // 2, oz.shape[1]
    for h in (0, 1):
        r = slice(h * cut, (h + 1) * cut)
        terms = []
        for own, f, b, u, d in ((oz, fz, bz, uz, dz), (ox, fx, bx, ux, dx)):
            step, straight = (u, b) if h == 0 else (d, f)
            terms.append(own[r, :] + unpack(step, 0, cut) + unpack(straight, cut, cut))
        g0, g1 = mult[0] * terms[0], mult[0] * terms[1]
        e0, e1 = e[r, :half].astype(F32), e[r, half:].astype(F32)
        square = jnp.sum(e0 * e0, axis=1, keepdims=True) + jnp.sum(e1 * e1, axis=1, keepdims=True)
        factor = lax.rsqrt(square + 1e-06)
        inner = jnp.sum(e0 * g0, axis=1, keepdims=True) + jnp.sum(e1 * g1, axis=1, keepdims=True)
        scale = factor * factor * factor * inner
        grad[r, :half] = (factor * g0 - scale * e0).astype(BF16)
        grad[r, half:] = (factor * g1 - scale * e1).astype(BF16)


def local(embeddings, partner, logit_scale):
    rows, width = embeddings.shape
    cut, side = rows // 2, 4 * rows
    total = rows * 2 * X * Z
    c, x, z = lax.axis_index("c"), lax.axis_index("x"), lax.axis_index("z")

    emb = swap(embeddings)
    mate = swap(partner.reshape(1, rows)).reshape(rows, 1)
    digits = jnp.concatenate([mate // 64, mate % 64, jnp.zeros((rows, LANES - 2), jnp.int32)], 1)
    wide = shape(rows, width + LANES, dtype=BF16)
    u, v = call(unit_kernel, "unit", (emb, digits.astype(BF16)), (emb, wide))

    zu, zd, xu, xd = lax.optimization_barrier((up(v, "z"), down(v, "z"), up(u, "x"), down(u, "x")))
    half_z, half_x = shape(cut, width + LANES, dtype=BF16), shape(cut, width, dtype=BF16)
    xa, xb, za, zb = call(
        halves_kernel, "halves", (xu, xd, zu, zd), (half_x, half_x, half_z, half_z)
    )
    xa, xb, za, zb = lax.optimization_barrier(
        (up(xa, "x"), down(xb, "x"), up(za, "z"), down(zb, "z"))
    )
    b = stack("stack", u, xd, xu, xa, xb)
    bo = other_core(b)
    along = {"z": width * 9 // 16, "x": width * 7 // 16}
    flops = 2 * side * side * width
    a, last, mates, early = call(
        early_kernel, "early", (v, zd, zu, za, zb, b),
        (
            shape(side, width, dtype=BF16), shape(side, along["x"], dtype=BF16),
            shape(side, LANES), shape(side, side),
        ),
        flops=flops,
    )
    within = jnp.arange(rows, dtype=jnp.int32)
    cols = jnp.concatenate(
        [((cc * X + (x + k) % X) * Z + z) * rows + within for cc in (c, 1 - c) for k in ORDER]
    ).reshape(1, -1).astype(F32)
    last_other = other_core(after(last, bo))
    scores, rstat, cstat = call(
        tail_kernel, "tail", (logit_scale, a, bo, early, mates, cols),
        (shape(side, 2 * side), shape(8, side), shape(8, 2 * side)), flops=flops,
    )
    cstat_other = other_core(cstat)
    rstats = gather_small(rstat, "z")
    merged, lse_r = call(merge_kernel, "merge", (cstat, cstat_other, *rstats), (cstat, rstat))
    cstats = gather_small(merged, "x")
    near, far, part = call(
        weights_kernel, "weights", (scores, mates, lse_r, *cstats, cols),
        (shape(side, side, dtype=BF16), shape(side, side, dtype=BF16), shape(1, LANES)),
    )
    far_other = other_core(far)

    def sizes(axis):
        w = along[axis]
        message, kept = shape(rows, w + LANES, dtype=I16), shape(cut, w)
        return (
            (message, message, kept, kept, shape(rows, w)),
            dict(scratch=[pltpu.VMEM((side, w), F32)], flops=4 * side * side * w, mib=20),
        )

    outs, options = sizes("z")
    fz, bz, k1z, k3z, oz = call(z_kernel, "along_z", (near, far, b, bo), outs, **options)
    fz, bz = up(fz, "z"), down(bz, "z")
    outs, options = sizes("x")
    fx, bx, k1x, k3x, ox = call(x_kernel, "along_x", (near, far_other, a, last_other), outs, **options)
    fx, bx = up(fx, "x"), down(bx, "x")
    short = {i: shape(cut, w + LANES, dtype=I16) for i, w in along.items()}
    uz, dz = call(forward_kernel, "forward_z", (fz, bz, k1z, k3z), (short["z"],) * 2)
    uz, dz = up(uz, "z"), down(dz, "z")
    ux, dx = call(forward_kernel, "forward_x", (fx, bx, k1x, k3x), (short["x"],) * 2)
    ux, dx = up(ux, "x"), down(dx, "x")
    grad, = call(
        finish_kernel, "finish",
        (logit_scale, emb, oz, fz, bz, uz, dz, ox, fx, bx, ux, dx),
        (shape(rows, width, dtype=BF16),),
    )
    part = after(part, grad)
    both = swap(part) + lax.ppermute(part, ("yl", "c"), SWAP_OTHER)
    return swap(grad), (both[0, :1] / total)


def solution(mesh):
    fine = Mesh(
        mesh.devices.reshape(2, X, Z, 2, 2), ("yl", "x", "z", "yh", "c")
    )
    rows = ("yh", "c", "yl", "x", "z")
    return jax.shard_map(
        local,
        mesh=fine,
        in_specs=(P(rows, None), P(rows), P()),
        out_specs=(P(rows, None), P(("yh", "c"))),
        check_vma=False,
    )
```

time: 200 us -> 176 us (0.88)
  Pallas kernels: 50.5 us -> 30.2 us
  starting transfers between devices: 56.6 us -> 52 us
  local copies, waits for them, and re-layouts: 7.59 us -> 11 us
  waiting for transfers between devices: 81.6 us -> 79.6 us
    pallas_call x14 -> x12, Pallas kernels: 50.5 us -> 30.2 us  [call(): pl.pallas_call(kernel, name=name, out_shape=tuple((jax.ShapeDtypeStruct(o...]
    ppermute x8, waiting for transfers between devices: 29.2 us -> 45.5 us  [up(): return lax.ppermute(v, axis, ring(4, 1))]
    ppermute x9 -> x6, waiting for transfers between devices: 16.5 us -> 6.53 us  [gather_small(): return [v] + [lax.ppermute(v, axis, ring(4, -k)) for k in ORDER[1:]]]
    ppermute x4, starting transfers between devices: 25.1 us -> 18.2 us  [swap(): return lax.ppermute(v, ('yl', 'c'), SWAP)]
    ppermute x4, waiting for transfers between devices: 31.9 us -> 27.1 us  [swap(): return lax.ppermute(v, ('yl', 'c'), SWAP)]
    ppermute x8 -> x4, waiting for transfers between devices: 3.95 us -> 0.48 us  [other_core(): return lax.ppermute(v, 'c', ring(2, 1))]
    unnamed x47 -> x17, local copies, waits for them, and re-layouts: 7.48 us -> 10.7 us
    ppermute x8 -> x4, starting transfers between devices: 1.64 us -> 4.05 us  [other_core(): return lax.ppermute(v, 'c', ring(2, 1))]
  transfers between devices with their start and end apart: 38 -> 31, of which waited for: 18 -> 13; matrix products, arithmetic and copies ran while one was open for 0% -> 0% of each run, Pallas kernels for 24% -> 16%
where the time goes in v3:
time: 176 us
  waiting for transfers between devices  79.6 us (45%)
  starting transfers between devices  52 us (30%)
  Pallas kernels  30.2 us (17%)
  local copies, waits for them, and re-layouts  11 us (6%)
  between operations  2.75 us (2%)
    ppermute x8, waiting for transfers between devices, up(): return lax.ppermute(v, axis, ring(4, 1))  45.5 us
    pallas_call x12, Pallas kernels, call(): pl.pallas_call(kernel, name=name, out_shape=tuple((jax.ShapeDtypeStruct(o...  30.2 us
    ppermute x4, waiting for transfers between devices, swap(): return lax.ppermute(v, ('yl', 'c'), SWAP)  27.1 us
    ppermute x4, starting transfers between devices, swap(): return lax.ppermute(v, ('yl', 'c'), SWAP)  18.2 us
    ppermute x8, starting transfers between devices, down(): return lax.ppermute(v, axis, ring(4, -1))  17.2 us
    unnamed x17, local copies, waits for them, and re-layouts  10.7 us
    ppermute x6, waiting for transfers between devices, gather_small(): return [v] + [lax.ppermute(v, axis, ring(4, -k)) for k in ORDER[1:]]  6.53 us
    ppermute x6, starting transfers between devices, gather_small(): return [v] + [lax.ppermute(v, axis, ring(4, -k)) for k in ORDER[1:]]  6.31 us
  transfers between devices with their start and end apart: 31, of which 13 were waited for; matrix products, arithmetic and copies ran while one was open for 0% of the time, Pallas kernels for 16%

profile of v3, /device:TPU:1, one launch (start us, length us, event | category | flops | bytes accessed | tf_op | source)
XLA Modules:
  0.0 175.8 jit_solution(4505840367374341758)
XLA Ops:
  0.6 4.6 %collective-permute-start = (bf16[160,4096]{1,0:T(8,128)(2,1)}, bf16[160,4096]{1,0:T(8,128)(2,1)S(1)}, u32[]{:S(2)}, u32[]{:S(2)}) collective-permute-start(bf16[160,4096]{1,0:T(8,128)(2,1)} %param.3), channel_id=1, source_target_pairs={{0,0},{1,64},{64,1},{65,65},{2,2},{3,66},{66,3},{67,67},{4,4},{5,6... | collective-permute-start | bytes 3932168 | tf_op jit(solution)/shard_map/ppermute | solution.py:30
  7.2 13.8 %collective-permute-done.1 = s32[1,160]{1,0:T(1,128)S(1)} collective-permute-done((s32[1,160]{1,0:T(1,128)}, s32[1,160]{1,0:T(1,128)S(1)}, u32[]{:S(2)}, u32[]{:S(2)}) %collective-permute-start.1) | collective-permute-done | bytes 672 | tf_op jit(solution)/shard_map/ppermute | solution.py:30
  28.5 21.4 %collective-permute-done.4.xu.refs_2_ = bf16[160,4096]{1,0:T(8,128)(2,1)S(1)} collective-permute-done((bf16[160,4096]{1,0:T(8,128)(2,1)S(1)}, bf16[160,4096]{1,0:T(8,128)(2,1)S(1)}, u32[]{:S(2)}, u32[]{:S(2)}) %collective-permute-start.4) | collective-permute-done | bytes 1310752 | tf_op jit(solution)/shard_map/ppermute | solution.py:38
  50.5 2.4 %collective-permute-start.9 = (bf16[80,4224]{1,0:T(8,128)(2,1)S(1)}, bf16[80,4224]{1,0:T(8,128)(2,1)S(1)}, u32[]{:S(2)}, u32[]{:S(2)}) collective-permute-start(bf16[80,4224]{1,0:T(8,128)(2,1)S(1)} %get-tuple-element.53), channel_id=1, source_target_pairs={{0,12},{4,0},{8,4},{12,8},{1,13},{5,1},{9,5},{13,9},{2,14},{6,2},{... | collective-permute-start | bytes 2027528 | tf_op jit(solution)/shard_map/ppermute | solution.py:42
  55.6 8.0 %collective-permute-done.6.refs_3_ = bf16[80,4096]{1,0:T(8,128)(2,1)S(1)} collective-permute-done((bf16[80,4096]{1,0:T(8,128)(2,1)S(1)}, bf16[80,4096]{1,0:T(8,128)(2,1)S(1)}, u32[]{:S(2)}, u32[]{:S(2)}) %collective-permute-start.6) | collective-permute-done | bytes 655392 | tf_op jit(solution)/shard_map/ppermute | solution.py:38
  64.0 5.8 %early.1 = (bf16[640,4096]{1,0:T(8,128)(2,1)S(1)}, bf16[640,1792]{1,0:T(8,128)(2,1)}, f32[640,128]{1,0:T(8,128)S(1)}, f32[640,640]{1,0:T(8,128)S(1)}) custom-call(bf16[160,4224]{1,0:T(8,128)(2,1)S(1)} %get-tuple-element.44.v, bf16[160,4224]{1,0:T(8,128)(2,1)S(1)} %collective-permute-done.3.zd, bf16[160,4224]{1,0:T(8,128)(2,1)S(1)} %collective-permute-done.2.zu, ...), custom_call_target="tpu_custom_call" | custom-call | flops 3355443200 | bytes 20152320 | tf_op jit(solution)/shard_map/early/pallas_call | solution.py:65
  69.8 2.3 %copy-done = bf16[640,4096]{1,0:T(8,128)(2,1)} copy-done((bf16[640,4096]{1,0:T(8,128)(2,1)}, bf16[640,4096]{1,0:T(8,128)(2,1)S(1)}, u32[]{:S(2)}) %copy-start) | copy-done | bytes 5242904
  72.7 2.3 %copy-done.4 = bf16[640,4096]{1,0:T(8,128)(2,1)} copy-done((bf16[640,4096]{1,0:T(8,128)(2,1)}, bf16[640,4096]{1,0:T(8,128)(2,1)S(1)}, u32[]{:S(2)}) %copy-start.4) | copy-done | bytes 5242904
  75.9 2.5 %copy-done.1 = bf16[640,4096]{1,0:T(8,128)(2,1)S(1)} copy-done((bf16[640,4096]{1,0:T(8,128)(2,1)S(1)}, bf16[640,4096]{1,0:T(8,128)(2,1)}, u32[]{:S(2)}) %copy-start.1) | copy-done | bytes 5242904
  78.4 2.5 %copy-done.5 = bf16[640,4096]{1,0:T(8,128)(2,1)S(1)} copy-done((bf16[640,4096]{1,0:T(8,128)(2,1)S(1)}, bf16[640,4096]{1,0:T(8,128)(2,1)}, u32[]{:S(2)}) %copy-start.5) | copy-done | bytes 5242904
  80.9 7.1 %tail.1 = (f32[640,1280]{1,0:T(8,128)S(1)}, f32[8,640]{1,0:T(8,128)S(1)}, f32[8,1280]{1,0:T(8,128)S(1)}) custom-call(f32[1]{0:T(128)S(6)} %copy.10.mult, bf16[640,4096]{1,0:T(8,128)(2,1)S(1)} %copy-done.1, bf16[640,4096]{1,0:T(8,128)(2,1)S(1)} %copy-done.5, f32[640,640]{1,0:T(8,128)S(1)} %get-tuple-element.59.early, f32[640,128]{1,0:T(8,128)S(1)} %get-tuple-element.60.mates, ...), custom_call_target="tpu_custom_call" | custom-call | flops 3355443200 | bytes 15795204 | tf_op jit(solution)/shard_map/tail/pallas_call | solution.py:65
  94.3 2.7 %collective-permute-start.15 = (f32[8,1280]{1,0:T(8,128)S(1)}, f32[8,1280]{1,0:T(8,128)S(1)}, u32[]{:S(2)}, u32[]{:S(2)}) collective-permute-start(f32[8,1280]{1,0:T(8,128)S(1)} %get-tuple-element.65.c0), channel_id=1, source_target_pairs={{0,48},{16,0},{32,16},{48,32},{1,49},{17,1},{33,17},{49,33},{2,50}... | collective-permute-start | bytes 122888 | tf_op jit(solution)/shard_map/ppermute | solution.py:50
  98.3 3.2 %collective-permute-done.16.c2 = f32[8,1280]{1,0:T(8,128)S(1)} collective-permute-done((f32[8,1280]{1,0:T(8,128)S(1)}, f32[8,1280]{1,0:T(8,128)S(1)}, u32[]{:S(2)}, u32[]{:S(2)}) %collective-permute-start.16) | collective-permute-done | bytes 40992 | tf_op jit(solution)/shard_map/ppermute | solution.py:50
  103.4 3.4 %collective-permute-start.22 = (bf16[640,640]{1,0:T(8,128)(2,1)S(1)}, bf16[640,640]{1,0:T(8,128)(2,1)S(1)}, u32[]{:S(2)}, u32[]{:S(2)}) collective-permute-start(bf16[640,640]{1,0:T(8,128)(2,1)S(1)} %get-tuple-element.67.far), channel_id=1, source_target_pairs={{0,1},{1,0},{2,3},{3,2},{4,5},{5,4},{6,7},{7,6},{8,9},{9,8},{10,11... | collective-permute-start | bytes 2457608 | tf_op jit(solution)/shard_map/ppermute | solution.py:34
  106.7 5.5 %along_z.1 = (s16[160,2432]{1,0:T(8,128)(2,1)S(1)}, s16[160,2432]{1,0:T(8,128)(2,1)S(1)}, f32[80,2304]{1,0:T(8,128)S(1)}, f32[80,2304]{1,0:T(8,128)S(1)}, f32[160,2304]{1,0:T(8,128)S(1)}) custom-call(bf16[640,640]{1,0:T(8,128)(2,1)S(1)} %get-tuple-element.66.near, bf16[640,640]{1,0:T(8,128)(2,1)S(1)} %get-tuple-element.67.far, ...), custom_call_target="tpu_custom_call" | custom-call | flops 3774873600 | bytes 16629760 | tf_op jit(solution)/shard_map/along_z/pallas_call | solution.py:65
  112.5 2.7 %collective-permute-start.19 = (s16[160,2432]{1,0:T(8,128)(2,1)S(1)}, s16[160,2432]{1,0:T(8,128)(2,1)S(1)}, u32[]{:S(2)}, u32[]{:S(2)}) collective-permute-start(s16[160,2432]{1,0:T(8,128)(2,1)S(1)} %get-tuple-element.70), channel_id=1, source_target_pairs={{0,12},{4,0},{8,4},{12,8},{1,13},{5,1},{9,5},{13,9},{2,14},{6,2},{... | collective-permute-start | bytes 2334728 | tf_op jit(solution)/shard_map/ppermute | solution.py:42
  115.2 6.0 %along_x.1 = (s16[160,1920]{1,0:T(8,128)(2,1)S(1)}, s16[160,1920]{1,0:T(8,128)(2,1)S(1)}, f32[80,1792]{1,0:T(8,128)S(1)}, f32[80,1792]{1,0:T(8,128)S(1)}, f32[160,1792]{1,0:T(8,128)S(1)}) custom-call(bf16[640,640]{1,0:T(8,128)(2,1)S(1)} %get-tuple-element.66.near, bf16[640,640]{1,0:T(8,128)(2,1)S(1)} %collective-permute-done.22.far, ...), custom_call_target="tpu_custom_call" | custom-call | flops 2936012800 | bytes 12697600 | tf_op jit(solution)/shard_map/along_x/pallas_call | solution.py:65
  121.4 2.8 %collective-permute-start.25 = (s16[160,1920]{1,0:T(8,128)(2,1)S(1)}, s16[160,1920]{1,0:T(8,128)(2,1)S(1)}, u32[]{:S(2)}, u32[]{:S(2)}) collective-permute-start(s16[160,1920]{1,0:T(8,128)(2,1)S(1)} %get-tuple-element.79), channel_id=1, source_target_pairs={{0,48},{16,0},{32,16},{48,32},{1,49},{17,1},{33,17},{49,33},{2,50}... | collective-permute-start | bytes 1843208 | tf_op jit(solution)/shard_map/ppermute | solution.py:42
  124.1 8.5 %collective-permute-done.18.fwd.fz = s16[160,2432]{1,0:T(8,128)(2,1)S(1)} collective-permute-done((s16[160,2432]{1,0:T(8,128)(2,1)S(1)}, s16[160,2432]{1,0:T(8,128)(2,1)S(1)}, u32[]{:S(2)}, u32[]{:S(2)}) %collective-permute-start.18) | collective-permute-done | bytes 778272 | tf_op jit(solution)/shard_map/ppermute | solution.py:38
  133.7 2.3 %collective-permute-start.21 = (s16[80,2432]{1,0:T(8,128)(2,1)S(1)}, s16[80,2432]{1,0:T(8,128)(2,1)S(1)}, u32[]{:S(2)}, u32[]{:S(2)}) collective-permute-start(s16[80,2432]{1,0:T(8,128)(2,1)S(1)} %get-tuple-element.74), channel_id=1, source_target_pairs={{0,12},{4,0},{8,4},{12,8},{1,13},{5,1},{9,5},{13,9},{2,14},{6,2},{... | collective-permute-start | bytes 1167368 | tf_op jit(solution)/shard_map/ppermute | solution.py:42
  140.8 3.5 %collective-permute-done.20.uz = s16[80,2432]{1,0:T(8,128)(2,1)S(1)} collective-permute-done((s16[80,2432]{1,0:T(8,128)(2,1)S(1)}, s16[80,2432]{1,0:T(8,128)(2,1)S(1)}, u32[]{:S(2)}, u32[]{:S(2)}) %collective-permute-start.20) | collective-permute-done | bytes 389152 | tf_op jit(solution)/shard_map/ppermute | solution.py:38
  144.3 2.5 %collective-permute-done.26.ux = s16[80,1920]{1,0:T(8,128)(2,1)S(1)} collective-permute-done((s16[80,1920]{1,0:T(8,128)(2,1)S(1)}, s16[80,1920]{1,0:T(8,128)(2,1)S(1)}, u32[]{:S(2)}, u32[]{:S(2)}) %collective-permute-start.26) | collective-permute-done | bytes 307232 | tf_op jit(solution)/shard_map/ppermute | solution.py:38
  148.4 9.7 %collective-permute-start.28 = (bf16[160,4096]{1,0:T(8,128)(2,1)S(1)}, bf16[160,4096]{1,0:T(8,128)(2,1)S(1)}, u32[]{:S(2)}, u32[]{:S(2)}) collective-permute-start(bf16[160,4096]{1,0:T(8,128)(2,1)S(1)} %finish.1), channel_id=1, source_target_pairs={{0,0},{1,64},{64,1},{65,65},{2,2},{3,66},{66,3},{67,67},{4,4},{5,6... | collective-permute-start | bytes 3932168 | tf_op jit(solution)/shard_map/ppermute | solution.py:30
  160.2 13.3 %collective-permute-done.29 = f32[1,128]{1,0:T(1,128)S(1)} collective-permute-done((f32[1,128]{1,0:T(1,128)S(1)}, f32[1,128]{1,0:T(1,128)S(1)}, u32[]{:S(2)}, u32[]{:S(2)}) %collective-permute-start.29) | collective-permute-done | bytes 544 | tf_op jit(solution)/shard_map/ppermute | solution.py:30
  (84 shorter events, 34.4 us)
Async XLA Ops:
  0.6 20.7 %collective-permute-start = (bf16[160,4096]{1,0:T(8,128)(2,1)}, bf16[160,4096]{1,0:T(8,128)(2,1)S(1)}, u32[]{:S(2)}, u32[]{:S(2)}) collective-permute-start(bf16[160,4096]{1,0:T(8,128)(2,1)} %param.3), channel_id=1, source_target_pairs={{0,0},{1,64},{64,1},{65,65},{2,2},{3,66},{66,3},{67,67},{4,4},{5,6... | collective-permute-start | bytes 3932168 | tf_op jit(solution)/shard_map/ppermute | solution.py:30
  5.2 15.8 %collective-permute-start.1 = (s32[1,160]{1,0:T(1,128)}, s32[1,160]{1,0:T(1,128)S(1)}, u32[]{:S(2)}, u32[]{:S(2)}) collective-permute-start(s32[1,160]{1,0:T(1,128)} %bitcast.23), channel_id=1, source_target_pairs={{0,0},{1,64},{64,1},{65,65},{2,2},{3,66},{66,3},{67,67},{4,4},{5,6... | collective-permute-start | bytes 1928 | tf_op jit(solution)/shard_map/ppermute | solution.py:30
  21.9 28.0 %collective-permute-start.2 = (bf16[160,4224]{1,0:T(8,128)(2,1)S(1)}, bf16[160,4224]{1,0:T(8,128)(2,1)S(1)}, u32[]{:S(2)}, u32[]{:S(2)}) collective-permute-start(bf16[160,4224]{1,0:T(8,128)(2,1)S(1)} %get-tuple-element.44.v), channel_id=1, source_target_pairs={{0,4},{4,8},{8,12},{12,0},{1,5},{5,9},{9,13},{13,1},{2,6},{6,10},{... | collective-permute-start | bytes 4055048 | tf_op jit(solution)/shard_map/ppermute | solution.py:38
  23.6 26.3 %collective-permute-start.3 = (bf16[160,4224]{1,0:T(8,128)(2,1)S(1)}, bf16[160,4224]{1,0:T(8,128)(2,1)S(1)}, u32[]{:S(2)}, u32[]{:S(2)}) collective-permute-start(bf16[160,4224]{1,0:T(8,128)(2,1)S(1)} %get-tuple-element.44.v), channel_id=1, source_target_pairs={{0,12},{4,0},{8,4},{12,8},{1,13},{5,1},{9,5},{13,9},{2,14},{6,2},{... | collective-permute-start | bytes 4055048 | tf_op jit(solution)/shard_map/ppermute | solution.py:42
  25.8 24.1 %collective-permute-start.4 = (bf16[160,4096]{1,0:T(8,128)(2,1)S(1)}, bf16[160,4096]{1,0:T(8,128)(2,1)S(1)}, u32[]{:S(2)}, u32[]{:S(2)}) collective-permute-start(bf16[160,4096]{1,0:T(8,128)(2,1)S(1)} %get-tuple-element.45.refs_0_), channel_id=1, source_target_pairs={{0,16},{16,32},{32,48},{48,0},{1,17},{17,33},{33,49},{49,1},{2,18}... | collective-permute-start | bytes 3932168 | tf_op jit(solution)/shard_map/ppermute | solution.py:38
  27.1 22.9 %collective-permute-start.5 = (bf16[160,4096]{1,0:T(8,128)(2,1)S(1)}, bf16[160,4096]{1,0:T(8,128)(2,1)S(1)}, u32[]{:S(2)}, u32[]{:S(2)}) collective-permute-start(bf16[160,4096]{1,0:T(8,128)(2,1)S(1)} %get-tuple-element.45.refs_0_), channel_id=1, source_target_pairs={{0,48},{16,0},{32,16},{48,32},{1,49},{17,1},{33,17},{49,33},{2,50}... | collective-permute-start | bytes 3932168 | tf_op jit(solution)/shard_map/ppermute | solution.py:42
  50.1 13.4 %collective-permute-start.8 = (bf16[80,4224]{1,0:T(8,128)(2,1)S(1)}, bf16[80,4224]{1,0:T(8,128)(2,1)S(1)}, u32[]{:S(2)}, u32[]{:S(2)}) collective-permute-start(bf16[80,4224]{1,0:T(8,128)(2,1)S(1)} %get-tuple-element.52), channel_id=1, source_target_pairs={{0,4},{4,8},{8,12},{12,0},{1,5},{5,9},{9,13},{13,1},{2,6},{6,10},{... | collective-permute-start | bytes 2027528 | tf_op jit(solution)/shard_map/ppermute | solution.py:38
  50.5 13.0 %collective-permute-start.9 = (bf16[80,4224]{1,0:T(8,128)(2,1)S(1)}, bf16[80,4224]{1,0:T(8,128)(2,1)S(1)}, u32[]{:S(2)}, u32[]{:S(2)}) collective-permute-start(bf16[80,4224]{1,0:T(8,128)(2,1)S(1)} %get-tuple-element.53), channel_id=1, source_target_pairs={{0,12},{4,0},{8,4},{12,8},{1,13},{5,1},{9,5},{13,9},{2,14},{6,2},{... | collective-permute-start | bytes 2027528 | tf_op jit(solution)/shard_map/ppermute | solution.py:42
  52.9 10.6 %collective-permute-start.6 = (bf16[80,4096]{1,0:T(8,128)(2,1)S(1)}, bf16[80,4096]{1,0:T(8,128)(2,1)S(1)}, u32[]{:S(2)}, u32[]{:S(2)}) collective-permute-start(bf16[80,4096]{1,0:T(8,128)(2,1)S(1)} %get-tuple-element.50), channel_id=1, source_target_pairs={{0,16},{16,32},{32,48},{48,0},{1,17},{17,33},{33,49},{49,1},{2,18}... | collective-permute-start | bytes 1966088 | tf_op jit(solution)/shard_map/ppermute | solution.py:38
  54.1 9.4 %collective-permute-start.7 = (bf16[80,4096]{1,0:T(8,128)(2,1)S(1)}, bf16[80,4096]{1,0:T(8,128)(2,1)S(1)}, u32[]{:S(2)}, u32[]{:S(2)}) collective-permute-start(bf16[80,4096]{1,0:T(8,128)(2,1)S(1)} %get-tuple-element.51), channel_id=1, source_target_pairs={{0,48},{16,0},{32,16},{48,32},{1,49},{17,1},{33,17},{49,33},{2,50}... | collective-permute-start | bytes 1966088 | tf_op jit(solution)/shard_map/ppermute | solution.py:42
  63.9 8.7 %collective-permute-start.10 = (bf16[640,4096]{1,0:T(8,128)(2,1)S(1)}, bf16[640,4096]{1,0:T(8,128)(2,1)S(1)}, u32[]{:S(2)}, u32[]{:S(2)}) collective-permute-start(bf16[640,4096]{1,0:T(8,128)(2,1)S(1)} %stack.1.b), channel_id=1, source_target_pairs={{0,1},{1,0},{2,3},{3,2},{4,5},{5,4},{6,7},{7,6},{8,9},{9,8},{10,11... | collective-permute-start | bytes 15728648 | tf_op jit(solution)/shard_map/ppermute | solution.py:34
  74.9 40.2 %collective-permute-start.23 = (bf16[640,1792]{1,0:T(8,128)(2,1)}, bf16[640,1792]{1,0:T(8,128)(2,1)}, u32[]{:S(2)}, u32[]{:S(2)}) collective-permute-start(bf16[640,1792]{1,0:T(8,128)(2,1)} %get-tuple-element.76), channel_id=1, source_target_pairs={{0,1},{1,0},{2,3},{3,2},{4,5},{5,4},{6,7},{7,6},{8,9},{9,8},{10,11... | collective-permute-start | bytes 6881288 | tf_op jit(solution)/shard_map/ppermute | solution.py:34
  103.4 11.8 %collective-permute-start.22 = (bf16[640,640]{1,0:T(8,128)(2,1)S(1)}, bf16[640,640]{1,0:T(8,128)(2,1)S(1)}, u32[]{:S(2)}, u32[]{:S(2)}) collective-permute-start(bf16[640,640]{1,0:T(8,128)(2,1)S(1)} %get-tuple-element.67.far), channel_id=1, source_target_pairs={{0,1},{1,0},{2,3},{3,2},{4,5},{5,4},{6,7},{7,6},{8,9},{9,8},{10,11... | collective-permute-start | bytes 2457608 | tf_op jit(solution)/shard_map/ppermute | solution.py:34
  112.2 20.5 %collective-permute-start.18 = (s16[160,2432]{1,0:T(8,128)(2,1)S(1)}, s16[160,2432]{1,0:T(8,128)(2,1)S(1)}, u32[]{:S(2)}, u32[]{:S(2)}) collective-permute-start(s16[160,2432]{1,0:T(8,128)(2,1)S(1)} %get-tuple-element.69), channel_id=1, source_target_pairs={{0,4},{4,8},{8,12},{12,0},{1,5},{5,9},{9,13},{13,1},{2,6},{6,10},{... | collective-permute-start | bytes 2334728 | tf_op jit(solution)/shard_map/ppermute | solution.py:38
  112.5 20.2 %collective-permute-start.19 = (s16[160,2432]{1,0:T(8,128)(2,1)S(1)}, s16[160,2432]{1,0:T(8,128)(2,1)S(1)}, u32[]{:S(2)}, u32[]{:S(2)}) collective-permute-start(s16[160,2432]{1,0:T(8,128)(2,1)S(1)} %get-tuple-element.70), channel_id=1, source_target_pairs={{0,12},{4,0},{8,4},{12,8},{1,13},{5,1},{9,5},{13,9},{2,14},{6,2},{... | collective-permute-start | bytes 2334728 | tf_op jit(solution)/shard_map/ppermute | solution.py:42
  121.2 16.4 %collective-permute-start.24 = (s16[160,1920]{1,0:T(8,128)(2,1)S(1)}, s16[160,1920]{1,0:T(8,128)(2,1)S(1)}, u32[]{:S(2)}, u32[]{:S(2)}) collective-permute-start(s16[160,1920]{1,0:T(8,128)(2,1)S(1)} %get-tuple-element.78), channel_id=1, source_target_pairs={{0,16},{16,32},{32,48},{48,0},{1,17},{17,33},{33,49},{49,1},{2,18}... | collective-permute-start | bytes 1843208 | tf_op jit(solution)/shard_map/ppermute | solution.py:38
  121.4 16.2 %collective-permute-start.25 = (s16[160,1920]{1,0:T(8,128)(2,1)S(1)}, s16[160,1920]{1,0:T(8,128)(2,1)S(1)}, u32[]{:S(2)}, u32[]{:S(2)}) collective-permute-start(s16[160,1920]{1,0:T(8,128)(2,1)S(1)} %get-tuple-element.79), channel_id=1, source_target_pairs={{0,48},{16,0},{32,16},{48,32},{1,49},{17,1},{33,17},{49,33},{2,50}... | collective-permute-start | bytes 1843208 | tf_op jit(solution)/shard_map/ppermute | solution.py:42
  133.3 11.0 %collective-permute-start.20 = (s16[80,2432]{1,0:T(8,128)(2,1)S(1)}, s16[80,2432]{1,0:T(8,128)(2,1)S(1)}, u32[]{:S(2)}, u32[]{:S(2)}) collective-permute-start(s16[80,2432]{1,0:T(8,128)(2,1)S(1)} %get-tuple-element.73), channel_id=1, source_target_pairs={{0,4},{4,8},{8,12},{12,0},{1,5},{5,9},{9,13},{13,1},{2,6},{6,10},{... | collective-permute-start | bytes 1167368 | tf_op jit(solution)/shard_map/ppermute | solution.py:38
  133.7 10.5 %collective-permute-start.21 = (s16[80,2432]{1,0:T(8,128)(2,1)S(1)}, s16[80,2432]{1,0:T(8,128)(2,1)S(1)}, u32[]{:S(2)}, u32[]{:S(2)}) collective-permute-start(s16[80,2432]{1,0:T(8,128)(2,1)S(1)} %get-tuple-element.74), channel_id=1, source_target_pairs={{0,12},{4,0},{8,4},{12,8},{1,13},{5,1},{9,5},{13,9},{2,14},{6,2},{... | collective-permute-start | bytes 1167368 | tf_op jit(solution)/shard_map/ppermute | solution.py:42
  138.0 8.8 %collective-permute-start.26 = (s16[80,1920]{1,0:T(8,128)(2,1)S(1)}, s16[80,1920]{1,0:T(8,128)(2,1)S(1)}, u32[]{:S(2)}, u32[]{:S(2)}) collective-permute-start(s16[80,1920]{1,0:T(8,128)(2,1)S(1)} %get-tuple-element.82), channel_id=1, source_target_pairs={{0,16},{16,32},{32,48},{48,0},{1,17},{17,33},{33,49},{49,1},{2,18}... | collective-permute-start | bytes 921608 | tf_op jit(solution)/shard_map/ppermute | solution.py:38
  138.8 8.0 %collective-permute-start.27 = (s16[80,1920]{1,0:T(8,128)(2,1)S(1)}, s16[80,1920]{1,0:T(8,128)(2,1)S(1)}, u32[]{:S(2)}, u32[]{:S(2)}) collective-permute-start(s16[80,1920]{1,0:T(8,128)(2,1)S(1)} %get-tuple-element.83), channel_id=1, source_target_pairs={{0,48},{16,0},{32,16},{48,32},{1,49},{17,1},{33,17},{49,33},{2,50}... | collective-permute-start | bytes 921608 | tf_op jit(solution)/shard_map/ppermute | solution.py:42
  148.4 25.1 %collective-permute-start.28 = (bf16[160,4096]{1,0:T(8,128)(2,1)S(1)}, bf16[160,4096]{1,0:T(8,128)(2,1)S(1)}, u32[]{:S(2)}, u32[]{:S(2)}) collective-permute-start(bf16[160,4096]{1,0:T(8,128)(2,1)S(1)} %finish.1), channel_id=1, source_target_pairs={{0,0},{1,64},{64,1},{65,65},{2,2},{3,66},{66,3},{67,67},{4,4},{5,6... | collective-permute-start | bytes 3932168 | tf_op jit(solution)/shard_map/ppermute | solution.py:30
  158.2 15.3 %collective-permute-start.29 = (f32[1,128]{1,0:T(1,128)S(1)}, f32[1,128]{1,0:T(1,128)S(1)}, u32[]{:S(2)}, u32[]{:S(2)}) collective-permute-start(f32[1,128]{1,0:T(1,128)S(1)} %get-tuple-element.85), channel_id=1, source_target_pairs={{0,0},{1,64},{64,1},{65,65},{2,2},{3,66},{66,3},{67,67},{4,4},{5,6... | collective-permute-start | bytes 1544 | tf_op jit(solution)/shard_map/ppermute | solution.py:30
  160.1 13.4 %collective-permute-start.30 = (f32[1,128]{1,0:T(1,128)S(1)}, f32[1,128]{1,0:T(1,128)S(1)}, u32[]{:S(2)}, u32[]{:S(2)}) collective-permute-start(f32[1,128]{1,0:T(1,128)S(1)} %get-tuple-element.85), channel_id=1, source_target_pairs={{1,0},{65,1},{0,64},{64,65},{3,2},{67,3},{2,66},{66,67},{5,4},{69,... | collective-permute-start | bytes 1544 | tf_op jit(solution)/shard_map/ppermute | solution.py:349
  (15 other events, 93.2 us)

commit v4 on v3

--- a/solution.py
+++ b/solution.py
@@ -98,7 +98,15 @@
     return call(stack_kernel, name, refs, (out,))[0]
 
 
-def unit_kernel(e, digits, u, v):
+def unit_kernel(e, digits, u, v, cols):
+    rows = e.shape[0]
+    c, x, z = lax.axis_index("c"), lax.axis_index("x"), lax.axis_index("z")
+    within = lax.broadcasted_iota(jnp.int32, (1, rows), 1)
+    for i, cc in enumerate((c, 1 - c)):
+        for j, k in enumerate(ORDER):
+            first = ((cc * X + lax.rem(x + k, X)) * Z + z) * rows
+            at = (4 * i + j) * rows
+            cols[:, at : at + rows] = (first + within).astype(F32)
     wide = e[...].astype(F32)
     unit = wide * lax.rsqrt(jnp.sum(wide * wide, axis=1, keepdims=True) + 1e-06)
     u[...] = unit.astype(BF16)
@@ -222,43 +230,59 @@
     return q * (jnp.exp(k * (1.0 / STEPS)) * (1.0 / LEVELS))
 
 
-def hand_out(acc, fwd, bwd, keep1, keep3, own):
+def hand_out(acc, late_fwd, late_bwd, keep1, keep3, own):
     rows = own.shape[0]
     cut = rows // 2
-    pack(fwd, 0, acc[3 * rows : 3 * rows + cut, :])
-    pack(fwd, cut, acc[rows + cut : 2 * rows, :])
-    pack(bwd, 0, acc[3 * rows + cut : 4 * rows, :])
-    pack(bwd, cut, acc[2 * rows : 2 * rows + cut, :])
+    pack(late_fwd, 0, acc[rows + cut : 2 * rows, :])
+    pack(late_bwd, 0, acc[2 * rows : 2 * rows + cut, :])
     keep1[...] = acc[rows : rows + cut, :]
     keep3[...] = acc[2 * rows + cut : 3 * rows, :]
     own[...] = acc[0:rows, :]
 
 
-def z_kernel(near, far, b, o, fwd, bwd, keep1, keep3, own, acc):
-    w = acc.shape[1]
-    acc[...] = dot(near[...], b[:, :w], NN) + dot(far[...], o[:, :w], NN)
-    hand_out(acc, fwd, bwd, keep1, keep3, own)
-
-
-def x_kernel(near, far, a, o, fwd, bwd, keep1, keep3, own, acc):
-    w = a.shape[1] - acc.shape[1]
-    acc[...] = dot(near[...], a[:, w:], TN) + dot(far[...], o[...], TN)
-    hand_out(acc, fwd, bwd, keep1, keep3, own)
-
-
-def forward_kernel(fwd, bwd, keep1, keep3, to_up, to_down):
+def z_first_kernel(near, far, b, o, fwd, bwd, acc):
+    n, w = acc.shape
+    r = slice(near.shape[0] - n, None)
+    acc[...] = dot(near[r, :], b[:, :w], NN) + dot(far[r, :], o[:, :w], NN)
+    pack(fwd, 0, acc[0 : n // 2, :])
+    pack(bwd, 0, acc[n // 2 :, :])
+
+
+def z_kernel(near, far, b, o, late_fwd, late_bwd, keep1, keep3, own, acc):
+    n, w = acc.shape
+    acc[...] = dot(near[0:n, :], b[:, :w], NN) + dot(far[0:n, :], o[:, :w], NN)
+    hand_out(acc, late_fwd, late_bwd, keep1, keep3, own)
+
+
+def x_first_kernel(near, far, a, o, fwd, bwd, acc):
+    n, w = acc.shape[0], a.shape[1] - acc.shape[1]
+    r = slice(near.shape[1] - n, None)
+    acc[...] = dot(near[:, r], a[:, w:], TN) + dot(far[:, r], o[...], TN)
+    pack(fwd, 0, acc[0 : n // 2, :])
+    pack(bwd, 0, acc[n // 2 :, :])
+
+
+def x_kernel(near, far, a, o, late_fwd, late_bwd, keep1, keep3, own, acc):
+    n, w = acc.shape[0], a.shape[1] - acc.shape[1]
+    acc[...] = dot(near[:, 0:n], a[:, w:], TN) + dot(far[:, 0:n], o[...], TN)
+    hand_out(acc, late_fwd, late_bwd, keep1, keep3, own)
+
+
+def forward_kernel(fwd, bwd, late_fwd, late_bwd, keep1, keep3, to_up, to_down):
     cut = keep1.shape[0]
     pack(to_up, 0, unpack(fwd, 0, cut) + keep1[...])
     pack(to_down, 0, unpack(bwd, 0, cut) + keep3[...])
-
-
-def finish_kernel(mult, e, oz, fz, bz, uz, dz, ox, fx, bx, ux, dx, grad):
+    to_up[cut:, :] = late_fwd[...]
+    to_down[cut:, :] = late_bwd[...]
+
+
+def finish_kernel(mult, e, oz, uz, dz, ox, ux, dx, grad):
     cut, half = e.shape[0] // 2, oz.shape[1]
     for h in (0, 1):
         r = slice(h * cut, (h + 1) * cut)
         terms = []
-        for own, f, b, u, d in ((oz, fz, bz, uz, dz), (ox, fx, bx, ux, dx)):
-            step, straight = (u, b) if h == 0 else (d, f)
+        for own, u, d in ((oz, uz, dz), (ox, ux, dx)):
+            step, straight = (u, d) if h == 0 else (d, u)
             terms.append(own[r, :] + unpack(step, 0, cut) + unpack(straight, cut, cut))
         g0, g1 = mult[0] * terms[0], mult[0] * terms[1]
         e0, e1 = e[r, :half].astype(F32), e[r, half:].astype(F32)
@@ -274,13 +298,14 @@
     rows, width = embeddings.shape
     cut, side = rows // 2, 4 * rows
     total = rows * 2 * X * Z
-    c, x, z = lax.axis_index("c"), lax.axis_index("x"), lax.axis_index("z")
 
     emb = swap(embeddings)
     mate = swap(partner.reshape(1, rows)).reshape(rows, 1)
     digits = jnp.concatenate([mate // 64, mate % 64, jnp.zeros((rows, LANES - 2), jnp.int32)], 1)
     wide = shape(rows, width + LANES, dtype=BF16)
-    u, v = call(unit_kernel, "unit", (emb, digits.astype(BF16)), (emb, wide))
+    u, v, cols = call(
+        unit_kernel, "unit", (emb, digits.astype(BF16)), (emb, wide, shape(1, 2 * side))
+    )
 
     zu, zd, xu, xd = lax.optimization_barrier((up(v, "z"), down(v, "z"), up(u, "x"), down(u, "x")))
     half_z, half_x = shape(cut, width + LANES, dtype=BF16), shape(cut, width, dtype=BF16)
@@ -302,10 +327,6 @@
         ),
         flops=flops,
     )
-    within = jnp.arange(rows, dtype=jnp.int32)
-    cols = jnp.concatenate(
-        [((cc * X + (x + k) % X) * Z + z) * rows + within for cc in (c, 1 - c) for k in ORDER]
-    ).reshape(1, -1).astype(F32)
     last_other = other_core(after(last, bo))
     scores, rstat, cstat = call(
         tail_kernel, "tail", (logit_scale, a, bo, early, mates, cols),
@@ -321,28 +342,35 @@
     )
     far_other = other_core(far)
 
-    def sizes(axis):
+    def terms(kernels, axis, operands):
         w = along[axis]
-        message, kept = shape(rows, w + LANES, dtype=I16), shape(cut, w)
-        return (
-            (message, message, kept, kept, shape(rows, w)),
-            dict(scratch=[pltpu.VMEM((side, w), F32)], flops=4 * side * side * w, mib=20),
+        message, kept = shape(cut, w + LANES, dtype=I16), shape(cut, w)
+        flops = 4 * side * rows * w
+        first = lambda *o: call(
+            kernels[0], "first_" + axis, o, (message, message),
+            scratch=[pltpu.VMEM((rows, w), F32)], flops=flops,
         )
-
-    outs, options = sizes("z")
-    fz, bz, k1z, k3z, oz = call(z_kernel, "along_z", (near, far, b, bo), outs, **options)
+        rest = lambda *o: call(
+            kernels[1], "rest_" + axis, o, (message, message, kept, kept, shape(rows, w)),
+            scratch=[pltpu.VMEM((3 * rows, w), F32)], flops=3 * flops, mib=18,
+        )
+        return first(*operands), rest
+
+    operands_z, operands_x = (near, far, b, bo), (near, far_other, a, last_other)
+    (fz, bz), rest_z = terms((z_first_kernel, z_kernel), "z", operands_z)
+    (fx, bx), rest_x = terms((x_first_kernel, x_kernel), "x", operands_x)
+    *kept_z, oz = rest_z(after(near, fx), *operands_z[1:])
+    *kept_x, ox = rest_x(after(near, oz), *operands_x[1:])
     fz, bz = up(fz, "z"), down(bz, "z")
-    outs, options = sizes("x")
-    fx, bx, k1x, k3x, ox = call(x_kernel, "along_x", (near, far_other, a, last_other), outs, **options)
     fx, bx = up(fx, "x"), down(bx, "x")
-    short = {i: shape(cut, w + LANES, dtype=I16) for i, w in along.items()}
-    uz, dz = call(forward_kernel, "forward_z", (fz, bz, k1z, k3z), (short["z"],) * 2)
+    message = {i: shape(rows, w + LANES, dtype=I16) for i, w in along.items()}
+    uz, dz = call(forward_kernel, "forward_z", (fz, bz, *kept_z), (message["z"],) * 2)
     uz, dz = up(uz, "z"), down(dz, "z")
-    ux, dx = call(forward_kernel, "forward_x", (fx, bx, k1x, k3x), (short["x"],) * 2)
+    ux, dx = call(forward_kernel, "forward_x", (fx, bx, *kept_x), (message["x"],) * 2)
     ux, dx = up(ux, "x"), down(dx, "x")
     grad, = call(
         finish_kernel, "finish",
-        (logit_scale, emb, oz, fz, bz, uz, dz, ox, fx, bx, ux, dx),
+        (logit_scale, emb, oz, uz, dz, ox, ux, dx),
         (shape(rows, width, dtype=BF16),),
     )
     part = after(part, grad)

time: 176 us -> 166 us (0.943)
  local copies, waits for them, and re-layouts: 11 us -> 1.25 us
  Pallas kernels: 30.2 us -> 27.9 us
    ppermute x8, waiting for transfers between devices: 0.03 us -> 17.9 us  [down(): return lax.ppermute(v, axis, ring(4, -1))]
    ppermute x8, waiting for transfers between devices: 45.5 us -> 27.9 us  [up(): return lax.ppermute(v, axis, ring(4, 1))]
    unnamed x17 -> x1, local copies, waits for them, and re-layouts: 10.7 us -> 1.06 us
    ppermute x8, starting transfers between devices: 17.2 us -> 22 us  [down(): return lax.ppermute(v, axis, ring(4, -1))]
    ppermute x8, starting transfers between devices: 6.23 us -> 2.05 us  [up(): return lax.ppermute(v, axis, ring(4, 1))]
    ppermute x4, waiting for transfers between devices: 0.48 us -> 4.22 us  [other_core(): return lax.ppermute(v, 'c', ring(2, 1))]
    ppermute x6, waiting for transfers between devices: 6.53 us -> 3.8 us  [gather_small(): return [v] + [lax.ppermute(v, axis, ring(4, -k)) for k in ORDER[1:]]]
    pallas_call x12 -> x14, Pallas kernels: 30.2 us -> 27.9 us  [call(): pl.pallas_call(kernel, name=name, out_shape=tuple((jax.ShapeDtypeStruct(o...]
  transfers between devices with their start and end apart: 31 -> 31, of which waited for: 13 -> 15; matrix products, arithmetic and copies ran while one was open for 0% -> 0% of each run, Pallas kernels for 16% -> 15%
where the time goes in v4:
time: 166 us; the launch traced here: 165 us
  waiting for transfers between devices  80.9 us (49%)
  starting transfers between devices  52.6 us (32%)
  Pallas kernels  27.9 us (17%)
  between operations  2.71 us (2%)
    ppermute x8, waiting for transfers between devices, up(): return lax.ppermute(v, axis, ring(4, 1))  27.9 us
    pallas_call x14, Pallas kernels, call(): pl.pallas_call(kernel, name=name, out_shape=tuple((jax.ShapeDtypeStruct(o...  27.9 us
    ppermute x4, waiting for transfers between devices, swap(): return lax.ppermute(v, ('yl', 'c'), SWAP)  26.6 us
    ppermute x8, starting transfers between devices, down(): return lax.ppermute(v, axis, ring(4, -1))  22 us
    ppermute x8, waiting for transfers between devices, down(): return lax.ppermute(v, axis, ring(4, -1))  17.9 us
    ppermute x4, starting transfers between devices, swap(): return lax.ppermute(v, ('yl', 'c'), SWAP)  17.1 us
    ppermute x6, starting transfers between devices, gather_small(): return [v] + [lax.ppermute(v, axis, ring(4, -k)) for k in ORDER[1:]]  7.72 us
    ppermute x4, waiting for transfers between devices, other_core(): return lax.ppermute(v, 'c', ring(2, 1))  4.22 us
  transfers between devices with their start and end apart: 31, of which 15 were waited for; matrix products, arithmetic and copies ran while one was open for 0% of the time, Pallas kernels for 15%

profile of v4, /device:TPU:1, one launch (start us, length us, event | category | flops | bytes accessed | tf_op | source)
XLA Modules:
  0.0 165.5 jit_solution(8522715308953328911)
XLA Ops:
  0.6 4.6 %collective-permute-start = (bf16[160,4096]{1,0:T(8,128)(2,1)}, bf16[160,4096]{1,0:T(8,128)(2,1)S(1)}, u32[]{:S(2)}, u32[]{:S(2)}) collective-permute-start(bf16[160,4096]{1,0:T(8,128)(2,1)} %param.3), channel_id=1, source_target_pairs={{0,0},{1,64},{64,1},{65,65},{2,2},{3,66},{66,3},{67,67},{4,4},{5,6... | collective-permute-start | bytes 3932168 | tf_op jit(solution)/shard_map/ppermute | solution.py:30
  7.2 13.8 %collective-permute-done.1 = s32[1,160]{1,0:T(1,128)S(1)} collective-permute-done((s32[1,160]{1,0:T(1,128)}, s32[1,160]{1,0:T(1,128)S(1)}, u32[]{:S(2)}, u32[]{:S(2)}) %collective-permute-start.1) | collective-permute-done | bytes 672 | tf_op jit(solution)/shard_map/ppermute | solution.py:30
  22.0 3.8 %collective-permute-start.3 = (bf16[160,4224]{1,0:T(8,128)(2,1)S(1)}, bf16[160,4224]{1,0:T(8,128)(2,1)S(1)}, u32[]{:S(2)}, u32[]{:S(2)}) collective-permute-start(bf16[160,4224]{1,0:T(8,128)(2,1)S(1)} %get-tuple-element.51.v), channel_id=1, source_target_pairs={{0,12},{4,0},{8,4},{12,8},{1,13},{5,1},{9,5},{13,9},{2,14},{6,2},{... | collective-permute-start | bytes 4055048 | tf_op jit(solution)/shard_map/ppermute | solution.py:42
  25.8 2.5 %collective-permute-start.5 = (bf16[160,4096]{1,0:T(8,128)(2,1)S(1)}, bf16[160,4096]{1,0:T(8,128)(2,1)S(1)}, u32[]{:S(2)}, u32[]{:S(2)}) collective-permute-start(bf16[160,4096]{1,0:T(8,128)(2,1)S(1)} %get-tuple-element.52.refs_0_), channel_id=1, source_target_pairs={{0,48},{16,0},{32,16},{48,32},{1,49},{17,1},{33,17},{49,33},{2,50}... | collective-permute-start | bytes 3932168 | tf_op jit(solution)/shard_map/ppermute | solution.py:42
  28.3 17.9 %collective-permute-done.5.xd.refs_1_ = bf16[160,4096]{1,0:T(8,128)(2,1)S(1)} collective-permute-done((bf16[160,4096]{1,0:T(8,128)(2,1)S(1)}, bf16[160,4096]{1,0:T(8,128)(2,1)S(1)}, u32[]{:S(2)}, u32[]{:S(2)}) %collective-permute-start.5) | collective-permute-done | bytes 1310752 | tf_op jit(solution)/shard_map/ppermute | solution.py:42
  46.1 6.2 %collective-permute-done.4.xu.refs_2_ = bf16[160,4096]{1,0:T(8,128)(2,1)S(1)} collective-permute-done((bf16[160,4096]{1,0:T(8,128)(2,1)S(1)}, bf16[160,4096]{1,0:T(8,128)(2,1)S(1)}, u32[]{:S(2)}, u32[]{:S(2)}) %collective-permute-start.4) | collective-permute-done | bytes 1310752 | tf_op jit(solution)/shard_map/ppermute | solution.py:38
  53.0 3.2 %collective-permute-start.9 = (bf16[80,4224]{1,0:T(8,128)(2,1)S(1)}, bf16[80,4224]{1,0:T(8,128)(2,1)S(1)}, u32[]{:S(2)}, u32[]{:S(2)}) collective-permute-start(bf16[80,4224]{1,0:T(8,128)(2,1)S(1)} %get-tuple-element.60), channel_id=1, source_target_pairs={{0,12},{4,0},{8,4},{12,8},{1,13},{5,1},{9,5},{13,9},{2,14},{6,2},{... | collective-permute-start | bytes 2027528 | tf_op jit(solution)/shard_map/ppermute | solution.py:42
  56.2 2.7 %collective-permute-start.7 = (bf16[80,4096]{1,0:T(8,128)(2,1)S(1)}, bf16[80,4096]{1,0:T(8,128)(2,1)S(1)}, u32[]{:S(2)}, u32[]{:S(2)}) collective-permute-start(bf16[80,4096]{1,0:T(8,128)(2,1)S(1)} %get-tuple-element.58), channel_id=1, source_target_pairs={{0,48},{16,0},{32,16},{48,32},{1,49},{17,1},{33,17},{49,33},{2,50}... | collective-permute-start | bytes 1966088 | tf_op jit(solution)/shard_map/ppermute | solution.py:42
  58.9 8.0 %collective-permute-done.6.refs_3_ = bf16[80,4096]{1,0:T(8,128)(2,1)S(1)} collective-permute-done((bf16[80,4096]{1,0:T(8,128)(2,1)S(1)}, bf16[80,4096]{1,0:T(8,128)(2,1)S(1)}, u32[]{:S(2)}, u32[]{:S(2)}) %collective-permute-start.6) | collective-permute-done | bytes 655392 | tf_op jit(solution)/shard_map/ppermute | solution.py:38
  67.3 4.4 %early.1 = (bf16[640,4096]{1,0:T(8,128)(2,1)S(1)}, bf16[640,1792]{1,0:T(8,128)(2,1)S(1)}, f32[640,128]{1,0:T(8,128)S(1)}, f32[640,640]{1,0:T(8,128)S(1)}) custom-call(bf16[160,4224]{1,0:T(8,128)(2,1)S(1)} %get-tuple-element.51.v, bf16[160,4224]{1,0:T(8,128)(2,1)S(1)} %collective-permute-done.3.zd, bf16[160,4224]{1,0:T(8,128)(2,1)S(1)} %collective-permute-done.2.zu, ...), custom_call_target="tpu_custom_call" | custom-call | flops 3355443200 | bytes 20152320 | tf_op jit(solution)/shard_map/early/pallas_call | solution.py:65
  71.7 4.2 %collective-permute-done.10.b.o = bf16[640,4096]{1,0:T(8,128)(2,1)S(1)} collective-permute-done((bf16[640,4096]{1,0:T(8,128)(2,1)S(1)}, bf16[640,4096]{1,0:T(8,128)(2,1)S(1)}, u32[]{:S(2)}, u32[]{:S(2)}) %collective-permute-start.10) | collective-permute-done | bytes 5242912 | tf_op jit(solution)/shard_map/ppermute | solution.py:34
  76.7 7.1 %tail.1 = (f32[640,1280]{1,0:T(8,128)S(1)}, f32[8,640]{1,0:T(8,128)S(1)}, f32[8,1280]{1,0:T(8,128)S(1)}) custom-call(f32[1]{0:T(128)S(6)} %copy.10.mult, bf16[640,4096]{1,0:T(8,128)(2,1)S(1)} %get-tuple-element.65.a, bf16[640,4096]{1,0:T(8,128)(2,1)S(1)} %collective-permute-done.10.b.o, f32[640,640]{1,0:T(8,128)S(1)} %get-tuple-element.66.early, ...), custom_call_target="tpu_custom_call" | custom-call | flops 3355443200 | bytes 15795204 | tf_op jit(solution)/shard_map/tail/pallas_call | solution.py:65
  90.8 2.1 %collective-permute-start.16 = (f32[8,1280]{1,0:T(8,128)S(1)}, f32[8,1280]{1,0:T(8,128)S(1)}, u32[]{:S(2)}, u32[]{:S(2)}) collective-permute-start(f32[8,1280]{1,0:T(8,128)S(1)} %get-tuple-element.73.c0), channel_id=1, source_target_pairs={{0,16},{16,32},{32,48},{48,0},{1,17},{17,33},{33,49},{49,1},{2,18}... | collective-permute-start | bytes 122888 | tf_op jit(solution)/shard_map/ppermute | solution.py:50
  97.9 3.0 %collective-permute-start.18 = (bf16[640,640]{1,0:T(8,128)(2,1)S(1)}, bf16[640,640]{1,0:T(8,128)(2,1)S(1)}, u32[]{:S(2)}, u32[]{:S(2)}) collective-permute-start(bf16[640,640]{1,0:T(8,128)(2,1)S(1)} %get-tuple-element.75.far), channel_id=1, source_target_pairs={{0,1},{1,0},{2,3},{3,2},{4,5},{5,4},{6,7},{7,6},{8,9},{9,8},{10,11... | collective-permute-start | bytes 2457608 | tf_op jit(solution)/shard_map/ppermute | solution.py:34
  103.3 2.4 %collective-permute-start.21 = (s16[80,2432]{1,0:T(8,128)(2,1)S(1)}, s16[80,2432]{1,0:T(8,128)(2,1)S(1)}, u32[]{:S(2)}, u32[]{:S(2)}) collective-permute-start(s16[80,2432]{1,0:T(8,128)(2,1)S(1)} %get-tuple-element.82), channel_id=1, source_target_pairs={{0,12},{4,0},{8,4},{12,8},{1,13},{5,1},{9,5},{13,9},{2,14},{6,2},{... | collective-permute-start | bytes 1167368 | tf_op jit(solution)/shard_map/ppermute | solution.py:42
  107.4 2.7 %collective-permute-start.25 = (s16[80,1920]{1,0:T(8,128)(2,1)S(1)}, s16[80,1920]{1,0:T(8,128)(2,1)S(1)}, u32[]{:S(2)}, u32[]{:S(2)}) collective-permute-start(s16[80,1920]{1,0:T(8,128)(2,1)S(1)} %get-tuple-element.91), channel_id=1, source_target_pairs={{0,48},{16,0},{32,16},{48,32},{1,49},{17,1},{33,17},{49,33},{2,50}... | collective-permute-start | bytes 921608 | tf_op jit(solution)/shard_map/ppermute | solution.py:42
  110.0 3.9 %rest_z.1 = (s16[80,2432]{1,0:T(8,128)(2,1)S(1)}, s16[80,2432]{1,0:T(8,128)(2,1)S(1)}, f32[80,2304]{1,0:T(8,128)S(1)}, f32[80,2304]{1,0:T(8,128)S(1)}, f32[160,2304]{1,0:T(8,128)S(1)}) custom-call(bf16[640,640]{1,0:T(8,128)(2,1)S(1)} %get-tuple-element.89.near, bf16[640,640]{1,0:T(8,128)(2,1)S(1)} %get-tuple-element.75.far, bf16[640,4096]{1,0:T(8,128)(2,1)S(1)} %stack.1.b, ...), custom_call_target="tpu_custom_call" | custom-call | flops 2831155200 | bytes 15851520 | tf_op jit(solution)/shard_map/rest_z/pallas_call | solution.py:65
  116.4 2.0 %collective-permute-start.23 = (s16[160,2432]{1,0:T(8,128)(2,1)S(1)}, s16[160,2432]{1,0:T(8,128)(2,1)S(1)}, u32[]{:S(2)}, u32[]{:S(2)}) collective-permute-start(s16[160,2432]{1,0:T(8,128)(2,1)S(1)} %get-tuple-element.88), channel_id=1, source_target_pairs={{0,12},{4,0},{8,4},{12,8},{1,13},{5,1},{9,5},{13,9},{2,14},{6,2},{... | collective-permute-start | bytes 2334728 | tf_op jit(solution)/shard_map/ppermute | solution.py:42
  118.4 3.2 %rest_x.1 = (s16[80,1920]{1,0:T(8,128)(2,1)S(1)}, s16[80,1920]{1,0:T(8,128)(2,1)S(1)}, f32[80,1792]{1,0:T(8,128)S(1)}, f32[80,1792]{1,0:T(8,128)S(1)}, f32[160,1792]{1,0:T(8,128)S(1)}) custom-call(bf16[640,640]{1,0:T(8,128)(2,1)S(1)} %get-tuple-element.89.near, bf16[640,640]{1,0:T(8,128)(2,1)S(1)} %collective-permute-done.18.far, ...), custom_call_target="tpu_custom_call" | custom-call | flops 2202009600 | bytes 12083200 | tf_op jit(solution)/shard_map/rest_x/pallas_call | solution.py:65
  122.2 2.7 %collective-permute-start.27 = (s16[160,1920]{1,0:T(8,128)(2,1)S(1)}, s16[160,1920]{1,0:T(8,128)(2,1)S(1)}, u32[]{:S(2)}, u32[]{:S(2)}) collective-permute-start(s16[160,1920]{1,0:T(8,128)(2,1)S(1)} %get-tuple-element.97), channel_id=1, source_target_pairs={{0,48},{16,0},{32,16},{48,32},{1,49},{17,1},{33,17},{49,33},{2,50}... | collective-permute-start | bytes 1843208 | tf_op jit(solution)/shard_map/ppermute | solution.py:42
  124.8 10.4 %collective-permute-done.22.uz = s16[160,2432]{1,0:T(8,128)(2,1)S(1)} collective-permute-done((s16[160,2432]{1,0:T(8,128)(2,1)S(1)}, s16[160,2432]{1,0:T(8,128)(2,1)S(1)}, u32[]{:S(2)}, u32[]{:S(2)}) %collective-permute-start.22) | collective-permute-done | bytes 778272 | tf_op jit(solution)/shard_map/ppermute | solution.py:38
  135.3 2.3 %collective-permute-done.26.ux = s16[160,1920]{1,0:T(8,128)(2,1)S(1)} collective-permute-done((s16[160,1920]{1,0:T(8,128)(2,1)S(1)}, s16[160,1920]{1,0:T(8,128)(2,1)S(1)}, u32[]{:S(2)}, u32[]{:S(2)}) %collective-permute-start.26) | collective-permute-done | bytes 614432 | tf_op jit(solution)/shard_map/ppermute | solution.py:38
  139.2 8.7 %collective-permute-start.28 = (bf16[160,4096]{1,0:T(8,128)(2,1)S(1)}, bf16[160,4096]{1,0:T(8,128)(2,1)S(1)}, u32[]{:S(2)}, u32[]{:S(2)}) collective-permute-start(bf16[160,4096]{1,0:T(8,128)(2,1)S(1)} %finish.1), channel_id=1, source_target_pairs={{0,0},{1,64},{64,1},{65,65},{2,2},{3,66},{66,3},{67,67},{4,4},{5,6... | collective-permute-start | bytes 3932168 | tf_op jit(solution)/shard_map/ppermute | solution.py:30
  150.4 12.8 %collective-permute-done.29 = f32[1,128]{1,0:T(1,128)S(1)} collective-permute-done((f32[1,128]{1,0:T(1,128)S(1)}, f32[1,128]{1,0:T(1,128)S(1)}, u32[]{:S(2)}, u32[]{:S(2)}) %collective-permute-start.29) | collective-permute-done | bytes 544 | tf_op jit(solution)/shard_map/ppermute | solution.py:30
  (59 shorter events, 28.4 us)
Async XLA Ops:
  0.6 20.7 %collective-permute-start = (bf16[160,4096]{1,0:T(8,128)(2,1)}, bf16[160,4096]{1,0:T(8,128)(2,1)S(1)}, u32[]{:S(2)}, u32[]{:S(2)}) collective-permute-start(bf16[160,4096]{1,0:T(8,128)(2,1)} %param.3), channel_id=1, source_target_pairs={{0,0},{1,64},{64,1},{65,65},{2,2},{3,66},{66,3},{67,67},{4,4},{5,6... | collective-permute-start | bytes 3932168 | tf_op jit(solution)/shard_map/ppermute | solution.py:30
  5.2 15.8 %collective-permute-start.1 = (s32[1,160]{1,0:T(1,128)}, s32[1,160]{1,0:T(1,128)S(1)}, u32[]{:S(2)}, u32[]{:S(2)}) collective-permute-start(s32[1,160]{1,0:T(1,128)} %bitcast.5), channel_id=1, source_target_pairs={{0,0},{1,64},{64,1},{65,65},{2,2},{3,66},{66,3},{67,67},{4,4},{5,6... | collective-permute-start | bytes 1928 | tf_op jit(solution)/shard_map/ppermute | solution.py:30
  22.0 30.3 %collective-permute-start.3 = (bf16[160,4224]{1,0:T(8,128)(2,1)S(1)}, bf16[160,4224]{1,0:T(8,128)(2,1)S(1)}, u32[]{:S(2)}, u32[]{:S(2)}) collective-permute-start(bf16[160,4224]{1,0:T(8,128)(2,1)S(1)} %get-tuple-element.51.v), channel_id=1, source_target_pairs={{0,12},{4,0},{8,4},{12,8},{1,13},{5,1},{9,5},{13,9},{2,14},{6,2},{... | collective-permute-start | bytes 4055048 | tf_op jit(solution)/shard_map/ppermute | solution.py:42
  25.8 26.5 %collective-permute-start.2 = (bf16[160,4224]{1,0:T(8,128)(2,1)S(1)}, bf16[160,4224]{1,0:T(8,128)(2,1)S(1)}, u32[]{:S(2)}, u32[]{:S(2)}) collective-permute-start(bf16[160,4224]{1,0:T(8,128)(2,1)S(1)} %get-tuple-element.51.v), channel_id=1, source_target_pairs={{0,4},{4,8},{8,12},{12,0},{1,5},{5,9},{9,13},{13,1},{2,6},{6,10},{... | collective-permute-start | bytes 4055048 | tf_op jit(solution)/shard_map/ppermute | solution.py:38
  25.8 20.3 %collective-permute-start.5 = (bf16[160,4096]{1,0:T(8,128)(2,1)S(1)}, bf16[160,4096]{1,0:T(8,128)(2,1)S(1)}, u32[]{:S(2)}, u32[]{:S(2)}) collective-permute-start(bf16[160,4096]{1,0:T(8,128)(2,1)S(1)} %get-tuple-element.52.refs_0_), channel_id=1, source_target_pairs={{0,48},{16,0},{32,16},{48,32},{1,49},{17,1},{33,17},{49,33},{2,50}... | collective-permute-start | bytes 3932168 | tf_op jit(solution)/shard_map/ppermute | solution.py:42
  28.3 24.0 %collective-permute-start.4 = (bf16[160,4096]{1,0:T(8,128)(2,1)S(1)}, bf16[160,4096]{1,0:T(8,128)(2,1)S(1)}, u32[]{:S(2)}, u32[]{:S(2)}) collective-permute-start(bf16[160,4096]{1,0:T(8,128)(2,1)S(1)} %get-tuple-element.52.refs_0_), channel_id=1, source_target_pairs={{0,16},{16,32},{32,48},{48,0},{1,17},{17,33},{33,49},{49,1},{2,18}... | collective-permute-start | bytes 3932168 | tf_op jit(solution)/shard_map/ppermute | solution.py:38
  52.5 14.4 %collective-permute-start.8 = (bf16[80,4224]{1,0:T(8,128)(2,1)S(1)}, bf16[80,4224]{1,0:T(8,128)(2,1)S(1)}, u32[]{:S(2)}, u32[]{:S(2)}) collective-permute-start(bf16[80,4224]{1,0:T(8,128)(2,1)S(1)} %get-tuple-element.59), channel_id=1, source_target_pairs={{0,4},{4,8},{8,12},{12,0},{1,5},{5,9},{9,13},{13,1},{2,6},{6,10},{... | collective-permute-start | bytes 2027528 | tf_op jit(solution)/shard_map/ppermute | solution.py:38
  53.0 13.9 %collective-permute-start.9 = (bf16[80,4224]{1,0:T(8,128)(2,1)S(1)}, bf16[80,4224]{1,0:T(8,128)(2,1)S(1)}, u32[]{:S(2)}, u32[]{:S(2)}) collective-permute-start(bf16[80,4224]{1,0:T(8,128)(2,1)S(1)} %get-tuple-element.60), channel_id=1, source_target_pairs={{0,12},{4,0},{8,4},{12,8},{1,13},{5,1},{9,5},{13,9},{2,14},{6,2},{... | collective-permute-start | bytes 2027528 | tf_op jit(solution)/shard_map/ppermute | solution.py:42
  56.2 10.6 %collective-permute-start.6 = (bf16[80,4096]{1,0:T(8,128)(2,1)S(1)}, bf16[80,4096]{1,0:T(8,128)(2,1)S(1)}, u32[]{:S(2)}, u32[]{:S(2)}) collective-permute-start(bf16[80,4096]{1,0:T(8,128)(2,1)S(1)} %get-tuple-element.57), channel_id=1, source_target_pairs={{0,16},{16,32},{32,48},{48,0},{1,17},{17,33},{33,49},{49,1},{2,18}... | collective-permute-start | bytes 1966088 | tf_op jit(solution)/shard_map/ppermute | solution.py:38
  56.2 10.6 %collective-permute-start.7 = (bf16[80,4096]{1,0:T(8,128)(2,1)S(1)}, bf16[80,4096]{1,0:T(8,128)(2,1)S(1)}, u32[]{:S(2)}, u32[]{:S(2)}) collective-permute-start(bf16[80,4096]{1,0:T(8,128)(2,1)S(1)} %get-tuple-element.58), channel_id=1, source_target_pairs={{0,48},{16,0},{32,16},{48,32},{1,49},{17,1},{33,17},{49,33},{2,50}... | collective-permute-start | bytes 1966088 | tf_op jit(solution)/shard_map/ppermute | solution.py:42
  67.2 8.7 %collective-permute-start.10 = (bf16[640,4096]{1,0:T(8,128)(2,1)S(1)}, bf16[640,4096]{1,0:T(8,128)(2,1)S(1)}, u32[]{:S(2)}, u32[]{:S(2)}) collective-permute-start(bf16[640,4096]{1,0:T(8,128)(2,1)S(1)} %stack.1.b), channel_id=1, source_target_pairs={{0,1},{1,0},{2,3},{3,2},{4,5},{5,4},{6,7},{7,6},{8,9},{9,8},{10,11... | collective-permute-start | bytes 15728648 | tf_op jit(solution)/shard_map/ppermute | solution.py:34
  76.0 29.7 %collective-permute-start.19 = (bf16[640,1792]{1,0:T(8,128)(2,1)S(1)}, bf16[640,1792]{1,0:T(8,128)(2,1)S(1)}, u32[]{:S(2)}, u32[]{:S(2)}) collective-permute-start(bf16[640,1792]{1,0:T(8,128)(2,1)S(1)} %get-tuple-element.77), channel_id=1, source_target_pairs={{0,1},{1,0},{2,3},{3,2},{4,5},{5,4},{6,7},{7,6},{8,9},{9,8},{10,11... | collective-permute-start | bytes 6881288 | tf_op jit(solution)/shard_map/ppermute | solution.py:34
  83.8 5.5 %collective-permute-start.11 = (f32[8,1280]{1,0:T(8,128)S(1)}, f32[8,1280]{1,0:T(8,128)S(1)}, u32[]{:S(2)}, u32[]{:S(2)}) collective-permute-start(f32[8,1280]{1,0:T(8,128)S(1)} %get-tuple-element.70.mine), channel_id=1, source_target_pairs={{0,1},{1,0},{2,3},{3,2},{4,5},{5,4},{6,7},{7,6},{8,9},{9,8},{10,11... | collective-permute-start | bytes 122888 | tf_op jit(solution)/shard_map/ppermute | solution.py:34
  97.9 7.8 %collective-permute-start.18 = (bf16[640,640]{1,0:T(8,128)(2,1)S(1)}, bf16[640,640]{1,0:T(8,128)(2,1)S(1)}, u32[]{:S(2)}, u32[]{:S(2)}) collective-permute-start(bf16[640,640]{1,0:T(8,128)(2,1)S(1)} %get-tuple-element.75.far), channel_id=1, source_target_pairs={{0,1},{1,0},{2,3},{3,2},{4,5},{5,4},{6,7},{7,6},{8,9},{9,8},{10,11... | collective-permute-start | bytes 2457608 | tf_op jit(solution)/shard_map/ppermute | solution.py:34
  102.6 12.4 %collective-permute-start.20 = (s16[80,2432]{1,0:T(8,128)(2,1)S(1)}, s16[80,2432]{1,0:T(8,128)(2,1)S(1)}, u32[]{:S(2)}, u32[]{:S(2)}) collective-permute-start(s16[80,2432]{1,0:T(8,128)(2,1)S(1)} %get-tuple-element.81), channel_id=1, source_target_pairs={{0,4},{4,8},{8,12},{12,0},{1,5},{5,9},{9,13},{13,1},{2,6},{6,10},{... | collective-permute-start | bytes 1167368 | tf_op jit(solution)/shard_map/ppermute | solution.py:38
  103.3 11.7 %collective-permute-start.21 = (s16[80,2432]{1,0:T(8,128)(2,1)S(1)}, s16[80,2432]{1,0:T(8,128)(2,1)S(1)}, u32[]{:S(2)}, u32[]{:S(2)}) collective-permute-start(s16[80,2432]{1,0:T(8,128)(2,1)S(1)} %get-tuple-element.82), channel_id=1, source_target_pairs={{0,12},{4,0},{8,4},{12,8},{1,13},{5,1},{9,5},{13,9},{2,14},{6,2},{... | collective-permute-start | bytes 1167368 | tf_op jit(solution)/shard_map/ppermute | solution.py:42
  107.3 14.3 %collective-permute-start.24 = (s16[80,1920]{1,0:T(8,128)(2,1)S(1)}, s16[80,1920]{1,0:T(8,128)(2,1)S(1)}, u32[]{:S(2)}, u32[]{:S(2)}) collective-permute-start(s16[80,1920]{1,0:T(8,128)(2,1)S(1)} %get-tuple-element.78), channel_id=1, source_target_pairs={{0,16},{16,32},{32,48},{48,0},{1,17},{17,33},{33,49},{49,1},{2,18}... | collective-permute-start | bytes 921608 | tf_op jit(solution)/shard_map/ppermute | solution.py:38
  107.4 14.2 %collective-permute-start.25 = (s16[80,1920]{1,0:T(8,128)(2,1)S(1)}, s16[80,1920]{1,0:T(8,128)(2,1)S(1)}, u32[]{:S(2)}, u32[]{:S(2)}) collective-permute-start(s16[80,1920]{1,0:T(8,128)(2,1)S(1)} %get-tuple-element.91), channel_id=1, source_target_pairs={{0,48},{16,0},{32,16},{48,32},{1,49},{17,1},{33,17},{49,33},{2,50}... | collective-permute-start | bytes 921608 | tf_op jit(solution)/shard_map/ppermute | solution.py:42
  115.6 19.6 %collective-permute-start.22 = (s16[160,2432]{1,0:T(8,128)(2,1)S(1)}, s16[160,2432]{1,0:T(8,128)(2,1)S(1)}, u32[]{:S(2)}, u32[]{:S(2)}) collective-permute-start(s16[160,2432]{1,0:T(8,128)(2,1)S(1)} %get-tuple-element.87), channel_id=1, source_target_pairs={{0,4},{4,8},{8,12},{12,0},{1,5},{5,9},{9,13},{13,1},{2,6},{6,10},{... | collective-permute-start | bytes 2334728 | tf_op jit(solution)/shard_map/ppermute | solution.py:38
  116.4 18.9 %collective-permute-start.23 = (s16[160,2432]{1,0:T(8,128)(2,1)S(1)}, s16[160,2432]{1,0:T(8,128)(2,1)S(1)}, u32[]{:S(2)}, u32[]{:S(2)}) collective-permute-start(s16[160,2432]{1,0:T(8,128)(2,1)S(1)} %get-tuple-element.88), channel_id=1, source_target_pairs={{0,12},{4,0},{8,4},{12,8},{1,13},{5,1},{9,5},{13,9},{2,14},{6,2},{... | collective-permute-start | bytes 2334728 | tf_op jit(solution)/shard_map/ppermute | solution.py:42
  122.1 15.5 %collective-permute-start.26 = (s16[160,1920]{1,0:T(8,128)(2,1)S(1)}, s16[160,1920]{1,0:T(8,128)(2,1)S(1)}, u32[]{:S(2)}, u32[]{:S(2)}) collective-permute-start(s16[160,1920]{1,0:T(8,128)(2,1)S(1)} %get-tuple-element.96), channel_id=1, source_target_pairs={{0,16},{16,32},{32,48},{48,0},{1,17},{17,33},{33,49},{49,1},{2,18}... | collective-permute-start | bytes 1843208 | tf_op jit(solution)/shard_map/ppermute | solution.py:38
  122.2 15.4 %collective-permute-start.27 = (s16[160,1920]{1,0:T(8,128)(2,1)S(1)}, s16[160,1920]{1,0:T(8,128)(2,1)S(1)}, u32[]{:S(2)}, u32[]{:S(2)}) collective-permute-start(s16[160,1920]{1,0:T(8,128)(2,1)S(1)} %get-tuple-element.97), channel_id=1, source_target_pairs={{0,48},{16,0},{32,16},{48,32},{1,49},{17,1},{33,17},{49,33},{2,50}... | collective-permute-start | bytes 1843208 | tf_op jit(solution)/shard_map/ppermute | solution.py:42
  139.2 24.1 %collective-permute-start.28 = (bf16[160,4096]{1,0:T(8,128)(2,1)S(1)}, bf16[160,4096]{1,0:T(8,128)(2,1)S(1)}, u32[]{:S(2)}, u32[]{:S(2)}) collective-permute-start(bf16[160,4096]{1,0:T(8,128)(2,1)S(1)} %finish.1), channel_id=1, source_target_pairs={{0,0},{1,64},{64,1},{65,65},{2,2},{3,66},{66,3},{67,67},{4,4},{5,6... | collective-permute-start | bytes 3932168 | tf_op jit(solution)/shard_map/ppermute | solution.py:30
  148.0 15.3 %collective-permute-start.29 = (f32[1,128]{1,0:T(1,128)S(1)}, f32[1,128]{1,0:T(1,128)S(1)}, u32[]{:S(2)}, u32[]{:S(2)}) collective-permute-start(f32[1,128]{1,0:T(1,128)S(1)} %get-tuple-element.99), channel_id=1, source_target_pairs={{0,0},{1,64},{64,1},{65,65},{2,2},{3,66},{66,3},{67,67},{4,4},{5,6... | collective-permute-start | bytes 1544 | tf_op jit(solution)/shard_map/ppermute | solution.py:30
  (7 other events, 25.3 us)

commit v5 on v4

--- a/solution.py
+++ b/solution.py
@@ -114,7 +114,54 @@
     v[:, e.shape[1] :] = digits[...]
 
 
-def early_kernel(v, zd, zu, za, zb, b, a, last, mates, s):
+def statistics(s, ids, mates, multiplier, own, rstat, cstat):
+    tall, wide = s.shape
+
+    def first(i, carry):
+        top, pos = carry
+        r = pl.ds(pl.multiple_of(i * LANES, LANES), LANES)
+        v = s[r, :] * multiplier
+        pos += jnp.sum(jnp.where(ids == mates[r, 0:1], v, F32(0.0)), axis=0, keepdims=True)
+        if own:
+            row_ids = i * LANES + lax.broadcasted_iota(jnp.int32, (LANES, wide), 0)
+            col_ids = lax.broadcasted_iota(jnp.int32, (LANES, wide), 1)
+            v = jnp.where((row_ids == col_ids) & (row_ids < tall // 4), F32(-1e30), v)
+        s[r, :] = v
+        m = jnp.max(v, axis=1, keepdims=True)
+        l = jnp.sum(jnp.exp(v - m), axis=1, keepdims=True)
+        rstat[0:1, r] = jnp.transpose(jnp.broadcast_to(m, (LANES, LANES)))[0:1, :]
+        rstat[1:2, r] = jnp.transpose(jnp.broadcast_to(l, (LANES, LANES)))[0:1, :]
+        return jnp.maximum(top, jnp.max(v, axis=0, keepdims=True)), pos
+
+    start = jnp.full((1, wide), -1e30, F32), jnp.zeros((1, wide), F32)
+    top, pos = lax.fori_loop(0, tall // LANES, first, start)
+
+    def second(i, low):
+        r = pl.ds(pl.multiple_of(i * LANES, LANES), LANES)
+        return low + jnp.sum(jnp.exp(s[r, :] - top), axis=0, keepdims=True)
+
+    cstat[0:1, :] = top
+    cstat[1:2, :] = lax.fori_loop(0, tall // LANES, second, jnp.zeros((1, wide), F32))
+    cstat[2:3, :] = pos
+
+
+def near_kernel(v, zd, zu, b, bo, s1, s2, a):
+    at = 0
+    for r in (v, zd, zu):
+        a[at : at + r.shape[0], :] = r[:, : a.shape[1]]
+        at += r.shape[0]
+    s1[...] = dot(a[...], b[...], NT)
+    s2[...] = dot(a[...], bo[...], NT)
+
+
+def complete(s, known, a, b, t):
+    n = known.shape[0]
+    s[0:n, 0:n] = known[...]
+    s[n:, 0:n] = dot(a[n:, :], b[...], NT)
+    s[:, n:] = dot(a[...], t[...], NT)
+
+
+def early_kernel(mult, v, zd, zu, za, zb, b, t, known, cols, a, last, mates, s, rstat, cstat):
     width, w = a.shape[1], last.shape[1]
     at = 0
     for r in (v, zd, zu, za, zb):
@@ -124,49 +171,28 @@
         two = r[:, width:].astype(F32)
         mates[at : at + n, :] = jnp.broadcast_to(two[:, 0:1] * F32(64.0) + two[:, 1:2], (n, LANES))
         at += n
-    s[...] = dot(a[...], b[...], NT)
+    complete(s, known, a, b, t)
+    rstat[...] = jnp.zeros(rstat.shape, F32)
+    cstat[...] = jnp.zeros(cstat.shape, F32)
+    statistics(s, cols[:, : s.shape[1]], mates, mult[0], True, rstat, cstat)
 
 
 def column(row, n):
     return jnp.transpose(jnp.broadcast_to(row, (LANES, n)))[:, :1]
 
 
-def tail_kernel(mult, a, b, early, mates, cols, s, rstat, cstat):
-    side, rows = early.shape[0], early.shape[0] // 4
-    s[:, 0:side] = early[...]
-    s[:, side:] = dot(a[...], b[...], NT)
-    multiplier = mult[0]
-    tall, wide = s.shape
-    rstat[...] = jnp.zeros(rstat.shape, F32)
-    ids = cols[...]
-
-    def first(i, carry):
-        top, pos = carry
-        r = pl.ds(pl.multiple_of(i * LANES, LANES), LANES)
-        v = s[r, :] * multiplier
-        pos += jnp.sum(jnp.where(ids == mates[r, 0:1], v, F32(0.0)), axis=0, keepdims=True)
-        row_ids = i * LANES + lax.broadcasted_iota(jnp.int32, (LANES, wide), 0)
-        col_ids = lax.broadcasted_iota(jnp.int32, (LANES, wide), 1)
-        v = jnp.where((row_ids == col_ids) & (row_ids < rows), F32(-1e30), v)
-        s[r, :] = v
-        m = jnp.max(v, axis=1, keepdims=True)
-        l = jnp.sum(jnp.exp(v - m), axis=1, keepdims=True)
-        rstat[0:1, r] = jnp.transpose(jnp.broadcast_to(m, (LANES, LANES)))[0:1, :]
-        rstat[1:2, r] = jnp.transpose(jnp.broadcast_to(l, (LANES, LANES)))[0:1, :]
-        return jnp.maximum(top, jnp.max(v, axis=0, keepdims=True)), pos
-
-    start = jnp.full((1, wide), -1e30, F32), jnp.zeros((1, wide), F32)
-    top, pos = lax.fori_loop(0, tall // LANES, first, start)
-    rstat[2:3, :] = jnp.full((1, tall), jnp.sum(pos), F32)
-
-    def second(i, low):
-        r = pl.ds(pl.multiple_of(i * LANES, LANES), LANES)
-        return low + jnp.sum(jnp.exp(s[r, :] - top), axis=0, keepdims=True)
-
-    low = lax.fori_loop(0, tall // LANES, second, jnp.zeros((1, wide), F32))
-    cstat[...] = jnp.zeros(cstat.shape, F32)
-    cstat[0:1, :] = top
-    cstat[1:2, :] = low
+def tail_kernel(mult, a, b, t, known, mates, cols, rs1, cs1, s, rstat, cstat, rs2, cs2):
+    side = s.shape[1]
+    complete(s, known, a, b, t)
+    statistics(s, cols[:, side:], mates, mult[0], False, rs2, cs2)
+    m1, m2 = rs1[0:1, :], rs2[0:1, :]
+    m = jnp.maximum(m1, m2)
+    positive = jnp.sum(cs1[2:3, :] + cs2[2:3, :], axis=1, keepdims=True)
+    rstat[...] = jnp.broadcast_to(positive, rstat.shape)
+    rstat[0:1, :] = m
+    rstat[1:2, :] = rs1[1:2, :] * jnp.exp(m1 - m) + rs2[1:2, :] * jnp.exp(m2 - m)
+    cstat[:, 0:side] = cs1[...]
+    cstat[:, side:] = cs2[...]
 
 
 def merge_kernel(mine, other, r0, r1, r2, r3, out, lse_r):
@@ -195,21 +221,20 @@
     return top + jnp.log(low)
 
 
-def weights_kernel(s, mates, lse_r, c0, c1, c2, c3, cols, near, far, part):
-    tall, wide = s.shape
-    side = wide // 2
+def weights_kernel(s1, s2, mates, lse_r, c0, c1, c2, c3, cols, near, far, part):
+    tall, side = s1.shape
     lse_c = combine((c0, c1, c2, c3), tall // 4)
     ids = cols[...]
 
     @pl.loop(0, tall // LANES)
     def _(i):
         r = pl.ds(pl.multiple_of(i * LANES, LANES), LANES)
-        v = s[r, :]
-        hit = ids == mates[r, 0:1]
-        w = jnp.exp(v - column(lse_r[0:1, r], LANES)) + jnp.exp(v - lse_c)
-        w = (w - jnp.where(hit, F32(2.0), F32(0.0))).astype(BF16)
-        near[r, :] = w[:, :side]
-        far[r, :] = w[:, side:]
+        mate, lse = mates[r, 0:1], column(lse_r[0:1, r], LANES)
+        for s, out, at in ((s1, near, 0), (s2, far, side)):
+            v = s[r, :]
+            w = jnp.exp(v - lse) + jnp.exp(v - lse_c[:, at : at + side])
+            hit = ids[:, at : at + side] == mate
+            out[r, :] = (w - jnp.where(hit, F32(2.0), F32(0.0))).astype(BF16)
 
     part[...] = c0[2:3, 0:LANES] + c1[2:3, 0:LANES] + c2[2:3, 0:LANES] + c3[2:3, 0:LANES]
 
@@ -240,17 +265,27 @@
     own[...] = acc[0:rows, :]
 
 
-def z_first_kernel(near, far, b, o, fwd, bwd, acc):
+def z_terms(near, far, r, w, b, t, bo, to):
+    n = b.shape[0]
+    return (
+        dot(near[r, 0:n], b[:, :w], NN)
+        + dot(near[r, n:], t[:, :w], NN)
+        + dot(far[r, 0:n], bo[:, :w], NN)
+        + dot(far[r, n:], to[:, :w], NN)
+    )
+
+
+def z_first_kernel(near, far, b, t, bo, to, fwd, bwd, acc):
     n, w = acc.shape
     r = slice(near.shape[0] - n, None)
-    acc[...] = dot(near[r, :], b[:, :w], NN) + dot(far[r, :], o[:, :w], NN)
+    acc[...] = z_terms(near, far, r, w, b, t, bo, to)
     pack(fwd, 0, acc[0 : n // 2, :])
     pack(bwd, 0, acc[n // 2 :, :])
 
 
-def z_kernel(near, far, b, o, late_fwd, late_bwd, keep1, keep3, own, acc):
+def z_kernel(near, far, b, t, bo, to, late_fwd, late_bwd, keep1, keep3, own, acc):
     n, w = acc.shape
-    acc[...] = dot(near[0:n, :], b[:, :w], NN) + dot(far[0:n, :], o[:, :w], NN)
+    acc[...] = z_terms(near, far, slice(0, n), w, b, t, bo, to)
     hand_out(acc, late_fwd, late_bwd, keep1, keep3, own)
 
 
@@ -312,32 +347,40 @@
     xa, xb, za, zb = call(
         halves_kernel, "halves", (xu, xd, zu, zd), (half_x, half_x, half_z, half_z)
     )
-    xa, xb, za, zb = lax.optimization_barrier(
-        (up(xa, "x"), down(xb, "x"), up(za, "z"), down(zb, "z"))
-    )
-    b = stack("stack", u, xd, xu, xa, xb)
+    b = stack("stack_b", u, xd, xu)
     bo = other_core(b)
+    n = b.shape[0]
+    known1, known2 = call(
+        near_kernel, "near", (v, zd, zu, b, bo), (shape(n, n), shape(n, n)),
+        scratch=[pltpu.VMEM((n, width), BF16)], flops=4 * n * n * width,
+    )
+    xa, xb, za, zb, known1, known2 = lax.optimization_barrier(
+        (up(xa, "x"), down(xb, "x"), up(za, "z"), down(zb, "z"), known1, known2)
+    )
+    t = stack("stack_t", xa, xb)
+    to = other_core(t)
     along = {"z": width * 9 // 16, "x": width * 7 // 16}
     flops = 2 * side * side * width
-    a, last, mates, early = call(
-        early_kernel, "early", (v, zd, zu, za, zb, b),
+    a, last, mates, near, rstat, cstat = call(
+        early_kernel, "early", (logit_scale, v, zd, zu, za, zb, b, t, known1, cols),
         (
             shape(side, width, dtype=BF16), shape(side, along["x"], dtype=BF16),
-            shape(side, LANES), shape(side, side),
+            shape(side, LANES), shape(side, side), shape(8, side), shape(8, side),
         ),
         flops=flops,
     )
-    last_other = other_core(after(last, bo))
-    scores, rstat, cstat = call(
-        tail_kernel, "tail", (logit_scale, a, bo, early, mates, cols),
-        (shape(side, 2 * side), shape(8, side), shape(8, 2 * side)), flops=flops,
+    last_other = other_core(after(last, to))
+    far, rstat, cstat = call(
+        tail_kernel, "tail", (logit_scale, a, bo, to, known2, mates, cols, rstat, cstat),
+        (shape(side, side), shape(8, side), shape(8, 2 * side)),
+        scratch=[pltpu.VMEM((8, side), F32), pltpu.VMEM((8, side), F32)], flops=flops,
     )
     cstat_other = other_core(cstat)
     rstats = gather_small(rstat, "z")
     merged, lse_r = call(merge_kernel, "merge", (cstat, cstat_other, *rstats), (cstat, rstat))
     cstats = gather_small(merged, "x")
     near, far, part = call(
-        weights_kernel, "weights", (scores, mates, lse_r, *cstats, cols),
+        weights_kernel, "weights", (near, far, mates, lse_r, *cstats, cols),
         (shape(side, side, dtype=BF16), shape(side, side, dtype=BF16), shape(1, LANES)),
     )
     far_other = other_core(far)
@@ -356,12 +399,12 @@
         )
         return first(*operands), rest
 
-    operands_z, operands_x = (near, far, b, bo), (near, far_other, a, last_other)
+    operands_z, operands_x = (near, far, b, t, bo, to), (near, far_other, a, last_other)
     (fz, bz), rest_z = terms((z_first_kernel, z_kernel), "z", operands_z)
     (fx, bx), rest_x = terms((x_first_kernel, x_kernel), "x", operands_x)
     *kept_z, oz = rest_z(after(near, fx), *operands_z[1:])
     *kept_x, ox = rest_x(after(near, oz), *operands_x[1:])
-    fz, bz = up(fz, "z"), down(bz, "z")
+    fz, bz, _ = lax.optimization_barrier((up(fz, "z"), down(bz, "z"), ox))
     fx, bx = up(fx, "x"), down(bx, "x")
     message = {i: shape(rows, w + LANES, dtype=I16) for i, w in along.items()}
     uz, dz = call(forward_kernel, "forward_z", (fz, bz, *kept_z), (message["z"],) * 2)

time: 166 us -> 157 us (0.946)
  waiting for transfers between devices: 80.9 us -> 71.7 us
  Pallas kernels: 27.9 us -> 30.1 us
    ppermute x8, waiting for transfers between devices: 17.9 us -> 0.02 us  [down(): return lax.ppermute(v, axis, ring(4, -1))]
    ppermute x8, waiting for transfers between devices: 27.9 us -> 36.3 us  [up(): return lax.ppermute(v, axis, ring(4, 1))]
    ppermute x8, starting transfers between devices: 22 us -> 17.6 us  [down(): return lax.ppermute(v, axis, ring(4, -1))]
    ppermute x8, starting transfers between devices: 2.05 us -> 5.92 us  [up(): return lax.ppermute(v, axis, ring(4, 1))]
    ppermute x6, waiting for transfers between devices: 3.8 us -> 7.09 us  [gather_small(): return [v] + [lax.ppermute(v, axis, ring(4, -k)) for k in ORDER[1:]]]
    ppermute x4 -> x5, waiting for transfers between devices: 4.22 us -> 1.17 us  [other_core(): return lax.ppermute(v, 'c', ring(2, 1))]
    ppermute x4 -> x5, starting transfers between devices: 3.66 us -> 6.2 us  [other_core(): return lax.ppermute(v, 'c', ring(2, 1))]
    pallas_call x14 -> x16, Pallas kernels: 27.9 us -> 30.1 us  [call(): pl.pallas_call(kernel, name=name, out_shape=tuple((jax.ShapeDtypeStruct(o...]
  transfers between devices with their start and end apart: 31 -> 32, of which waited for: 15 -> 10; matrix products, arithmetic and copies ran while one was open for 0% -> 0% of each run, Pallas kernels for 15% -> 18%
where the time goes in v5:
time: 157 us
  waiting for transfers between devices  71.7 us (46%)
  starting transfers between devices  51 us (32%)
  Pallas kernels  30.1 us (19%)
  between operations  2.74 us (2%)
    ppermute x8, waiting for transfers between devices, up(): return lax.ppermute(v, axis, ring(4, 1))  36.3 us
    pallas_call x16, Pallas kernels, call(): pl.pallas_call(kernel, name=name, out_shape=tuple((jax.ShapeDtypeStruct(o...  30.1 us
    ppermute x4, waiting for transfers between devices, swap(): return lax.ppermute(v, ('yl', 'c'), SWAP)  27.1 us
    ppermute x8, starting transfers between devices, down(): return lax.ppermute(v, axis, ring(4, -1))  17.6 us
    ppermute x4, starting transfers between devices, swap(): return lax.ppermute(v, ('yl', 'c'), SWAP)  15.4 us
    ppermute x6, waiting for transfers between devices, gather_small(): return [v] + [lax.ppermute(v, axis, ring(4, -k)) for k in ORDER[1:]]  7.09 us
    ppermute x5, starting transfers between devices, other_core(): return lax.ppermute(v, 'c', ring(2, 1))  6.2 us
    ppermute x8, starting transfers between devices, up(): return lax.ppermute(v, axis, ring(4, 1))  5.92 us
  transfers between devices with their start and end apart: 32, of which 10 were waited for; matrix products, arithmetic and copies ran while one was open for 0% of the time, Pallas kernels for 18%

profile of v5, /device:TPU:1, one launch (start us, length us, event | category | flops | bytes accessed | tf_op | source)
XLA Modules:
  0.0 157.0 jit_solution(10427359767126711582)
XLA Ops:
  0.6 4.6 %collective-permute-start = (bf16[160,4096]{1,0:T(8,128)(2,1)}, bf16[160,4096]{1,0:T(8,128)(2,1)S(1)}, u32[]{:S(2)}, u32[]{:S(2)}) collective-permute-start(bf16[160,4096]{1,0:T(8,128)(2,1)} %param.3), channel_id=1, source_target_pairs={{0,0},{1,64},{64,1},{65,65},{2,2},{3,66},{66,3},{67,67},{4,4},{5,6... | collective-permute-start | bytes 3932168 | tf_op jit(solution)/shard_map/ppermute | solution.py:30
  5.2 1.9 %collective-permute-start.1 = (s32[1,160]{1,0:T(1,128)}, s32[1,160]{1,0:T(1,128)S(1)}, u32[]{:S(2)}, u32[]{:S(2)}) collective-permute-start(s32[1,160]{1,0:T(1,128)} %bitcast.5), channel_id=1, source_target_pairs={{0,0},{1,64},{64,1},{65,65},{2,2},{3,66},{66,3},{67,67},{4,4},{5,6... | collective-permute-start | bytes 1928 | tf_op jit(solution)/shard_map/ppermute | solution.py:30
  7.2 13.8 %collective-permute-done.1 = s32[1,160]{1,0:T(1,128)S(1)} collective-permute-done((s32[1,160]{1,0:T(1,128)}, s32[1,160]{1,0:T(1,128)S(1)}, u32[]{:S(2)}, u32[]{:S(2)}) %collective-permute-start.1) | collective-permute-done | bytes 672 | tf_op jit(solution)/shard_map/ppermute | solution.py:30
  23.7 2.2 %collective-permute-start.3 = (bf16[160,4224]{1,0:T(8,128)(2,1)S(1)}, bf16[160,4224]{1,0:T(8,128)(2,1)S(1)}, u32[]{:S(2)}, u32[]{:S(2)}) collective-permute-start(bf16[160,4224]{1,0:T(8,128)(2,1)S(1)} %get-tuple-element.59.v), channel_id=1, source_target_pairs={{0,12},{4,0},{8,4},{12,8},{1,13},{5,1},{9,5},{13,9},{2,14},{6,2},{... | collective-permute-start | bytes 4055048 | tf_op jit(solution)/shard_map/ppermute | solution.py:42
  28.5 15.0 %collective-permute-done.4.xu.refs_2_ = bf16[160,4096]{1,0:T(8,128)(2,1)S(1)} collective-permute-done((bf16[160,4096]{1,0:T(8,128)(2,1)S(1)}, bf16[160,4096]{1,0:T(8,128)(2,1)S(1)}, u32[]{:S(2)}, u32[]{:S(2)}) %collective-permute-start.4) | collective-permute-done | bytes 1310752 | tf_op jit(solution)/shard_map/ppermute | solution.py:38
  44.2 2.7 %collective-permute-start.9 = (bf16[80,4224]{1,0:T(8,128)(2,1)S(1)}, bf16[80,4224]{1,0:T(8,128)(2,1)S(1)}, u32[]{:S(2)}, u32[]{:S(2)}) collective-permute-start(bf16[80,4224]{1,0:T(8,128)(2,1)S(1)} %get-tuple-element.68), channel_id=1, source_target_pairs={{0,12},{4,0},{8,4},{12,8},{1,13},{5,1},{9,5},{13,9},{2,14},{6,2},{... | collective-permute-start | bytes 2027528 | tf_op jit(solution)/shard_map/ppermute | solution.py:42
  50.7 4.3 %near.1 = (f32[480,480]{1,0:T(8,128)S(1)}, f32[480,480]{1,0:T(8,128)S(1)}) custom-call(bf16[160,4224]{1,0:T(8,128)(2,1)S(1)} %get-tuple-element.59.v, bf16[160,4224]{1,0:T(8,128)(2,1)S(1)} %collective-permute-done.3.zd, bf16[160,4224]{1,0:T(8,128)(2,1)S(1)} %collective-permute-done.2.zu, bf16[480,4096]{1,0:T(8,128)(2,1)S(1)} %stack_b.1.b, ...), custom_call_target="tpu_custom_call" | custom-call | flops 3774873600 | bytes 13762560 | tf_op jit(solution)/shard_map/near/pallas_call | solution.py:65
  54.9 8.3 %collective-permute-done.6.refs_0_ = bf16[80,4096]{1,0:T(8,128)(2,1)S(1)} collective-permute-done((bf16[80,4096]{1,0:T(8,128)(2,1)S(1)}, bf16[80,4096]{1,0:T(8,128)(2,1)S(1)}, u32[]{:S(2)}, u32[]{:S(2)}) %collective-permute-start.6) | collective-permute-done | bytes 655392 | tf_op jit(solution)/shard_map/ppermute | solution.py:38
  63.3 2.1 %collective-permute-start.11 = (bf16[160,4096]{1,0:T(8,128)(2,1)S(1)}, bf16[160,4096]{1,0:T(8,128)(2,1)S(1)}, u32[]{:S(2)}, u32[]{:S(2)}) collective-permute-start(bf16[160,4096]{1,0:T(8,128)(2,1)S(1)} %stack_t.1.t), channel_id=1, source_target_pairs={{0,1},{1,0},{2,3},{3,2},{4,5},{5,4},{6,7},{7,6},{8,9},{9,8},{10,11... | collective-permute-start | bytes 3932168 | tf_op jit(solution)/shard_map/ppermute | solution.py:34
  66.0 4.8 %early.1 = (bf16[640,4096]{1,0:T(8,128)(2,1)S(1)}, bf16[640,1792]{1,0:T(8,128)(2,1)S(1)}, f32[640,128]{1,0:T(8,128)S(1)}, f32[640,640]{1,0:T(8,128)S(1)}, f32[8,640]{1,0:T(8,128)S(1)}, /*index=5*/f32[8,640]{1,0:T(8,128)S(1)}) custom-call(f32[1]{0:T(128)S(6)} %copy.10.mult, bf16[160,4224]{1,0:T(8,128)(2,1)S(1)} %get-tuple-element.59.v, ...), custom_call_target="tpu_custom_call" | custom-call | flops 3355443200 | bytes 21120004 | tf_op jit(solution)/shard_map/early/pallas_call | solution.py:65
  71.2 4.6 %tail.1 = (f32[640,640]{1,0:T(8,128)S(1)}, f32[8,640]{1,0:T(8,128)S(1)}, f32[8,1280]{1,0:T(8,128)S(1)}) custom-call(f32[1]{0:T(128)S(6)} %copy.10.mult, bf16[640,4096]{1,0:T(8,128)(2,1)S(1)} %get-tuple-element.78.a, bf16[480,4096]{1,0:T(8,128)(2,1)S(1)} %collective-permute-done.10.bo.b, bf16[160,4096]{1,0:T(8,128)(2,1)S(1)} %collective-permute-done.11.t.to, ...), custom_call_target="tpu_custom_call" | custom-call | flops 3355443200 | bytes 13480964 | tf_op jit(solution)/shard_map/tail/pallas_call | solution.py:65
  82.2 2.7 %collective-permute-start.16 = (f32[8,1280]{1,0:T(8,128)S(1)}, f32[8,1280]{1,0:T(8,128)S(1)}, u32[]{:S(2)}, u32[]{:S(2)}) collective-permute-start(f32[8,1280]{1,0:T(8,128)S(1)} %get-tuple-element.87.c0), channel_id=1, source_target_pairs={{0,48},{16,0},{32,16},{48,32},{1,49},{17,1},{33,17},{49,33},{2,50}... | collective-permute-start | bytes 122888 | tf_op jit(solution)/shard_map/ppermute | solution.py:50
  86.3 3.1 %collective-permute-done.17.c2 = f32[8,1280]{1,0:T(8,128)S(1)} collective-permute-done((f32[8,1280]{1,0:T(8,128)S(1)}, f32[8,1280]{1,0:T(8,128)S(1)}, u32[]{:S(2)}, u32[]{:S(2)}) %collective-permute-start.17) | collective-permute-done | bytes 40992 | tf_op jit(solution)/shard_map/ppermute | solution.py:50
  91.2 3.3 %collective-permute-start.19 = (bf16[640,640]{1,0:T(8,128)(2,1)S(1)}, bf16[640,640]{1,0:T(8,128)(2,1)S(1)}, u32[]{:S(2)}, u32[]{:S(2)}) collective-permute-start(bf16[640,640]{1,0:T(8,128)(2,1)S(1)} %get-tuple-element.89.far), channel_id=1, source_target_pairs={{0,1},{1,0},{2,3},{3,2},{4,5},{5,4},{6,7},{7,6},{8,9},{9,8},{10,11... | collective-permute-start | bytes 2457608 | tf_op jit(solution)/shard_map/ppermute | solution.py:34
  96.3 2.7 %collective-permute-start.22 = (s16[80,2432]{1,0:T(8,128)(2,1)S(1)}, s16[80,2432]{1,0:T(8,128)(2,1)S(1)}, u32[]{:S(2)}, u32[]{:S(2)}) collective-permute-start(s16[80,2432]{1,0:T(8,128)(2,1)S(1)} %get-tuple-element.96), channel_id=1, source_target_pairs={{0,12},{4,0},{8,4},{12,8},{1,13},{5,1},{9,5},{13,9},{2,14},{6,2},{... | collective-permute-start | bytes 1167368 | tf_op jit(solution)/shard_map/ppermute | solution.py:42
  101.0 4.1 %rest_z.1 = (s16[80,2432]{1,0:T(8,128)(2,1)S(1)}, s16[80,2432]{1,0:T(8,128)(2,1)S(1)}, f32[80,2304]{1,0:T(8,128)S(1)}, f32[80,2304]{1,0:T(8,128)S(1)}, f32[160,2304]{1,0:T(8,128)S(1)}) custom-call(bf16[640,640]{1,0:T(8,128)(2,1)S(1)} %get-tuple-element.97.near, bf16[640,640]{1,0:T(8,128)(2,1)S(1)} %get-tuple-element.89.far, bf16[480,4096]{1,0:T(8,128)(2,1)S(1)} %stack_b.1.b, ...), custom_call_target="tpu_custom_call" | custom-call | flops 2831155200 | bytes 15851520 | tf_op jit(solution)/shard_map/rest_z/pallas_call | solution.py:65
  105.0 2.8 %collective-permute-start.26 = (s16[80,1920]{1,0:T(8,128)(2,1)S(1)}, s16[80,1920]{1,0:T(8,128)(2,1)S(1)}, u32[]{:S(2)}, u32[]{:S(2)}) collective-permute-start(s16[80,1920]{1,0:T(8,128)(2,1)S(1)} %get-tuple-element.107), channel_id=1, source_target_pairs={{0,48},{16,0},{32,16},{48,32},{1,49},{17,1},{33,17},{49,33},{2,50}... | collective-permute-start | bytes 921608 | tf_op jit(solution)/shard_map/ppermute | solution.py:42
  107.8 3.2 %rest_x.1 = (s16[80,1920]{1,0:T(8,128)(2,1)S(1)}, s16[80,1920]{1,0:T(8,128)(2,1)S(1)}, f32[80,1792]{1,0:T(8,128)S(1)}, f32[80,1792]{1,0:T(8,128)S(1)}, f32[160,1792]{1,0:T(8,128)S(1)}) custom-call(bf16[640,640]{1,0:T(8,128)(2,1)S(1)} %get-tuple-element.97.near, bf16[640,640]{1,0:T(8,128)(2,1)S(1)} %collective-permute-done.19.far, ...), custom_call_target="tpu_custom_call" | custom-call | flops 2202009600 | bytes 12083200 | tf_op jit(solution)/shard_map/rest_x/pallas_call | solution.py:65
  111.7 2.7 %collective-permute-start.24 = (s16[160,2432]{1,0:T(8,128)(2,1)S(1)}, s16[160,2432]{1,0:T(8,128)(2,1)S(1)}, u32[]{:S(2)}, u32[]{:S(2)}) collective-permute-start(s16[160,2432]{1,0:T(8,128)(2,1)S(1)} %get-tuple-element.106), channel_id=1, source_target_pairs={{0,12},{4,0},{8,4},{12,8},{1,13},{5,1},{9,5},{13,9},{2,14},{6,2},{... | collective-permute-start | bytes 2334728 | tf_op jit(solution)/shard_map/ppermute | solution.py:42
  116.0 1.8 %collective-permute-start.28 = (s16[160,1920]{1,0:T(8,128)(2,1)S(1)}, s16[160,1920]{1,0:T(8,128)(2,1)S(1)}, u32[]{:S(2)}, u32[]{:S(2)}) collective-permute-start(s16[160,1920]{1,0:T(8,128)(2,1)S(1)} %get-tuple-element.113), channel_id=1, source_target_pairs={{0,48},{16,0},{32,16},{48,32},{1,49},{17,1},{33,17},{49,33},{2,50}... | collective-permute-start | bytes 1843208 | tf_op jit(solution)/shard_map/ppermute | solution.py:42
  117.8 13.0 %collective-permute-done.23.uz = s16[160,2432]{1,0:T(8,128)(2,1)S(1)} collective-permute-done((s16[160,2432]{1,0:T(8,128)(2,1)S(1)}, s16[160,2432]{1,0:T(8,128)(2,1)S(1)}, u32[]{:S(2)}, u32[]{:S(2)}) %collective-permute-start.23) | collective-permute-done | bytes 778272 | tf_op jit(solution)/shard_map/ppermute | solution.py:38
  132.4 7.0 %collective-permute-start.29 = (bf16[160,4096]{1,0:T(8,128)(2,1)S(1)}, bf16[160,4096]{1,0:T(8,128)(2,1)S(1)}, u32[]{:S(2)}, u32[]{:S(2)}) collective-permute-start(bf16[160,4096]{1,0:T(8,128)(2,1)S(1)} %finish.1), channel_id=1, source_target_pairs={{0,0},{1,64},{64,1},{65,65},{2,2},{3,66},{66,3},{67,67},{4,4},{5,6... | collective-permute-start | bytes 3932168 | tf_op jit(solution)/shard_map/ppermute | solution.py:30
  139.4 1.9 %collective-permute-start.30 = (f32[1,128]{1,0:T(1,128)S(1)}, f32[1,128]{1,0:T(1,128)S(1)}, u32[]{:S(2)}, u32[]{:S(2)}) collective-permute-start(f32[1,128]{1,0:T(1,128)S(1)} %get-tuple-element.115), channel_id=1, source_target_pairs={{0,0},{1,64},{64,1},{65,65},{2,2},{3,66},{66,3},{67,67},{4,4},{5,6... | collective-permute-start | bytes 1544 | tf_op jit(solution)/shard_map/ppermute | solution.py:30
  141.4 13.3 %collective-permute-done.30 = f32[1,128]{1,0:T(1,128)S(1)} collective-permute-done((f32[1,128]{1,0:T(1,128)S(1)}, f32[1,128]{1,0:T(1,128)S(1)}, u32[]{:S(2)}, u32[]{:S(2)}) %collective-permute-start.30) | collective-permute-done | bytes 544 | tf_op jit(solution)/shard_map/ppermute | solution.py:30
  (63 shorter events, 28.7 us)
Async XLA Ops:
  0.6 20.7 %collective-permute-start = (bf16[160,4096]{1,0:T(8,128)(2,1)}, bf16[160,4096]{1,0:T(8,128)(2,1)S(1)}, u32[]{:S(2)}, u32[]{:S(2)}) collective-permute-start(bf16[160,4096]{1,0:T(8,128)(2,1)} %param.3), channel_id=1, source_target_pairs={{0,0},{1,64},{64,1},{65,65},{2,2},{3,66},{66,3},{67,67},{4,4},{5,6... | collective-permute-start | bytes 3932168 | tf_op jit(solution)/shard_map/ppermute | solution.py:30
  5.2 15.8 %collective-permute-start.1 = (s32[1,160]{1,0:T(1,128)}, s32[1,160]{1,0:T(1,128)S(1)}, u32[]{:S(2)}, u32[]{:S(2)}) collective-permute-start(s32[1,160]{1,0:T(1,128)} %bitcast.5), channel_id=1, source_target_pairs={{0,0},{1,64},{64,1},{65,65},{2,2},{3,66},{66,3},{67,67},{4,4},{5,6... | collective-permute-start | bytes 1928 | tf_op jit(solution)/shard_map/ppermute | solution.py:30
  22.0 21.6 %collective-permute-start.2 = (bf16[160,4224]{1,0:T(8,128)(2,1)S(1)}, bf16[160,4224]{1,0:T(8,128)(2,1)S(1)}, u32[]{:S(2)}, u32[]{:S(2)}) collective-permute-start(bf16[160,4224]{1,0:T(8,128)(2,1)S(1)} %get-tuple-element.59.v), channel_id=1, source_target_pairs={{0,4},{4,8},{8,12},{12,0},{1,5},{5,9},{9,13},{13,1},{2,6},{6,10},{... | collective-permute-start | bytes 4055048 | tf_op jit(solution)/shard_map/ppermute | solution.py:38
  23.7 19.9 %collective-permute-start.3 = (bf16[160,4224]{1,0:T(8,128)(2,1)S(1)}, bf16[160,4224]{1,0:T(8,128)(2,1)S(1)}, u32[]{:S(2)}, u32[]{:S(2)}) collective-permute-start(bf16[160,4224]{1,0:T(8,128)(2,1)S(1)} %get-tuple-element.59.v), channel_id=1, source_target_pairs={{0,12},{4,0},{8,4},{12,8},{1,13},{5,1},{9,5},{13,9},{2,14},{6,2},{... | collective-permute-start | bytes 4055048 | tf_op jit(solution)/shard_map/ppermute | solution.py:42
  25.9 17.7 %collective-permute-start.4 = (bf16[160,4096]{1,0:T(8,128)(2,1)S(1)}, bf16[160,4096]{1,0:T(8,128)(2,1)S(1)}, u32[]{:S(2)}, u32[]{:S(2)}) collective-permute-start(bf16[160,4096]{1,0:T(8,128)(2,1)S(1)} %get-tuple-element.60.refs_0_), channel_id=1, source_target_pairs={{0,16},{16,32},{32,48},{48,0},{1,17},{17,33},{33,49},{49,1},{2,18}... | collective-permute-start | bytes 3932168 | tf_op jit(solution)/shard_map/ppermute | solution.py:38
  27.1 16.5 %collective-permute-start.5 = (bf16[160,4096]{1,0:T(8,128)(2,1)S(1)}, bf16[160,4096]{1,0:T(8,128)(2,1)S(1)}, u32[]{:S(2)}, u32[]{:S(2)}) collective-permute-start(bf16[160,4096]{1,0:T(8,128)(2,1)S(1)} %get-tuple-element.60.refs_0_), channel_id=1, source_target_pairs={{0,48},{16,0},{32,16},{48,32},{1,49},{17,1},{33,17},{49,33},{2,50}... | collective-permute-start | bytes 3932168 | tf_op jit(solution)/shard_map/ppermute | solution.py:42
  44.1 19.1 %collective-permute-start.8 = (bf16[80,4224]{1,0:T(8,128)(2,1)S(1)}, bf16[80,4224]{1,0:T(8,128)(2,1)S(1)}, u32[]{:S(2)}, u32[]{:S(2)}) collective-permute-start(bf16[80,4224]{1,0:T(8,128)(2,1)S(1)} %get-tuple-element.67), channel_id=1, source_target_pairs={{0,4},{4,8},{8,12},{12,0},{1,5},{5,9},{9,13},{13,1},{2,6},{6,10},{... | collective-permute-start | bytes 2027528 | tf_op jit(solution)/shard_map/ppermute | solution.py:38
  44.2 19.1 %collective-permute-start.9 = (bf16[80,4224]{1,0:T(8,128)(2,1)S(1)}, bf16[80,4224]{1,0:T(8,128)(2,1)S(1)}, u32[]{:S(2)}, u32[]{:S(2)}) collective-permute-start(bf16[80,4224]{1,0:T(8,128)(2,1)S(1)} %get-tuple-element.68), channel_id=1, source_target_pairs={{0,12},{4,0},{8,4},{12,8},{1,13},{5,1},{9,5},{13,9},{2,14},{6,2},{... | collective-permute-start | bytes 2027528 | tf_op jit(solution)/shard_map/ppermute | solution.py:42
  46.8 16.4 %collective-permute-start.6 = (bf16[80,4096]{1,0:T(8,128)(2,1)S(1)}, bf16[80,4096]{1,0:T(8,128)(2,1)S(1)}, u32[]{:S(2)}, u32[]{:S(2)}) collective-permute-start(bf16[80,4096]{1,0:T(8,128)(2,1)S(1)} %get-tuple-element.65), channel_id=1, source_target_pairs={{0,16},{16,32},{32,48},{48,0},{1,17},{17,33},{33,49},{49,1},{2,18}... | collective-permute-start | bytes 1966088 | tf_op jit(solution)/shard_map/ppermute | solution.py:38
  48.0 15.2 %collective-permute-start.7 = (bf16[80,4096]{1,0:T(8,128)(2,1)S(1)}, bf16[80,4096]{1,0:T(8,128)(2,1)S(1)}, u32[]{:S(2)}, u32[]{:S(2)}) collective-permute-start(bf16[80,4096]{1,0:T(8,128)(2,1)S(1)} %get-tuple-element.66), channel_id=1, source_target_pairs={{0,48},{16,0},{32,16},{48,32},{1,49},{17,1},{33,17},{49,33},{2,50}... | collective-permute-start | bytes 1966088 | tf_op jit(solution)/shard_map/ppermute | solution.py:42
  63.3 7.6 %collective-permute-start.11 = (bf16[160,4096]{1,0:T(8,128)(2,1)S(1)}, bf16[160,4096]{1,0:T(8,128)(2,1)S(1)}, u32[]{:S(2)}, u32[]{:S(2)}) collective-permute-start(bf16[160,4096]{1,0:T(8,128)(2,1)S(1)} %stack_t.1.t), channel_id=1, source_target_pairs={{0,1},{1,0},{2,3},{3,2},{4,5},{5,4},{6,7},{7,6},{8,9},{9,8},{10,11... | collective-permute-start | bytes 3932168 | tf_op jit(solution)/shard_map/ppermute | solution.py:34
  70.9 28.1 %collective-permute-start.20 = (bf16[640,1792]{1,0:T(8,128)(2,1)S(1)}, bf16[640,1792]{1,0:T(8,128)(2,1)S(1)}, u32[]{:S(2)}, u32[]{:S(2)}) collective-permute-start(bf16[640,1792]{1,0:T(8,128)(2,1)S(1)} %get-tuple-element.91), channel_id=1, source_target_pairs={{0,1},{1,0},{2,3},{3,2},{4,5},{5,4},{6,7},{7,6},{8,9},{9,8},{10,11... | collective-permute-start | bytes 6881288 | tf_op jit(solution)/shard_map/ppermute | solution.py:34
  91.2 7.8 %collective-permute-start.19 = (bf16[640,640]{1,0:T(8,128)(2,1)S(1)}, bf16[640,640]{1,0:T(8,128)(2,1)S(1)}, u32[]{:S(2)}, u32[]{:S(2)}) collective-permute-start(bf16[640,640]{1,0:T(8,128)(2,1)S(1)} %get-tuple-element.89.far), channel_id=1, source_target_pairs={{0,1},{1,0},{2,3},{3,2},{4,5},{5,4},{6,7},{7,6},{8,9},{9,8},{10,11... | collective-permute-start | bytes 2457608 | tf_op jit(solution)/shard_map/ppermute | solution.py:34
  96.2 14.8 %collective-permute-start.21 = (s16[80,2432]{1,0:T(8,128)(2,1)S(1)}, s16[80,2432]{1,0:T(8,128)(2,1)S(1)}, u32[]{:S(2)}, u32[]{:S(2)}) collective-permute-start(s16[80,2432]{1,0:T(8,128)(2,1)S(1)} %get-tuple-element.95), channel_id=1, source_target_pairs={{0,4},{4,8},{8,12},{12,0},{1,5},{5,9},{9,13},{13,1},{2,6},{6,10},{... | collective-permute-start | bytes 1167368 | tf_op jit(solution)/shard_map/ppermute | solution.py:38
  96.3 14.7 %collective-permute-start.22 = (s16[80,2432]{1,0:T(8,128)(2,1)S(1)}, s16[80,2432]{1,0:T(8,128)(2,1)S(1)}, u32[]{:S(2)}, u32[]{:S(2)}) collective-permute-start(s16[80,2432]{1,0:T(8,128)(2,1)S(1)} %get-tuple-element.96), channel_id=1, source_target_pairs={{0,12},{4,0},{8,4},{12,8},{1,13},{5,1},{9,5},{13,9},{2,14},{6,2},{... | collective-permute-start | bytes 1167368 | tf_op jit(solution)/shard_map/ppermute | solution.py:42
  100.5 13.8 %collective-permute-start.25 = (s16[80,1920]{1,0:T(8,128)(2,1)S(1)}, s16[80,1920]{1,0:T(8,128)(2,1)S(1)}, u32[]{:S(2)}, u32[]{:S(2)}) collective-permute-start(s16[80,1920]{1,0:T(8,128)(2,1)S(1)} %get-tuple-element.92), channel_id=1, source_target_pairs={{0,16},{16,32},{32,48},{48,0},{1,17},{17,33},{33,49},{49,1},{2,18}... | collective-permute-start | bytes 921608 | tf_op jit(solution)/shard_map/ppermute | solution.py:38
  105.0 9.3 %collective-permute-start.26 = (s16[80,1920]{1,0:T(8,128)(2,1)S(1)}, s16[80,1920]{1,0:T(8,128)(2,1)S(1)}, u32[]{:S(2)}, u32[]{:S(2)}) collective-permute-start(s16[80,1920]{1,0:T(8,128)(2,1)S(1)} %get-tuple-element.107), channel_id=1, source_target_pairs={{0,48},{16,0},{32,16},{48,32},{1,49},{17,1},{33,17},{49,33},{2,50}... | collective-permute-start | bytes 921608 | tf_op jit(solution)/shard_map/ppermute | solution.py:42
  111.6 19.2 %collective-permute-start.23 = (s16[160,2432]{1,0:T(8,128)(2,1)S(1)}, s16[160,2432]{1,0:T(8,128)(2,1)S(1)}, u32[]{:S(2)}, u32[]{:S(2)}) collective-permute-start(s16[160,2432]{1,0:T(8,128)(2,1)S(1)} %get-tuple-element.105), channel_id=1, source_target_pairs={{0,4},{4,8},{8,12},{12,0},{1,5},{5,9},{9,13},{13,1},{2,6},{6,10},{... | collective-permute-start | bytes 2334728 | tf_op jit(solution)/shard_map/ppermute | solution.py:38
  111.7 19.1 %collective-permute-start.24 = (s16[160,2432]{1,0:T(8,128)(2,1)S(1)}, s16[160,2432]{1,0:T(8,128)(2,1)S(1)}, u32[]{:S(2)}, u32[]{:S(2)}) collective-permute-start(s16[160,2432]{1,0:T(8,128)(2,1)S(1)} %get-tuple-element.106), channel_id=1, source_target_pairs={{0,12},{4,0},{8,4},{12,8},{1,13},{5,1},{9,5},{13,9},{2,14},{6,2},{... | collective-permute-start | bytes 2334728 | tf_op jit(solution)/shard_map/ppermute | solution.py:42
  114.9 15.9 %collective-permute-start.27 = (s16[160,1920]{1,0:T(8,128)(2,1)S(1)}, s16[160,1920]{1,0:T(8,128)(2,1)S(1)}, u32[]{:S(2)}, u32[]{:S(2)}) collective-permute-start(s16[160,1920]{1,0:T(8,128)(2,1)S(1)} %get-tuple-element.112), channel_id=1, source_target_pairs={{0,16},{16,32},{32,48},{48,0},{1,17},{17,33},{33,49},{49,1},{2,18}... | collective-permute-start | bytes 1843208 | tf_op jit(solution)/shard_map/ppermute | solution.py:38
  116.0 14.8 %collective-permute-start.28 = (s16[160,1920]{1,0:T(8,128)(2,1)S(1)}, s16[160,1920]{1,0:T(8,128)(2,1)S(1)}, u32[]{:S(2)}, u32[]{:S(2)}) collective-permute-start(s16[160,1920]{1,0:T(8,128)(2,1)S(1)} %get-tuple-element.113), channel_id=1, source_target_pairs={{0,48},{16,0},{32,16},{48,32},{1,49},{17,1},{33,17},{49,33},{2,50}... | collective-permute-start | bytes 1843208 | tf_op jit(solution)/shard_map/ppermute | solution.py:42
  132.4 22.4 %collective-permute-start.29 = (bf16[160,4096]{1,0:T(8,128)(2,1)S(1)}, bf16[160,4096]{1,0:T(8,128)(2,1)S(1)}, u32[]{:S(2)}, u32[]{:S(2)}) collective-permute-start(bf16[160,4096]{1,0:T(8,128)(2,1)S(1)} %finish.1), channel_id=1, source_target_pairs={{0,0},{1,64},{64,1},{65,65},{2,2},{3,66},{66,3},{67,67},{4,4},{5,6... | collective-permute-start | bytes 3932168 | tf_op jit(solution)/shard_map/ppermute | solution.py:30
  139.4 15.3 %collective-permute-start.30 = (f32[1,128]{1,0:T(1,128)S(1)}, f32[1,128]{1,0:T(1,128)S(1)}, u32[]{:S(2)}, u32[]{:S(2)}) collective-permute-start(f32[1,128]{1,0:T(1,128)S(1)} %get-tuple-element.115), channel_id=1, source_target_pairs={{0,0},{1,64},{64,1},{65,65},{2,2},{3,66},{66,3},{67,67},{4,4},{5,6... | collective-permute-start | bytes 1544 | tf_op jit(solution)/shard_map/ppermute | solution.py:30
  141.3 13.4 %collective-permute-start.31 = (f32[1,128]{1,0:T(1,128)S(1)}, f32[1,128]{1,0:T(1,128)S(1)}, u32[]{:S(2)}, u32[]{:S(2)}) collective-permute-start(f32[1,128]{1,0:T(1,128)S(1)} %get-tuple-element.115), channel_id=1, source_target_pairs={{1,0},{65,1},{0,64},{64,65},{3,2},{67,3},{2,66},{66,67},{5,4},{69,... | collective-permute-start | bytes 1544 | tf_op jit(solution)/shard_map/ppermute | solution.py:420
  (8 other events, 36.8 us)

commit v6 on v5

--- a/solution.py
+++ b/solution.py
@@ -114,85 +114,113 @@
     v[:, e.shape[1] :] = digits[...]
 
 
-def statistics(s, ids, mates, multiplier, own, rstat, cstat):
-    tall, wide = s.shape
-
-    def first(i, carry):
-        top, pos = carry
-        r = pl.ds(pl.multiple_of(i * LANES, LANES), LANES)
-        v = s[r, :] * multiplier
-        pos += jnp.sum(jnp.where(ids == mates[r, 0:1], v, F32(0.0)), axis=0, keepdims=True)
-        if own:
-            row_ids = i * LANES + lax.broadcasted_iota(jnp.int32, (LANES, wide), 0)
-            col_ids = lax.broadcasted_iota(jnp.int32, (LANES, wide), 1)
-            v = jnp.where((row_ids == col_ids) & (row_ids < tall // 4), F32(-1e30), v)
-        s[r, :] = v
+def as_row(v):
+    return jnp.transpose(jnp.broadcast_to(v, (v.shape[0], LANES)))[0:1, :]
+
+
+def join(m1, l1, m2, l2):
+    m = jnp.maximum(m1, m2)
+    return m, l1 * jnp.exp(m1 - m) + l2 * jnp.exp(m2 - m)
+
+
+def statistics(s, row, col, step, ids, mates, multiplier, own):
+    tops, lows, top, pos, low = [], [], None, F32(0.0), F32(0.0)
+    starts = range(row.start, row.stop, step)
+    for at in starts:
+        r = slice(at, at + step)
+        v = s[r, col] * multiplier
+        pos += jnp.sum(jnp.where(ids[:, col] == mates[r, 0:1], v, F32(0.0)), axis=0, keepdims=True)
+        if own and at == 0:
+            row_ids = lax.broadcasted_iota(jnp.int32, v.shape, 0)
+            col_ids = lax.broadcasted_iota(jnp.int32, v.shape, 1) + col.start
+            v = jnp.where(row_ids == col_ids, F32(-1e30), v)
+        s[r, col] = v
         m = jnp.max(v, axis=1, keepdims=True)
-        l = jnp.sum(jnp.exp(v - m), axis=1, keepdims=True)
-        rstat[0:1, r] = jnp.transpose(jnp.broadcast_to(m, (LANES, LANES)))[0:1, :]
-        rstat[1:2, r] = jnp.transpose(jnp.broadcast_to(l, (LANES, LANES)))[0:1, :]
-        return jnp.maximum(top, jnp.max(v, axis=0, keepdims=True)), pos
-
-    start = jnp.full((1, wide), -1e30, F32), jnp.zeros((1, wide), F32)
-    top, pos = lax.fori_loop(0, tall // LANES, first, start)
-
-    def second(i, low):
-        r = pl.ds(pl.multiple_of(i * LANES, LANES), LANES)
-        return low + jnp.sum(jnp.exp(s[r, :] - top), axis=0, keepdims=True)
-
-    cstat[0:1, :] = top
-    cstat[1:2, :] = lax.fori_loop(0, tall // LANES, second, jnp.zeros((1, wide), F32))
-    cstat[2:3, :] = pos
-
-
-def near_kernel(v, zd, zu, b, bo, s1, s2, a):
+        tops.append(as_row(m))
+        lows.append(as_row(jnp.sum(jnp.exp(v - m), axis=1, keepdims=True)))
+        m = jnp.max(v, axis=0, keepdims=True)
+        top = m if top is None else jnp.maximum(top, m)
+    for at in starts:
+        low += jnp.sum(jnp.exp(s[at : at + step, col] - top), axis=0, keepdims=True)
+    return jnp.concatenate(tops, 1), jnp.concatenate(lows, 1), top, low, pos
+
+
+def put_mates(r, mates, at):
+    n, width = r.shape[0], r.shape[1] - LANES
+    two = r[:, width:].astype(F32)
+    mates[at : at + n, :] = jnp.broadcast_to(two[:, 0:1] * F32(64.0) + two[:, 1:2], (n, LANES))
+
+
+def near_kernel(mult, v, zd, zu, b, bo, cols, s1, s2, known1, known2, a, mates):
+    step, n, width = v.shape[0], s1.shape[0], a.shape[1]
     at = 0
     for r in (v, zd, zu):
-        a[at : at + r.shape[0], :] = r[:, : a.shape[1]]
-        at += r.shape[0]
+        a[at : at + step, :] = r[:, :width]
+        put_mates(r, mates, at)
+        at += step
     s1[...] = dot(a[...], b[...], NT)
     s2[...] = dot(a[...], bo[...], NT)
-
-
-def complete(s, known, a, b, t):
-    n = known.shape[0]
-    s[0:n, 0:n] = known[...]
+    side = cols.shape[1] // 2
+    for s, known, first in ((s1, known1, 0), (s2, known2, side)):
+        ids = cols[:, first : first + n]
+        found = statistics(s, slice(0, n), slice(0, n), step, ids, mates, mult[0], first == 0)
+        known[...] = jnp.zeros(known.shape, F32)
+        for i, line in enumerate(found):
+            known[i : i + 1, :] = line
+
+
+def complete(s, tile, known, a, b, t, ids, mates, multiplier, own):
+    n, side = tile.shape[0], s.shape[0]
+    step = side - n
+    s[0:n, 0:n] = tile[...]
     s[n:, 0:n] = dot(a[n:, :], b[...], NT)
     s[:, n:] = dot(a[...], t[...], NT)
-
-
-def early_kernel(mult, v, zd, zu, za, zb, b, t, known, cols, a, last, mates, s, rstat, cstat):
+    rm0, rl0, cm0, cl0, pos0 = (known[i : i + 1, :] for i in range(5))
+    rm1, rl1, cm1, cl1, pos1 = statistics(
+        s, slice(0, n), slice(n, side), step, ids, mates, multiplier, own
+    )
+    rm2, rl2, cm2, cl2, pos2 = statistics(
+        s, slice(n, side), slice(0, side), step, ids, mates, multiplier, own
+    )
+    rm, rl = join(rm0, rl0, rm1, rl1)
+    cat = lambda x, y: jnp.concatenate([x, y], 1)
+    cm, cl = join(cat(cm0, cm1), cat(cl0, cl1), cm2, cl2)
+    return cat(rm, rm2), cat(rl, rl2), cm, cl, cat(pos0, pos1) + pos2
+
+
+def early_kernel(mult, v, zd, zu, za, zb, b, t, tile, known, cols, a, last, mates, s, rstat, cstat):
     width, w = a.shape[1], last.shape[1]
     at = 0
     for r in (v, zd, zu, za, zb):
         n = r.shape[0]
         a[at : at + n, :] = r[:, :width]
         last[at : at + n, :] = r[:, width - w : width]
-        two = r[:, width:].astype(F32)
-        mates[at : at + n, :] = jnp.broadcast_to(two[:, 0:1] * F32(64.0) + two[:, 1:2], (n, LANES))
+        put_mates(r, mates, at)
         at += n
-    complete(s, known, a, b, t)
+    found = complete(s, tile, known, a, b, t, cols[:, : s.shape[1]], mates, mult[0], True)
     rstat[...] = jnp.zeros(rstat.shape, F32)
     cstat[...] = jnp.zeros(cstat.shape, F32)
-    statistics(s, cols[:, : s.shape[1]], mates, mult[0], True, rstat, cstat)
+    for i, dst in enumerate((rstat, rstat, cstat, cstat, cstat)):
+        j = i if i < 2 else i - 2
+        dst[j : j + 1, :] = found[i]
 
 
 def column(row, n):
     return jnp.transpose(jnp.broadcast_to(row, (LANES, n)))[:, :1]
 
 
-def tail_kernel(mult, a, b, t, known, mates, cols, rs1, cs1, s, rstat, cstat, rs2, cs2):
+def tail_kernel(mult, a, b, t, tile, known, mates, cols, rs, cs, s, rstat, cstat):
     side = s.shape[1]
-    complete(s, known, a, b, t)
-    statistics(s, cols[:, side:], mates, mult[0], False, rs2, cs2)
-    m1, m2 = rs1[0:1, :], rs2[0:1, :]
-    m = jnp.maximum(m1, m2)
-    positive = jnp.sum(cs1[2:3, :] + cs2[2:3, :], axis=1, keepdims=True)
+    rm, rl, cm, cl, pos = complete(
+        s, tile, known, a, b, t, cols[:, side:], mates, mult[0], False
+    )
+    positive = jnp.sum(cs[2:3, :] + pos, axis=1, keepdims=True)
     rstat[...] = jnp.broadcast_to(positive, rstat.shape)
-    rstat[0:1, :] = m
-    rstat[1:2, :] = rs1[1:2, :] * jnp.exp(m1 - m) + rs2[1:2, :] * jnp.exp(m2 - m)
-    cstat[:, 0:side] = cs1[...]
-    cstat[:, side:] = cs2[...]
+    rstat[0:1, :], rstat[1:2, :] = join(rs[0:1, :], rs[1:2, :], rm, rl)
+    cstat[:, 0:side] = cs[...]
+    cstat[:, side:] = jnp.zeros(cs.shape, F32)
+    cstat[0:1, side:] = cm
+    cstat[1:2, side:] = cl
 
 
 def merge_kernel(mine, other, r0, r1, r2, r3, out, lse_r):
@@ -350,19 +378,21 @@
     b = stack("stack_b", u, xd, xu)
     bo = other_core(b)
     n = b.shape[0]
-    known1, known2 = call(
-        near_kernel, "near", (v, zd, zu, b, bo), (shape(n, n), shape(n, n)),
-        scratch=[pltpu.VMEM((n, width), BF16)], flops=4 * n * n * width,
-    )
-    xa, xb, za, zb, known1, known2 = lax.optimization_barrier(
-        (up(xa, "x"), down(xb, "x"), up(za, "z"), down(zb, "z"), known1, known2)
+    tile1, tile2, known1, known2 = call(
+        near_kernel, "near", (logit_scale, v, zd, zu, b, bo, cols),
+        (shape(n, n), shape(n, n), shape(8, n), shape(8, n)),
+        scratch=[pltpu.VMEM((n, width), BF16), pltpu.VMEM((n, LANES), F32)],
+        flops=4 * n * n * width,
+    )
+    xa, xb, za, zb, tile1, tile2 = lax.optimization_barrier(
+        (up(xa, "x"), down(xb, "x"), up(za, "z"), down(zb, "z"), tile1, tile2)
     )
     t = stack("stack_t", xa, xb)
     to = other_core(t)
     along = {"z": width * 9 // 16, "x": width * 7 // 16}
     flops = 2 * side * side * width
     a, last, mates, near, rstat, cstat = call(
-        early_kernel, "early", (logit_scale, v, zd, zu, za, zb, b, t, known1, cols),
+        early_kernel, "early", (logit_scale, v, zd, zu, za, zb, b, t, tile1, known1, cols),
         (
             shape(side, width, dtype=BF16), shape(side, along["x"], dtype=BF16),
             shape(side, LANES), shape(side, side), shape(8, side), shape(8, side),
@@ -371,9 +401,9 @@
     )
     last_other = other_core(after(last, to))
     far, rstat, cstat = call(
-        tail_kernel, "tail", (logit_scale, a, bo, to, known2, mates, cols, rstat, cstat),
+        tail_kernel, "tail", (logit_scale, a, bo, to, tile2, known2, mates, cols, rstat, cstat),
         (shape(side, side), shape(8, side), shape(8, 2 * side)),
-        scratch=[pltpu.VMEM((8, side), F32), pltpu.VMEM((8, side), F32)], flops=flops,
+        flops=flops,
     )
     cstat_other = other_core(cstat)
     rstats = gather_small(rstat, "z")

time: 157 us -> 155 us (0.987)
  waiting for transfers between devices: 71.7 us -> 69.7 us
where the time goes in v6:
time: 155 us
  waiting for transfers between devices  69.7 us (45%)
  starting transfers between devices  51.1 us (33%)
  Pallas kernels  30.2 us (19%)
  between operations  2.74 us (2%)
    ppermute x8, waiting for transfers between devices, up(): return lax.ppermute(v, axis, ring(4, 1))  35 us
    pallas_call x16, Pallas kernels, call(): pl.pallas_call(kernel, name=name, out_shape=tuple((jax.ShapeDtypeStruct(o...  30.2 us
    ppermute x4, waiting for transfers between devices, swap(): return lax.ppermute(v, ('yl', 'c'), SWAP)  27.1 us
    ppermute x8, starting transfers between devices, down(): return lax.ppermute(v, axis, ring(4, -1))  17.9 us
    ppermute x4, starting transfers between devices, swap(): return lax.ppermute(v, ('yl', 'c'), SWAP)  15.4 us
    ppermute x6, waiting for transfers between devices, gather_small(): return [v] + [lax.ppermute(v, axis, ring(4, -k)) for k in ORDER[1:]]  7.08 us
    ppermute x5, starting transfers between devices, other_core(): return lax.ppermute(v, 'c', ring(2, 1))  6.26 us
    ppermute x6, starting transfers between devices, gather_small(): return [v] + [lax.ppermute(v, axis, ring(4, -k)) for k in ORDER[1:]]  5.78 us
  transfers between devices with their start and end apart: 32, of which 10 were waited for; matrix products, arithmetic and copies ran while one was open for 0% of the time, Pallas kernels for 18%

profile of v6, /device:TPU:1, one launch (start us, length us, event | category | flops | bytes accessed | tf_op | source)
XLA Modules:
  0.0 155.2 jit_solution(4226503926291116742)
XLA Ops:
  0.6 4.6 %collective-permute-start = (bf16[160,4096]{1,0:T(8,128)(2,1)}, bf16[160,4096]{1,0:T(8,128)(2,1)S(1)}, u32[]{:S(2)}, u32[]{:S(2)}) collective-permute-start(bf16[160,4096]{1,0:T(8,128)(2,1)} %param.3), channel_id=1, source_target_pairs={{0,0},{1,64},{64,1},{65,65},{2,2},{3,66},{66,3},{67,67},{4,4},{5,6... | collective-permute-start | bytes 3932168 | tf_op jit(solution)/shard_map/ppermute | solution.py:30
  5.2 1.9 %collective-permute-start.1 = (s32[1,160]{1,0:T(1,128)}, s32[1,160]{1,0:T(1,128)S(1)}, u32[]{:S(2)}, u32[]{:S(2)}) collective-permute-start(s32[1,160]{1,0:T(1,128)} %bitcast.5), channel_id=1, source_target_pairs={{0,0},{1,64},{64,1},{65,65},{2,2},{3,66},{66,3},{67,67},{4,4},{5,6... | collective-permute-start | bytes 1928 | tf_op jit(solution)/shard_map/ppermute | solution.py:30
  7.2 13.8 %collective-permute-done.1 = s32[1,160]{1,0:T(1,128)S(1)} collective-permute-done((s32[1,160]{1,0:T(1,128)}, s32[1,160]{1,0:T(1,128)S(1)}, u32[]{:S(2)}, u32[]{:S(2)}) %collective-permute-start.1) | collective-permute-done | bytes 672 | tf_op jit(solution)/shard_map/ppermute | solution.py:30
  23.7 2.2 %collective-permute-start.3 = (bf16[160,4224]{1,0:T(8,128)(2,1)S(1)}, bf16[160,4224]{1,0:T(8,128)(2,1)S(1)}, u32[]{:S(2)}, u32[]{:S(2)}) collective-permute-start(bf16[160,4224]{1,0:T(8,128)(2,1)S(1)} %get-tuple-element.61.v), channel_id=1, source_target_pairs={{0,12},{4,0},{8,4},{12,8},{1,13},{5,1},{9,5},{13,9},{2,14},{6,2},{... | collective-permute-start | bytes 4055048 | tf_op jit(solution)/shard_map/ppermute | solution.py:42
  28.5 15.0 %collective-permute-done.4.xu.refs_2_ = bf16[160,4096]{1,0:T(8,128)(2,1)S(1)} collective-permute-done((bf16[160,4096]{1,0:T(8,128)(2,1)S(1)}, bf16[160,4096]{1,0:T(8,128)(2,1)S(1)}, u32[]{:S(2)}, u32[]{:S(2)}) %collective-permute-start.4) | collective-permute-done | bytes 1310752 | tf_op jit(solution)/shard_map/ppermute | solution.py:38
  44.2 2.7 %collective-permute-start.9 = (bf16[80,4224]{1,0:T(8,128)(2,1)S(1)}, bf16[80,4224]{1,0:T(8,128)(2,1)S(1)}, u32[]{:S(2)}, u32[]{:S(2)}) collective-permute-start(bf16[80,4224]{1,0:T(8,128)(2,1)S(1)} %get-tuple-element.70), channel_id=1, source_target_pairs={{0,12},{4,0},{8,4},{12,8},{1,13},{5,1},{9,5},{13,9},{2,14},{6,2},{... | collective-permute-start | bytes 2027528 | tf_op jit(solution)/shard_map/ppermute | solution.py:42
  50.7 5.3 %near.1 = (f32[480,480]{1,0:T(8,128)S(1)}, f32[480,480]{1,0:T(8,128)S(1)}, f32[8,480]{1,0:T(8,128)S(1)}, f32[8,480]{1,0:T(8,128)S(1)}) custom-call(f32[1]{0:T(128)S(6)} %copy.10.mult, bf16[160,4224]{1,0:T(8,128)(2,1)S(1)} %get-tuple-element.61.v, bf16[160,4224]{1,0:T(8,128)(2,1)S(1)} %collective-permute-done.3.zd, ...), custom_call_target="tpu_custom_call" | custom-call | flops 3774873600 | bytes 13798404 | tf_op jit(solution)/shard_map/near/pallas_call | solution.py:65
  55.9 7.3 %collective-permute-done.6.refs_0_ = bf16[80,4096]{1,0:T(8,128)(2,1)S(1)} collective-permute-done((bf16[80,4096]{1,0:T(8,128)(2,1)S(1)}, bf16[80,4096]{1,0:T(8,128)(2,1)S(1)}, u32[]{:S(2)}, u32[]{:S(2)}) %collective-permute-start.6) | collective-permute-done | bytes 655392 | tf_op jit(solution)/shard_map/ppermute | solution.py:38
  63.3 2.2 %collective-permute-start.11 = (bf16[160,4096]{1,0:T(8,128)(2,1)S(1)}, bf16[160,4096]{1,0:T(8,128)(2,1)S(1)}, u32[]{:S(2)}, u32[]{:S(2)}) collective-permute-start(bf16[160,4096]{1,0:T(8,128)(2,1)S(1)} %stack_t.1.t), channel_id=1, source_target_pairs={{0,1},{1,0},{2,3},{3,2},{4,5},{5,4},{6,7},{7,6},{8,9},{9,8},{10,11... | collective-permute-start | bytes 3932168 | tf_op jit(solution)/shard_map/ppermute | solution.py:34
  65.6 4.3 %early.1 = (bf16[640,4096]{1,0:T(8,128)(2,1)S(1)}, bf16[640,1792]{1,0:T(8,128)(2,1)S(1)}, f32[640,128]{1,0:T(8,128)S(1)}, f32[640,640]{1,0:T(8,128)S(1)}, f32[8,640]{1,0:T(8,128)S(1)}, /*index=5*/f32[8,640]{1,0:T(8,128)S(1)}) custom-call(f32[1]{0:T(128)S(6)} %copy.10.mult, bf16[160,4224]{1,0:T(8,128)(2,1)S(1)} %get-tuple-element.61.v, ...), custom_call_target="tpu_custom_call" | custom-call | flops 3355443200 | bytes 21135364 | tf_op jit(solution)/shard_map/early/pallas_call | solution.py:65
  69.9 4.3 %tail.1 = (f32[640,640]{1,0:T(8,128)S(1)}, f32[8,640]{1,0:T(8,128)S(1)}, f32[8,1280]{1,0:T(8,128)S(1)}) custom-call(f32[1]{0:T(128)S(6)} %copy.10.mult, bf16[640,4096]{1,0:T(8,128)(2,1)S(1)} %get-tuple-element.81.a, bf16[480,4096]{1,0:T(8,128)(2,1)S(1)} %collective-permute-done.10.bo.b, bf16[160,4096]{1,0:T(8,128)(2,1)S(1)} %collective-permute-done.11.t.to, ...), custom_call_target="tpu_custom_call" | custom-call | flops 3355443200 | bytes 13496324 | tf_op jit(solution)/shard_map/tail/pallas_call | solution.py:65
  80.6 2.7 %collective-permute-start.16 = (f32[8,1280]{1,0:T(8,128)S(1)}, f32[8,1280]{1,0:T(8,128)S(1)}, u32[]{:S(2)}, u32[]{:S(2)}) collective-permute-start(f32[8,1280]{1,0:T(8,128)S(1)} %get-tuple-element.91.c0), channel_id=1, source_target_pairs={{0,48},{16,0},{32,16},{48,32},{1,49},{17,1},{33,17},{49,33},{2,50}... | collective-permute-start | bytes 122888 | tf_op jit(solution)/shard_map/ppermute | solution.py:50
  84.8 3.1 %collective-permute-done.17.c2 = f32[8,1280]{1,0:T(8,128)S(1)} collective-permute-done((f32[8,1280]{1,0:T(8,128)S(1)}, f32[8,1280]{1,0:T(8,128)S(1)}, u32[]{:S(2)}, u32[]{:S(2)}) %collective-permute-start.17) | collective-permute-done | bytes 40992 | tf_op jit(solution)/shard_map/ppermute | solution.py:50
  89.6 3.3 %collective-permute-start.19 = (bf16[640,640]{1,0:T(8,128)(2,1)S(1)}, bf16[640,640]{1,0:T(8,128)(2,1)S(1)}, u32[]{:S(2)}, u32[]{:S(2)}) collective-permute-start(bf16[640,640]{1,0:T(8,128)(2,1)S(1)} %get-tuple-element.93.far), channel_id=1, source_target_pairs={{0,1},{1,0},{2,3},{3,2},{4,5},{5,4},{6,7},{7,6},{8,9},{9,8},{10,11... | collective-permute-start | bytes 2457608 | tf_op jit(solution)/shard_map/ppermute | solution.py:34
  94.7 2.7 %collective-permute-start.22 = (s16[80,2432]{1,0:T(8,128)(2,1)S(1)}, s16[80,2432]{1,0:T(8,128)(2,1)S(1)}, u32[]{:S(2)}, u32[]{:S(2)}) collective-permute-start(s16[80,2432]{1,0:T(8,128)(2,1)S(1)} %get-tuple-element.100), channel_id=1, source_target_pairs={{0,12},{4,0},{8,4},{12,8},{1,13},{5,1},{9,5},{13,9},{2,14},{6,2},{... | collective-permute-start | bytes 1167368 | tf_op jit(solution)/shard_map/ppermute | solution.py:42
  99.2 4.1 %rest_z.1 = (s16[80,2432]{1,0:T(8,128)(2,1)S(1)}, s16[80,2432]{1,0:T(8,128)(2,1)S(1)}, f32[80,2304]{1,0:T(8,128)S(1)}, f32[80,2304]{1,0:T(8,128)S(1)}, f32[160,2304]{1,0:T(8,128)S(1)}) custom-call(bf16[640,640]{1,0:T(8,128)(2,1)S(1)} %get-tuple-element.101.near, bf16[640,640]{1,0:T(8,128)(2,1)S(1)} %get-tuple-element.93.far, ...), custom_call_target="tpu_custom_call" | custom-call | flops 2831155200 | bytes 15851520 | tf_op jit(solution)/shard_map/rest_z/pallas_call | solution.py:65
  103.3 2.8 %collective-permute-start.26 = (s16[80,1920]{1,0:T(8,128)(2,1)S(1)}, s16[80,1920]{1,0:T(8,128)(2,1)S(1)}, u32[]{:S(2)}, u32[]{:S(2)}) collective-permute-start(s16[80,1920]{1,0:T(8,128)(2,1)S(1)} %get-tuple-element.111), channel_id=1, source_target_pairs={{0,48},{16,0},{32,16},{48,32},{1,49},{17,1},{33,17},{49,33},{2,50}... | collective-permute-start | bytes 921608 | tf_op jit(solution)/shard_map/ppermute | solution.py:42
  106.0 3.2 %rest_x.1 = (s16[80,1920]{1,0:T(8,128)(2,1)S(1)}, s16[80,1920]{1,0:T(8,128)(2,1)S(1)}, f32[80,1792]{1,0:T(8,128)S(1)}, f32[80,1792]{1,0:T(8,128)S(1)}, f32[160,1792]{1,0:T(8,128)S(1)}) custom-call(bf16[640,640]{1,0:T(8,128)(2,1)S(1)} %get-tuple-element.101.near, bf16[640,640]{1,0:T(8,128)(2,1)S(1)} %collective-permute-done.19.far, ...), custom_call_target="tpu_custom_call" | custom-call | flops 2202009600 | bytes 12083200 | tf_op jit(solution)/shard_map/rest_x/pallas_call | solution.py:65
  109.9 2.7 %collective-permute-start.24 = (s16[160,2432]{1,0:T(8,128)(2,1)S(1)}, s16[160,2432]{1,0:T(8,128)(2,1)S(1)}, u32[]{:S(2)}, u32[]{:S(2)}) collective-permute-start(s16[160,2432]{1,0:T(8,128)(2,1)S(1)} %get-tuple-element.110), channel_id=1, source_target_pairs={{0,12},{4,0},{8,4},{12,8},{1,13},{5,1},{9,5},{13,9},{2,14},{6,2},{... | collective-permute-start | bytes 2334728 | tf_op jit(solution)/shard_map/ppermute | solution.py:42
  114.3 2.0 %collective-permute-start.28 = (s16[160,1920]{1,0:T(8,128)(2,1)S(1)}, s16[160,1920]{1,0:T(8,128)(2,1)S(1)}, u32[]{:S(2)}, u32[]{:S(2)}) collective-permute-start(s16[160,1920]{1,0:T(8,128)(2,1)S(1)} %get-tuple-element.117), channel_id=1, source_target_pairs={{0,48},{16,0},{32,16},{48,32},{1,49},{17,1},{33,17},{49,33},{2,50}... | collective-permute-start | bytes 1843208 | tf_op jit(solution)/shard_map/ppermute | solution.py:42
  116.3 12.7 %collective-permute-done.23.uz = s16[160,2432]{1,0:T(8,128)(2,1)S(1)} collective-permute-done((s16[160,2432]{1,0:T(8,128)(2,1)S(1)}, s16[160,2432]{1,0:T(8,128)(2,1)S(1)}, u32[]{:S(2)}, u32[]{:S(2)}) %collective-permute-start.23) | collective-permute-done | bytes 778272 | tf_op jit(solution)/shard_map/ppermute | solution.py:38
  130.6 7.0 %collective-permute-start.29 = (bf16[160,4096]{1,0:T(8,128)(2,1)S(1)}, bf16[160,4096]{1,0:T(8,128)(2,1)S(1)}, u32[]{:S(2)}, u32[]{:S(2)}) collective-permute-start(bf16[160,4096]{1,0:T(8,128)(2,1)S(1)} %finish.1), channel_id=1, source_target_pairs={{0,0},{1,64},{64,1},{65,65},{2,2},{3,66},{66,3},{67,67},{4,4},{5,6... | collective-permute-start | bytes 3932168 | tf_op jit(solution)/shard_map/ppermute | solution.py:30
  137.6 1.9 %collective-permute-start.30 = (f32[1,128]{1,0:T(1,128)S(1)}, f32[1,128]{1,0:T(1,128)S(1)}, u32[]{:S(2)}, u32[]{:S(2)}) collective-permute-start(f32[1,128]{1,0:T(1,128)S(1)} %get-tuple-element.119), channel_id=1, source_target_pairs={{0,0},{1,64},{64,1},{65,65},{2,2},{3,66},{66,3},{67,67},{4,4},{5,6... | collective-permute-start | bytes 1544 | tf_op jit(solution)/shard_map/ppermute | solution.py:30
  139.6 13.3 %collective-permute-done.30 = f32[1,128]{1,0:T(1,128)S(1)} collective-permute-done((f32[1,128]{1,0:T(1,128)S(1)}, f32[1,128]{1,0:T(1,128)S(1)}, u32[]{:S(2)}, u32[]{:S(2)}) %collective-permute-start.30) | collective-permute-done | bytes 544 | tf_op jit(solution)/shard_map/ppermute | solution.py:30
  (63 shorter events, 27.7 us)
Async XLA Ops:
  0.6 20.7 %collective-permute-start = (bf16[160,4096]{1,0:T(8,128)(2,1)}, bf16[160,4096]{1,0:T(8,128)(2,1)S(1)}, u32[]{:S(2)}, u32[]{:S(2)}) collective-permute-start(bf16[160,4096]{1,0:T(8,128)(2,1)} %param.3), channel_id=1, source_target_pairs={{0,0},{1,64},{64,1},{65,65},{2,2},{3,66},{66,3},{67,67},{4,4},{5,6... | collective-permute-start | bytes 3932168 | tf_op jit(solution)/shard_map/ppermute | solution.py:30
  5.2 15.8 %collective-permute-start.1 = (s32[1,160]{1,0:T(1,128)}, s32[1,160]{1,0:T(1,128)S(1)}, u32[]{:S(2)}, u32[]{:S(2)}) collective-permute-start(s32[1,160]{1,0:T(1,128)} %bitcast.5), channel_id=1, source_target_pairs={{0,0},{1,64},{64,1},{65,65},{2,2},{3,66},{66,3},{67,67},{4,4},{5,6... | collective-permute-start | bytes 1928 | tf_op jit(solution)/shard_map/ppermute | solution.py:30
  22.0 21.6 %collective-permute-start.2 = (bf16[160,4224]{1,0:T(8,128)(2,1)S(1)}, bf16[160,4224]{1,0:T(8,128)(2,1)S(1)}, u32[]{:S(2)}, u32[]{:S(2)}) collective-permute-start(bf16[160,4224]{1,0:T(8,128)(2,1)S(1)} %get-tuple-element.61.v), channel_id=1, source_target_pairs={{0,4},{4,8},{8,12},{12,0},{1,5},{5,9},{9,13},{13,1},{2,6},{6,10},{... | collective-permute-start | bytes 4055048 | tf_op jit(solution)/shard_map/ppermute | solution.py:38
  23.7 19.9 %collective-permute-start.3 = (bf16[160,4224]{1,0:T(8,128)(2,1)S(1)}, bf16[160,4224]{1,0:T(8,128)(2,1)S(1)}, u32[]{:S(2)}, u32[]{:S(2)}) collective-permute-start(bf16[160,4224]{1,0:T(8,128)(2,1)S(1)} %get-tuple-element.61.v), channel_id=1, source_target_pairs={{0,12},{4,0},{8,4},{12,8},{1,13},{5,1},{9,5},{13,9},{2,14},{6,2},{... | collective-permute-start | bytes 4055048 | tf_op jit(solution)/shard_map/ppermute | solution.py:42
  25.9 17.7 %collective-permute-start.4 = (bf16[160,4096]{1,0:T(8,128)(2,1)S(1)}, bf16[160,4096]{1,0:T(8,128)(2,1)S(1)}, u32[]{:S(2)}, u32[]{:S(2)}) collective-permute-start(bf16[160,4096]{1,0:T(8,128)(2,1)S(1)} %get-tuple-element.62.refs_0_), channel_id=1, source_target_pairs={{0,16},{16,32},{32,48},{48,0},{1,17},{17,33},{33,49},{49,1},{2,18}... | collective-permute-start | bytes 3932168 | tf_op jit(solution)/shard_map/ppermute | solution.py:38
  27.1 16.5 %collective-permute-start.5 = (bf16[160,4096]{1,0:T(8,128)(2,1)S(1)}, bf16[160,4096]{1,0:T(8,128)(2,1)S(1)}, u32[]{:S(2)}, u32[]{:S(2)}) collective-permute-start(bf16[160,4096]{1,0:T(8,128)(2,1)S(1)} %get-tuple-element.62.refs_0_), channel_id=1, source_target_pairs={{0,48},{16,0},{32,16},{48,32},{1,49},{17,1},{33,17},{49,33},{2,50}... | collective-permute-start | bytes 3932168 | tf_op jit(solution)/shard_map/ppermute | solution.py:42
  43.8 6.9 %collective-permute-start.10 = (bf16[480,4096]{1,0:T(8,128)(2,1)S(1)}, bf16[480,4096]{1,0:T(8,128)(2,1)S(1)}, u32[]{:S(2)}, u32[]{:S(2)}) collective-permute-start(bf16[480,4096]{1,0:T(8,128)(2,1)S(1)} %stack_b.1.b), channel_id=1, source_target_pairs={{0,1},{1,0},{2,3},{3,2},{4,5},{5,4},{6,7},{7,6},{8,9},{9,8},{10,11... | collective-permute-start | bytes 11796488 | tf_op jit(solution)/shard_map/ppermute | solution.py:34
  44.1 19.1 %collective-permute-start.8 = (bf16[80,4224]{1,0:T(8,128)(2,1)S(1)}, bf16[80,4224]{1,0:T(8,128)(2,1)S(1)}, u32[]{:S(2)}, u32[]{:S(2)}) collective-permute-start(bf16[80,4224]{1,0:T(8,128)(2,1)S(1)} %get-tuple-element.69), channel_id=1, source_target_pairs={{0,4},{4,8},{8,12},{12,0},{1,5},{5,9},{9,13},{13,1},{2,6},{6,10},{... | collective-permute-start | bytes 2027528 | tf_op jit(solution)/shard_map/ppermute | solution.py:38
  44.2 19.1 %collective-permute-start.9 = (bf16[80,4224]{1,0:T(8,128)(2,1)S(1)}, bf16[80,4224]{1,0:T(8,128)(2,1)S(1)}, u32[]{:S(2)}, u32[]{:S(2)}) collective-permute-start(bf16[80,4224]{1,0:T(8,128)(2,1)S(1)} %get-tuple-element.70), channel_id=1, source_target_pairs={{0,12},{4,0},{8,4},{12,8},{1,13},{5,1},{9,5},{13,9},{2,14},{6,2},{... | collective-permute-start | bytes 2027528 | tf_op jit(solution)/shard_map/ppermute | solution.py:42
  46.8 16.4 %collective-permute-start.6 = (bf16[80,4096]{1,0:T(8,128)(2,1)S(1)}, bf16[80,4096]{1,0:T(8,128)(2,1)S(1)}, u32[]{:S(2)}, u32[]{:S(2)}) collective-permute-start(bf16[80,4096]{1,0:T(8,128)(2,1)S(1)} %get-tuple-element.67), channel_id=1, source_target_pairs={{0,16},{16,32},{32,48},{48,0},{1,17},{17,33},{33,49},{49,1},{2,18}... | collective-permute-start | bytes 1966088 | tf_op jit(solution)/shard_map/ppermute | solution.py:38
  48.0 15.2 %collective-permute-start.7 = (bf16[80,4096]{1,0:T(8,128)(2,1)S(1)}, bf16[80,4096]{1,0:T(8,128)(2,1)S(1)}, u32[]{:S(2)}, u32[]{:S(2)}) collective-permute-start(bf16[80,4096]{1,0:T(8,128)(2,1)S(1)} %get-tuple-element.68), channel_id=1, source_target_pairs={{0,48},{16,0},{32,16},{48,32},{1,49},{17,1},{33,17},{49,33},{2,50}... | collective-permute-start | bytes 1966088 | tf_op jit(solution)/shard_map/ppermute | solution.py:42
  69.8 27.6 %collective-permute-start.20 = (bf16[640,1792]{1,0:T(8,128)(2,1)S(1)}, bf16[640,1792]{1,0:T(8,128)(2,1)S(1)}, u32[]{:S(2)}, u32[]{:S(2)}) collective-permute-start(bf16[640,1792]{1,0:T(8,128)(2,1)S(1)} %get-tuple-element.95), channel_id=1, source_target_pairs={{0,1},{1,0},{2,3},{3,2},{4,5},{5,4},{6,7},{7,6},{8,9},{9,8},{10,11... | collective-permute-start | bytes 6881288 | tf_op jit(solution)/shard_map/ppermute | solution.py:34
  89.6 7.8 %collective-permute-start.19 = (bf16[640,640]{1,0:T(8,128)(2,1)S(1)}, bf16[640,640]{1,0:T(8,128)(2,1)S(1)}, u32[]{:S(2)}, u32[]{:S(2)}) collective-permute-start(bf16[640,640]{1,0:T(8,128)(2,1)S(1)} %get-tuple-element.93.far), channel_id=1, source_target_pairs={{0,1},{1,0},{2,3},{3,2},{4,5},{5,4},{6,7},{7,6},{8,9},{9,8},{10,11... | collective-permute-start | bytes 2457608 | tf_op jit(solution)/shard_map/ppermute | solution.py:34
  94.7 14.5 %collective-permute-start.21 = (s16[80,2432]{1,0:T(8,128)(2,1)S(1)}, s16[80,2432]{1,0:T(8,128)(2,1)S(1)}, u32[]{:S(2)}, u32[]{:S(2)}) collective-permute-start(s16[80,2432]{1,0:T(8,128)(2,1)S(1)} %get-tuple-element.99), channel_id=1, source_target_pairs={{0,4},{4,8},{8,12},{12,0},{1,5},{5,9},{9,13},{13,1},{2,6},{6,10},{... | collective-permute-start | bytes 1167368 | tf_op jit(solution)/shard_map/ppermute | solution.py:38
  94.7 14.5 %collective-permute-start.22 = (s16[80,2432]{1,0:T(8,128)(2,1)S(1)}, s16[80,2432]{1,0:T(8,128)(2,1)S(1)}, u32[]{:S(2)}, u32[]{:S(2)}) collective-permute-start(s16[80,2432]{1,0:T(8,128)(2,1)S(1)} %get-tuple-element.100), channel_id=1, source_target_pairs={{0,12},{4,0},{8,4},{12,8},{1,13},{5,1},{9,5},{13,9},{2,14},{6,2},{... | collective-permute-start | bytes 1167368 | tf_op jit(solution)/shard_map/ppermute | solution.py:42
  99.0 13.6 %collective-permute-start.25 = (s16[80,1920]{1,0:T(8,128)(2,1)S(1)}, s16[80,1920]{1,0:T(8,128)(2,1)S(1)}, u32[]{:S(2)}, u32[]{:S(2)}) collective-permute-start(s16[80,1920]{1,0:T(8,128)(2,1)S(1)} %get-tuple-element.96), channel_id=1, source_target_pairs={{0,16},{16,32},{32,48},{48,0},{1,17},{17,33},{33,49},{49,1},{2,18}... | collective-permute-start | bytes 921608 | tf_op jit(solution)/shard_map/ppermute | solution.py:38
  103.3 9.3 %collective-permute-start.26 = (s16[80,1920]{1,0:T(8,128)(2,1)S(1)}, s16[80,1920]{1,0:T(8,128)(2,1)S(1)}, u32[]{:S(2)}, u32[]{:S(2)}) collective-permute-start(s16[80,1920]{1,0:T(8,128)(2,1)S(1)} %get-tuple-element.111), channel_id=1, source_target_pairs={{0,48},{16,0},{32,16},{48,32},{1,49},{17,1},{33,17},{49,33},{2,50}... | collective-permute-start | bytes 921608 | tf_op jit(solution)/shard_map/ppermute | solution.py:42
  109.8 19.2 %collective-permute-start.23 = (s16[160,2432]{1,0:T(8,128)(2,1)S(1)}, s16[160,2432]{1,0:T(8,128)(2,1)S(1)}, u32[]{:S(2)}, u32[]{:S(2)}) collective-permute-start(s16[160,2432]{1,0:T(8,128)(2,1)S(1)} %get-tuple-element.109), channel_id=1, source_target_pairs={{0,4},{4,8},{8,12},{12,0},{1,5},{5,9},{9,13},{13,1},{2,6},{6,10},{... | collective-permute-start | bytes 2334728 | tf_op jit(solution)/shard_map/ppermute | solution.py:38
  109.9 19.1 %collective-permute-start.24 = (s16[160,2432]{1,0:T(8,128)(2,1)S(1)}, s16[160,2432]{1,0:T(8,128)(2,1)S(1)}, u32[]{:S(2)}, u32[]{:S(2)}) collective-permute-start(s16[160,2432]{1,0:T(8,128)(2,1)S(1)} %get-tuple-element.110), channel_id=1, source_target_pairs={{0,12},{4,0},{8,4},{12,8},{1,13},{5,1},{9,5},{13,9},{2,14},{6,2},{... | collective-permute-start | bytes 2334728 | tf_op jit(solution)/shard_map/ppermute | solution.py:42
  113.1 15.9 %collective-permute-start.27 = (s16[160,1920]{1,0:T(8,128)(2,1)S(1)}, s16[160,1920]{1,0:T(8,128)(2,1)S(1)}, u32[]{:S(2)}, u32[]{:S(2)}) collective-permute-start(s16[160,1920]{1,0:T(8,128)(2,1)S(1)} %get-tuple-element.116), channel_id=1, source_target_pairs={{0,16},{16,32},{32,48},{48,0},{1,17},{17,33},{33,49},{49,1},{2,18}... | collective-permute-start | bytes 1843208 | tf_op jit(solution)/shard_map/ppermute | solution.py:38
  114.3 14.8 %collective-permute-start.28 = (s16[160,1920]{1,0:T(8,128)(2,1)S(1)}, s16[160,1920]{1,0:T(8,128)(2,1)S(1)}, u32[]{:S(2)}, u32[]{:S(2)}) collective-permute-start(s16[160,1920]{1,0:T(8,128)(2,1)S(1)} %get-tuple-element.117), channel_id=1, source_target_pairs={{0,48},{16,0},{32,16},{48,32},{1,49},{17,1},{33,17},{49,33},{2,50}... | collective-permute-start | bytes 1843208 | tf_op jit(solution)/shard_map/ppermute | solution.py:42
  130.6 22.4 %collective-permute-start.29 = (bf16[160,4096]{1,0:T(8,128)(2,1)S(1)}, bf16[160,4096]{1,0:T(8,128)(2,1)S(1)}, u32[]{:S(2)}, u32[]{:S(2)}) collective-permute-start(bf16[160,4096]{1,0:T(8,128)(2,1)S(1)} %finish.1), channel_id=1, source_target_pairs={{0,0},{1,64},{64,1},{65,65},{2,2},{3,66},{66,3},{67,67},{4,4},{5,6... | collective-permute-start | bytes 3932168 | tf_op jit(solution)/shard_map/ppermute | solution.py:30
  137.6 15.3 %collective-permute-start.30 = (f32[1,128]{1,0:T(1,128)S(1)}, f32[1,128]{1,0:T(1,128)S(1)}, u32[]{:S(2)}, u32[]{:S(2)}) collective-permute-start(f32[1,128]{1,0:T(1,128)S(1)} %get-tuple-element.119), channel_id=1, source_target_pairs={{0,0},{1,64},{64,1},{65,65},{2,2},{3,66},{66,3},{67,67},{4,4},{5,6... | collective-permute-start | bytes 1544 | tf_op jit(solution)/shard_map/ppermute | solution.py:30
  139.5 13.4 %collective-permute-start.31 = (f32[1,128]{1,0:T(1,128)S(1)}, f32[1,128]{1,0:T(1,128)S(1)}, u32[]{:S(2)}, u32[]{:S(2)}) collective-permute-start(f32[1,128]{1,0:T(1,128)S(1)} %get-tuple-element.119), channel_id=1, source_target_pairs={{1,0},{65,1},{0,64},{64,65},{3,2},{67,3},{2,66},{66,67},{5,4},{69,... | collective-permute-start | bytes 1544 | tf_op jit(solution)/shard_map/ppermute | solution.py:450
  (8 other events, 36.5 us)

commit v7 on v6

--- a/solution.py
+++ b/solution.py
@@ -1,3 +1,4 @@
+import functools
 import math
 
 import jax
@@ -339,22 +340,21 @@
     to_down[cut:, :] = late_bwd[...]
 
 
-def finish_kernel(mult, e, oz, uz, dz, ox, ux, dx, grad):
-    cut, half = e.shape[0] // 2, oz.shape[1]
-    for h in (0, 1):
-        r = slice(h * cut, (h + 1) * cut)
-        terms = []
-        for own, u, d in ((oz, uz, dz), (ox, ux, dx)):
-            step, straight = (u, d) if h == 0 else (d, u)
-            terms.append(own[r, :] + unpack(step, 0, cut) + unpack(straight, cut, cut))
-        g0, g1 = mult[0] * terms[0], mult[0] * terms[1]
-        e0, e1 = e[r, :half].astype(F32), e[r, half:].astype(F32)
-        square = jnp.sum(e0 * e0, axis=1, keepdims=True) + jnp.sum(e1 * e1, axis=1, keepdims=True)
-        factor = lax.rsqrt(square + 1e-06)
-        inner = jnp.sum(e0 * g0, axis=1, keepdims=True) + jnp.sum(e1 * g1, axis=1, keepdims=True)
-        scale = factor * factor * factor * inner
-        grad[r, :half] = (factor * g0 - scale * e0).astype(BF16)
-        grad[r, half:] = (factor * g1 - scale * e1).astype(BF16)
+def finish_kernel(h, mult, e, oz, uz, dz, ox, ux, dx, grad):
+    cut, half = grad.shape[0], oz.shape[1]
+    r = slice(h * cut, (h + 1) * cut)
+    terms = []
+    for own, u, d in ((oz, uz, dz), (ox, ux, dx)):
+        step, straight = (u, d) if h == 0 else (d, u)
+        terms.append(own[r, :] + unpack(step, 0, cut) + unpack(straight, cut, cut))
+    g0, g1 = mult[0] * terms[0], mult[0] * terms[1]
+    e0, e1 = e[r, :half].astype(F32), e[r, half:].astype(F32)
+    square = jnp.sum(e0 * e0, axis=1, keepdims=True) + jnp.sum(e1 * e1, axis=1, keepdims=True)
+    factor = lax.rsqrt(square + 1e-06)
+    inner = jnp.sum(e0 * g0, axis=1, keepdims=True) + jnp.sum(e1 * g1, axis=1, keepdims=True)
+    scale = factor * factor * factor * inner
+    grad[:, :half] = (factor * g0 - scale * e0).astype(BF16)
+    grad[:, half:] = (factor * g1 - scale * e1).astype(BF16)
 
 
 def local(embeddings, partner, logit_scale):
@@ -441,14 +441,16 @@
     uz, dz = up(uz, "z"), down(dz, "z")
     ux, dx = call(forward_kernel, "forward_x", (fx, bx, *kept_x), (message["x"],) * 2)
     ux, dx = up(ux, "x"), down(dx, "x")
-    grad, = call(
-        finish_kernel, "finish",
-        (logit_scale, emb, oz, uz, dz, ox, ux, dx),
-        (shape(rows, width, dtype=BF16),),
-    )
-    part = after(part, grad)
+    grads = [
+        call(
+            functools.partial(finish_kernel, h), "finish",
+            (logit_scale, emb, oz, uz, dz, ox, ux, dx), (shape(cut, width, dtype=BF16),),
+        )[0]
+        for h in (0, 1)
+    ]
+    part = after(part, *grads)
     both = swap(part) + lax.ppermute(part, ("yl", "c"), SWAP_OTHER)
-    return swap(grad), (both[0, :1] / total)
+    return jnp.concatenate([swap(g) for g in grads], 0), (both[0, :1] / total)
 
 
 def solution(mesh):

time: 155 us -> 155 us (level)
  waiting for transfers between devices: 69.7 us -> 65.6 us
  starting transfers between devices: 51.1 us -> 54.5 us
    ppermute x4 -> x5, waiting for transfers between devices: 27.1 us -> 22.6 us  [swap(): return lax.ppermute(v, ('yl', 'c'), SWAP)]
    ppermute x4 -> x5, starting transfers between devices: 15.4 us -> 19.1 us  [swap(): return lax.ppermute(v, ('yl', 'c'), SWAP)]
    pallas_call x16 -> x17, Pallas kernels: 30.2 us -> 30.2 us  [call(): pl.pallas_call(kernel, name=name, out_shape=tuple((jax.ShapeDtypeStruct(o...]
  transfers between devices with their start and end apart: 32 -> 33, of which waited for: 10 -> 10; matrix products, arithmetic and copies ran while one was open for 0% -> 0% of each run, Pallas kernels for 18% -> 18%
where the time goes in v7:
time: 155 us
  waiting for transfers between devices  65.6 us (42%)
  starting transfers between devices  54.5 us (35%)
  Pallas kernels  30.2 us (19%)
  between operations  2.76 us (2%)
    ppermute x8, waiting for transfers between devices, up(): return lax.ppermute(v, axis, ring(4, 1))  35.3 us
    pallas_call x17, Pallas kernels, call(): pl.pallas_call(kernel, name=name, out_shape=tuple((jax.ShapeDtypeStruct(o...  30.2 us
    ppermute x5, waiting for transfers between devices, swap(): return lax.ppermute(v, ('yl', 'c'), SWAP)  22.6 us
    ppermute x5, starting transfers between devices, swap(): return lax.ppermute(v, ('yl', 'c'), SWAP)  19.1 us
    ppermute x8, starting transfers between devices, down(): return lax.ppermute(v, axis, ring(4, -1))  17.6 us
    ppermute x6, waiting for transfers between devices, gather_small(): return [v] + [lax.ppermute(v, axis, ring(4, -k)) for k in ORDER[1:]]  7.09 us
    ppermute x5, starting transfers between devices, other_core(): return lax.ppermute(v, 'c', ring(2, 1))  6.27 us
    ppermute x6, starting transfers between devices, gather_small(): return [v] + [lax.ppermute(v, axis, ring(4, -k)) for k in ORDER[1:]]  5.76 us
  transfers between devices with their start and end apart: 33, of which 10 were waited for; matrix products, arithmetic and copies ran while one was open for 0% of the time, Pallas kernels for 18%

profile of v7, /device:TPU:1, one launch (start us, length us, event | category | flops | bytes accessed | tf_op | source)
XLA Modules:
  0.0 154.5 jit_solution(11845317018174088004)
XLA Ops:
  0.6 4.6 %collective-permute-start = (bf16[160,4096]{1,0:T(8,128)(2,1)}, bf16[160,4096]{1,0:T(8,128)(2,1)S(1)}, u32[]{:S(2)}, u32[]{:S(2)}) collective-permute-start(bf16[160,4096]{1,0:T(8,128)(2,1)} %param.3), channel_id=1, source_target_pairs={{0,0},{1,64},{64,1},{65,65},{2,2},{3,66},{66,3},{67,67},{4,4},{5,6... | collective-permute-start | bytes 3932168 | tf_op jit(solution)/shard_map/ppermute | solution.py:31
  5.2 1.9 %collective-permute-start.1 = (s32[1,160]{1,0:T(1,128)}, s32[1,160]{1,0:T(1,128)S(1)}, u32[]{:S(2)}, u32[]{:S(2)}) collective-permute-start(s32[1,160]{1,0:T(1,128)} %bitcast.5), channel_id=1, source_target_pairs={{0,0},{1,64},{64,1},{65,65},{2,2},{3,66},{66,3},{67,67},{4,4},{5,6... | collective-permute-start | bytes 1928 | tf_op jit(solution)/shard_map/ppermute | solution.py:31
  7.2 13.8 %collective-permute-done.1 = s32[1,160]{1,0:T(1,128)S(1)} collective-permute-done((s32[1,160]{1,0:T(1,128)}, s32[1,160]{1,0:T(1,128)S(1)}, u32[]{:S(2)}, u32[]{:S(2)}) %collective-permute-start.1) | collective-permute-done | bytes 672 | tf_op jit(solution)/shard_map/ppermute | solution.py:31
  23.7 2.2 %collective-permute-start.3 = (bf16[160,4224]{1,0:T(8,128)(2,1)S(1)}, bf16[160,4224]{1,0:T(8,128)(2,1)S(1)}, u32[]{:S(2)}, u32[]{:S(2)}) collective-permute-start(bf16[160,4224]{1,0:T(8,128)(2,1)S(1)} %get-tuple-element.61.v), channel_id=1, source_target_pairs={{0,12},{4,0},{8,4},{12,8},{1,13},{5,1},{9,5},{13,9},{2,14},{6,2},{... | collective-permute-start | bytes 4055048 | tf_op jit(solution)/shard_map/ppermute | solution.py:43
  28.5 15.0 %collective-permute-done.4.xu.refs_2_ = bf16[160,4096]{1,0:T(8,128)(2,1)S(1)} collective-permute-done((bf16[160,4096]{1,0:T(8,128)(2,1)S(1)}, bf16[160,4096]{1,0:T(8,128)(2,1)S(1)}, u32[]{:S(2)}, u32[]{:S(2)}) %collective-permute-start.4) | collective-permute-done | bytes 1310752 | tf_op jit(solution)/shard_map/ppermute | solution.py:39
  44.2 2.7 %collective-permute-start.9 = (bf16[80,4224]{1,0:T(8,128)(2,1)S(1)}, bf16[80,4224]{1,0:T(8,128)(2,1)S(1)}, u32[]{:S(2)}, u32[]{:S(2)}) collective-permute-start(bf16[80,4224]{1,0:T(8,128)(2,1)S(1)} %get-tuple-element.70), channel_id=1, source_target_pairs={{0,12},{4,0},{8,4},{12,8},{1,13},{5,1},{9,5},{13,9},{2,14},{6,2},{... | collective-permute-start | bytes 2027528 | tf_op jit(solution)/shard_map/ppermute | solution.py:43
  50.7 5.3 %near.1 = (f32[480,480]{1,0:T(8,128)S(1)}, f32[480,480]{1,0:T(8,128)S(1)}, f32[8,480]{1,0:T(8,128)S(1)}, f32[8,480]{1,0:T(8,128)S(1)}) custom-call(f32[1]{0:T(128)S(6)} %copy.9.mult, bf16[160,4224]{1,0:T(8,128)(2,1)S(1)} %get-tuple-element.61.v, bf16[160,4224]{1,0:T(8,128)(2,1)S(1)} %collective-permute-done.3.zd, ...), custom_call_target="tpu_custom_call" | custom-call | flops 3774873600 | bytes 13798404 | tf_op jit(solution)/shard_map/near/pallas_call | solution.py:66
  55.9 7.3 %collective-permute-done.6.refs_0_ = bf16[80,4096]{1,0:T(8,128)(2,1)S(1)} collective-permute-done((bf16[80,4096]{1,0:T(8,128)(2,1)S(1)}, bf16[80,4096]{1,0:T(8,128)(2,1)S(1)}, u32[]{:S(2)}, u32[]{:S(2)}) %collective-permute-start.6) | collective-permute-done | bytes 655392 | tf_op jit(solution)/shard_map/ppermute | solution.py:39
  63.3 2.2 %collective-permute-start.11 = (bf16[160,4096]{1,0:T(8,128)(2,1)S(1)}, bf16[160,4096]{1,0:T(8,128)(2,1)S(1)}, u32[]{:S(2)}, u32[]{:S(2)}) collective-permute-start(bf16[160,4096]{1,0:T(8,128)(2,1)S(1)} %stack_t.1.t), channel_id=1, source_target_pairs={{0,1},{1,0},{2,3},{3,2},{4,5},{5,4},{6,7},{7,6},{8,9},{9,8},{10,11... | collective-permute-start | bytes 3932168 | tf_op jit(solution)/shard_map/ppermute | solution.py:35
  65.6 4.3 %early.1 = (bf16[640,4096]{1,0:T(8,128)(2,1)S(1)}, bf16[640,1792]{1,0:T(8,128)(2,1)S(1)}, f32[640,128]{1,0:T(8,128)S(1)}, f32[640,640]{1,0:T(8,128)S(1)}, f32[8,640]{1,0:T(8,128)S(1)}, /*index=5*/f32[8,640]{1,0:T(8,128)S(1)}) custom-call(f32[1]{0:T(128)S(6)} %copy.9.mult, bf16[160,4224]{1,0:T(8,128)(2,1)S(1)} %get-tuple-element.61.v, ...), custom_call_target="tpu_custom_call" | custom-call | flops 3355443200 | bytes 21135364 | tf_op jit(solution)/shard_map/early/pallas_call | solution.py:66
  69.9 4.3 %tail.1 = (f32[640,640]{1,0:T(8,128)S(1)}, f32[8,640]{1,0:T(8,128)S(1)}, f32[8,1280]{1,0:T(8,128)S(1)}) custom-call(f32[1]{0:T(128)S(6)} %copy.9.mult, bf16[640,4096]{1,0:T(8,128)(2,1)S(1)} %get-tuple-element.81.a, bf16[480,4096]{1,0:T(8,128)(2,1)S(1)} %collective-permute-done.10.bo.b, bf16[160,4096]{1,0:T(8,128)(2,1)S(1)} %collective-permute-done.11.t.to, ...), custom_call_target="tpu_custom_call" | custom-call | flops 3355443200 | bytes 13496324 | tf_op jit(solution)/shard_map/tail/pallas_call | solution.py:66
  80.6 2.7 %collective-permute-start.16 = (f32[8,1280]{1,0:T(8,128)S(1)}, f32[8,1280]{1,0:T(8,128)S(1)}, u32[]{:S(2)}, u32[]{:S(2)}) collective-permute-start(f32[8,1280]{1,0:T(8,128)S(1)} %get-tuple-element.91.c0), channel_id=1, source_target_pairs={{0,48},{16,0},{32,16},{48,32},{1,49},{17,1},{33,17},{49,33},{2,50}... | collective-permute-start | bytes 122888 | tf_op jit(solution)/shard_map/ppermute | solution.py:51
  84.8 3.1 %collective-permute-done.17.c2 = f32[8,1280]{1,0:T(8,128)S(1)} collective-permute-done((f32[8,1280]{1,0:T(8,128)S(1)}, f32[8,1280]{1,0:T(8,128)S(1)}, u32[]{:S(2)}, u32[]{:S(2)}) %collective-permute-start.17) | collective-permute-done | bytes 40992 | tf_op jit(solution)/shard_map/ppermute | solution.py:51
  89.6 3.3 %collective-permute-start.19 = (bf16[640,640]{1,0:T(8,128)(2,1)S(1)}, bf16[640,640]{1,0:T(8,128)(2,1)S(1)}, u32[]{:S(2)}, u32[]{:S(2)}) collective-permute-start(bf16[640,640]{1,0:T(8,128)(2,1)S(1)} %get-tuple-element.93.far), channel_id=1, source_target_pairs={{0,1},{1,0},{2,3},{3,2},{4,5},{5,4},{6,7},{7,6},{8,9},{9,8},{10,11... | collective-permute-start | bytes 2457608 | tf_op jit(solution)/shard_map/ppermute | solution.py:35
  94.7 2.7 %collective-permute-start.22 = (s16[80,2432]{1,0:T(8,128)(2,1)S(1)}, s16[80,2432]{1,0:T(8,128)(2,1)S(1)}, u32[]{:S(2)}, u32[]{:S(2)}) collective-permute-start(s16[80,2432]{1,0:T(8,128)(2,1)S(1)} %get-tuple-element.100), channel_id=1, source_target_pairs={{0,12},{4,0},{8,4},{12,8},{1,13},{5,1},{9,5},{13,9},{2,14},{6,2},{... | collective-permute-start | bytes 1167368 | tf_op jit(solution)/shard_map/ppermute | solution.py:43
  99.2 4.1 %rest_z.1 = (s16[80,2432]{1,0:T(8,128)(2,1)S(1)}, s16[80,2432]{1,0:T(8,128)(2,1)S(1)}, f32[80,2304]{1,0:T(8,128)S(1)}, f32[80,2304]{1,0:T(8,128)S(1)}, f32[160,2304]{1,0:T(8,128)S(1)}) custom-call(bf16[640,640]{1,0:T(8,128)(2,1)S(1)} %get-tuple-element.101.near, bf16[640,640]{1,0:T(8,128)(2,1)S(1)} %get-tuple-element.93.far, ...), custom_call_target="tpu_custom_call" | custom-call | flops 2831155200 | bytes 15851520 | tf_op jit(solution)/shard_map/rest_z/pallas_call | solution.py:66
  103.3 2.8 %collective-permute-start.26 = (s16[80,1920]{1,0:T(8,128)(2,1)S(1)}, s16[80,1920]{1,0:T(8,128)(2,1)S(1)}, u32[]{:S(2)}, u32[]{:S(2)}) collective-permute-start(s16[80,1920]{1,0:T(8,128)(2,1)S(1)} %get-tuple-element.111), channel_id=1, source_target_pairs={{0,48},{16,0},{32,16},{48,32},{1,49},{17,1},{33,17},{49,33},{2,50}... | collective-permute-start | bytes 921608 | tf_op jit(solution)/shard_map/ppermute | solution.py:43
  106.0 3.2 %rest_x.1 = (s16[80,1920]{1,0:T(8,128)(2,1)S(1)}, s16[80,1920]{1,0:T(8,128)(2,1)S(1)}, f32[80,1792]{1,0:T(8,128)S(1)}, f32[80,1792]{1,0:T(8,128)S(1)}, f32[160,1792]{1,0:T(8,128)S(1)}) custom-call(bf16[640,640]{1,0:T(8,128)(2,1)S(1)} %get-tuple-element.101.near, bf16[640,640]{1,0:T(8,128)(2,1)S(1)} %collective-permute-done.19.far, ...), custom_call_target="tpu_custom_call" | custom-call | flops 2202009600 | bytes 12083200 | tf_op jit(solution)/shard_map/rest_x/pallas_call | solution.py:66
  109.9 2.7 %collective-permute-start.24 = (s16[160,2432]{1,0:T(8,128)(2,1)S(1)}, s16[160,2432]{1,0:T(8,128)(2,1)S(1)}, u32[]{:S(2)}, u32[]{:S(2)}) collective-permute-start(s16[160,2432]{1,0:T(8,128)(2,1)S(1)} %get-tuple-element.110), channel_id=1, source_target_pairs={{0,12},{4,0},{8,4},{12,8},{1,13},{5,1},{9,5},{13,9},{2,14},{6,2},{... | collective-permute-start | bytes 2334728 | tf_op jit(solution)/shard_map/ppermute | solution.py:43
  116.0 13.0 %collective-permute-done.23.uz = s16[160,2432]{1,0:T(8,128)(2,1)S(1)} collective-permute-done((s16[160,2432]{1,0:T(8,128)(2,1)S(1)}, s16[160,2432]{1,0:T(8,128)(2,1)S(1)}, u32[]{:S(2)}, u32[]{:S(2)}) %collective-permute-start.23) | collective-permute-done | bytes 778272 | tf_op jit(solution)/shard_map/ppermute | solution.py:39
  129.8 7.0 %collective-permute-start.30 = (bf16[80,4096]{1,0:T(8,128)(2,1)S(1)}, bf16[80,4096]{1,0:T(8,128)(2,1)S(1)}, u32[]{:S(2)}, u32[]{:S(2)}) collective-permute-start(bf16[80,4096]{1,0:T(8,128)(2,1)S(1)} %finish.3), channel_id=1, source_target_pairs={{0,0},{1,64},{64,1},{65,65},{2,2},{3,66},{66,3},{67,67},{4,4},{5,6... | collective-permute-start | bytes 1966088 | tf_op jit(solution)/shard_map/ppermute | solution.py:31
  137.7 1.9 %collective-permute-start.29 = (bf16[80,4096]{1,0:T(8,128)(2,1)S(1)}, bf16[80,4096]{1,0:T(8,128)(2,1)S(1)}, u32[]{:S(2)}, u32[]{:S(2)}) collective-permute-start(bf16[80,4096]{1,0:T(8,128)(2,1)S(1)} %finish.2), channel_id=1, source_target_pairs={{0,0},{1,64},{64,1},{65,65},{2,2},{3,66},{66,3},{67,67},{4,4},{5,6... | collective-permute-start | bytes 1966088 | tf_op jit(solution)/shard_map/ppermute | solution.py:31
  139.6 3.6 %collective-permute-start.31 = (f32[1,128]{1,0:T(1,128)S(1)}, f32[1,128]{1,0:T(1,128)S(1)}, u32[]{:S(2)}, u32[]{:S(2)}) collective-permute-start(f32[1,128]{1,0:T(1,128)S(1)} %get-tuple-element.119), channel_id=1, source_target_pairs={{0,0},{1,64},{64,1},{65,65},{2,2},{3,66},{66,3},{67,67},{4,4},{5,6... | collective-permute-start | bytes 1544 | tf_op jit(solution)/shard_map/ppermute | solution.py:31
  143.3 8.8 %collective-permute-done.31 = f32[1,128]{1,0:T(1,128)S(1)} collective-permute-done((f32[1,128]{1,0:T(1,128)S(1)}, f32[1,128]{1,0:T(1,128)S(1)}, u32[]{:S(2)}, u32[]{:S(2)}) %collective-permute-start.31) | collective-permute-done | bytes 544 | tf_op jit(solution)/shard_map/ppermute | solution.py:31
  (66 shorter events, 29.5 us)
Async XLA Ops:
  0.6 20.7 %collective-permute-start = (bf16[160,4096]{1,0:T(8,128)(2,1)}, bf16[160,4096]{1,0:T(8,128)(2,1)S(1)}, u32[]{:S(2)}, u32[]{:S(2)}) collective-permute-start(bf16[160,4096]{1,0:T(8,128)(2,1)} %param.3), channel_id=1, source_target_pairs={{0,0},{1,64},{64,1},{65,65},{2,2},{3,66},{66,3},{67,67},{4,4},{5,6... | collective-permute-start | bytes 3932168 | tf_op jit(solution)/shard_map/ppermute | solution.py:31
  5.2 15.8 %collective-permute-start.1 = (s32[1,160]{1,0:T(1,128)}, s32[1,160]{1,0:T(1,128)S(1)}, u32[]{:S(2)}, u32[]{:S(2)}) collective-permute-start(s32[1,160]{1,0:T(1,128)} %bitcast.5), channel_id=1, source_target_pairs={{0,0},{1,64},{64,1},{65,65},{2,2},{3,66},{66,3},{67,67},{4,4},{5,6... | collective-permute-start | bytes 1928 | tf_op jit(solution)/shard_map/ppermute | solution.py:31
  22.0 21.6 %collective-permute-start.2 = (bf16[160,4224]{1,0:T(8,128)(2,1)S(1)}, bf16[160,4224]{1,0:T(8,128)(2,1)S(1)}, u32[]{:S(2)}, u32[]{:S(2)}) collective-permute-start(bf16[160,4224]{1,0:T(8,128)(2,1)S(1)} %get-tuple-element.61.v), channel_id=1, source_target_pairs={{0,4},{4,8},{8,12},{12,0},{1,5},{5,9},{9,13},{13,1},{2,6},{6,10},{... | collective-permute-start | bytes 4055048 | tf_op jit(solution)/shard_map/ppermute | solution.py:39
  23.7 19.9 %collective-permute-start.3 = (bf16[160,4224]{1,0:T(8,128)(2,1)S(1)}, bf16[160,4224]{1,0:T(8,128)(2,1)S(1)}, u32[]{:S(2)}, u32[]{:S(2)}) collective-permute-start(bf16[160,4224]{1,0:T(8,128)(2,1)S(1)} %get-tuple-element.61.v), channel_id=1, source_target_pairs={{0,12},{4,0},{8,4},{12,8},{1,13},{5,1},{9,5},{13,9},{2,14},{6,2},{... | collective-permute-start | bytes 4055048 | tf_op jit(solution)/shard_map/ppermute | solution.py:43
  25.9 17.7 %collective-permute-start.4 = (bf16[160,4096]{1,0:T(8,128)(2,1)S(1)}, bf16[160,4096]{1,0:T(8,128)(2,1)S(1)}, u32[]{:S(2)}, u32[]{:S(2)}) collective-permute-start(bf16[160,4096]{1,0:T(8,128)(2,1)S(1)} %get-tuple-element.62.refs_0_), channel_id=1, source_target_pairs={{0,16},{16,32},{32,48},{48,0},{1,17},{17,33},{33,49},{49,1},{2,18}... | collective-permute-start | bytes 3932168 | tf_op jit(solution)/shard_map/ppermute | solution.py:39
  27.1 16.5 %collective-permute-start.5 = (bf16[160,4096]{1,0:T(8,128)(2,1)S(1)}, bf16[160,4096]{1,0:T(8,128)(2,1)S(1)}, u32[]{:S(2)}, u32[]{:S(2)}) collective-permute-start(bf16[160,4096]{1,0:T(8,128)(2,1)S(1)} %get-tuple-element.62.refs_0_), channel_id=1, source_target_pairs={{0,48},{16,0},{32,16},{48,32},{1,49},{17,1},{33,17},{49,33},{2,50}... | collective-permute-start | bytes 3932168 | tf_op jit(solution)/shard_map/ppermute | solution.py:43
  44.1 19.1 %collective-permute-start.8 = (bf16[80,4224]{1,0:T(8,128)(2,1)S(1)}, bf16[80,4224]{1,0:T(8,128)(2,1)S(1)}, u32[]{:S(2)}, u32[]{:S(2)}) collective-permute-start(bf16[80,4224]{1,0:T(8,128)(2,1)S(1)} %get-tuple-element.69), channel_id=1, source_target_pairs={{0,4},{4,8},{8,12},{12,0},{1,5},{5,9},{9,13},{13,1},{2,6},{6,10},{... | collective-permute-start | bytes 2027528 | tf_op jit(solution)/shard_map/ppermute | solution.py:39
  44.2 19.1 %collective-permute-start.9 = (bf16[80,4224]{1,0:T(8,128)(2,1)S(1)}, bf16[80,4224]{1,0:T(8,128)(2,1)S(1)}, u32[]{:S(2)}, u32[]{:S(2)}) collective-permute-start(bf16[80,4224]{1,0:T(8,128)(2,1)S(1)} %get-tuple-element.70), channel_id=1, source_target_pairs={{0,12},{4,0},{8,4},{12,8},{1,13},{5,1},{9,5},{13,9},{2,14},{6,2},{... | collective-permute-start | bytes 2027528 | tf_op jit(solution)/shard_map/ppermute | solution.py:43
  46.8 16.4 %collective-permute-start.6 = (bf16[80,4096]{1,0:T(8,128)(2,1)S(1)}, bf16[80,4096]{1,0:T(8,128)(2,1)S(1)}, u32[]{:S(2)}, u32[]{:S(2)}) collective-permute-start(bf16[80,4096]{1,0:T(8,128)(2,1)S(1)} %get-tuple-element.67), channel_id=1, source_target_pairs={{0,16},{16,32},{32,48},{48,0},{1,17},{17,33},{33,49},{49,1},{2,18}... | collective-permute-start | bytes 1966088 | tf_op jit(solution)/shard_map/ppermute | solution.py:39
  48.0 15.2 %collective-permute-start.7 = (bf16[80,4096]{1,0:T(8,128)(2,1)S(1)}, bf16[80,4096]{1,0:T(8,128)(2,1)S(1)}, u32[]{:S(2)}, u32[]{:S(2)}) collective-permute-start(bf16[80,4096]{1,0:T(8,128)(2,1)S(1)} %get-tuple-element.68), channel_id=1, source_target_pairs={{0,48},{16,0},{32,16},{48,32},{1,49},{17,1},{33,17},{49,33},{2,50}... | collective-permute-start | bytes 1966088 | tf_op jit(solution)/shard_map/ppermute | solution.py:43
  69.8 27.5 %collective-permute-start.20 = (bf16[640,1792]{1,0:T(8,128)(2,1)S(1)}, bf16[640,1792]{1,0:T(8,128)(2,1)S(1)}, u32[]{:S(2)}, u32[]{:S(2)}) collective-permute-start(bf16[640,1792]{1,0:T(8,128)(2,1)S(1)} %get-tuple-element.95), channel_id=1, source_target_pairs={{0,1},{1,0},{2,3},{3,2},{4,5},{5,4},{6,7},{7,6},{8,9},{9,8},{10,11... | collective-permute-start | bytes 6881288 | tf_op jit(solution)/shard_map/ppermute | solution.py:35
  89.6 7.8 %collective-permute-start.19 = (bf16[640,640]{1,0:T(8,128)(2,1)S(1)}, bf16[640,640]{1,0:T(8,128)(2,1)S(1)}, u32[]{:S(2)}, u32[]{:S(2)}) collective-permute-start(bf16[640,640]{1,0:T(8,128)(2,1)S(1)} %get-tuple-element.93.far), channel_id=1, source_target_pairs={{0,1},{1,0},{2,3},{3,2},{4,5},{5,4},{6,7},{7,6},{8,9},{9,8},{10,11... | collective-permute-start | bytes 2457608 | tf_op jit(solution)/shard_map/ppermute | solution.py:35
  94.6 14.5 %collective-permute-start.21 = (s16[80,2432]{1,0:T(8,128)(2,1)S(1)}, s16[80,2432]{1,0:T(8,128)(2,1)S(1)}, u32[]{:S(2)}, u32[]{:S(2)}) collective-permute-start(s16[80,2432]{1,0:T(8,128)(2,1)S(1)} %get-tuple-element.99), channel_id=1, source_target_pairs={{0,4},{4,8},{8,12},{12,0},{1,5},{5,9},{9,13},{13,1},{2,6},{6,10},{... | collective-permute-start | bytes 1167368 | tf_op jit(solution)/shard_map/ppermute | solution.py:39
  94.7 14.5 %collective-permute-start.22 = (s16[80,2432]{1,0:T(8,128)(2,1)S(1)}, s16[80,2432]{1,0:T(8,128)(2,1)S(1)}, u32[]{:S(2)}, u32[]{:S(2)}) collective-permute-start(s16[80,2432]{1,0:T(8,128)(2,1)S(1)} %get-tuple-element.100), channel_id=1, source_target_pairs={{0,12},{4,0},{8,4},{12,8},{1,13},{5,1},{9,5},{13,9},{2,14},{6,2},{... | collective-permute-start | bytes 1167368 | tf_op jit(solution)/shard_map/ppermute | solution.py:43
  99.0 13.6 %collective-permute-start.25 = (s16[80,1920]{1,0:T(8,128)(2,1)S(1)}, s16[80,1920]{1,0:T(8,128)(2,1)S(1)}, u32[]{:S(2)}, u32[]{:S(2)}) collective-permute-start(s16[80,1920]{1,0:T(8,128)(2,1)S(1)} %get-tuple-element.96), channel_id=1, source_target_pairs={{0,16},{16,32},{32,48},{48,0},{1,17},{17,33},{33,49},{49,1},{2,18}... | collective-permute-start | bytes 921608 | tf_op jit(solution)/shard_map/ppermute | solution.py:39
  103.3 9.3 %collective-permute-start.26 = (s16[80,1920]{1,0:T(8,128)(2,1)S(1)}, s16[80,1920]{1,0:T(8,128)(2,1)S(1)}, u32[]{:S(2)}, u32[]{:S(2)}) collective-permute-start(s16[80,1920]{1,0:T(8,128)(2,1)S(1)} %get-tuple-element.111), channel_id=1, source_target_pairs={{0,48},{16,0},{32,16},{48,32},{1,49},{17,1},{33,17},{49,33},{2,50}... | collective-permute-start | bytes 921608 | tf_op jit(solution)/shard_map/ppermute | solution.py:43
  109.8 19.1 %collective-permute-start.23 = (s16[160,2432]{1,0:T(8,128)(2,1)S(1)}, s16[160,2432]{1,0:T(8,128)(2,1)S(1)}, u32[]{:S(2)}, u32[]{:S(2)}) collective-permute-start(s16[160,2432]{1,0:T(8,128)(2,1)S(1)} %get-tuple-element.109), channel_id=1, source_target_pairs={{0,4},{4,8},{8,12},{12,0},{1,5},{5,9},{9,13},{13,1},{2,6},{6,10},{... | collective-permute-start | bytes 2334728 | tf_op jit(solution)/shard_map/ppermute | solution.py:39
  109.9 19.1 %collective-permute-start.24 = (s16[160,2432]{1,0:T(8,128)(2,1)S(1)}, s16[160,2432]{1,0:T(8,128)(2,1)S(1)}, u32[]{:S(2)}, u32[]{:S(2)}) collective-permute-start(s16[160,2432]{1,0:T(8,128)(2,1)S(1)} %get-tuple-element.110), channel_id=1, source_target_pairs={{0,12},{4,0},{8,4},{12,8},{1,13},{5,1},{9,5},{13,9},{2,14},{6,2},{... | collective-permute-start | bytes 2334728 | tf_op jit(solution)/shard_map/ppermute | solution.py:43
  113.1 15.9 %collective-permute-start.27 = (s16[160,1920]{1,0:T(8,128)(2,1)S(1)}, s16[160,1920]{1,0:T(8,128)(2,1)S(1)}, u32[]{:S(2)}, u32[]{:S(2)}) collective-permute-start(s16[160,1920]{1,0:T(8,128)(2,1)S(1)} %get-tuple-element.116), channel_id=1, source_target_pairs={{0,16},{16,32},{32,48},{48,0},{1,17},{17,33},{33,49},{49,1},{2,18}... | collective-permute-start | bytes 1843208 | tf_op jit(solution)/shard_map/ppermute | solution.py:39
  114.2 14.8 %collective-permute-start.28 = (s16[160,1920]{1,0:T(8,128)(2,1)S(1)}, s16[160,1920]{1,0:T(8,128)(2,1)S(1)}, u32[]{:S(2)}, u32[]{:S(2)}) collective-permute-start(s16[160,1920]{1,0:T(8,128)(2,1)S(1)} %get-tuple-element.117), channel_id=1, source_target_pairs={{0,48},{16,0},{32,16},{48,32},{1,49},{17,1},{33,17},{49,33},{2,50}... | collective-permute-start | bytes 1843208 | tf_op jit(solution)/shard_map/ppermute | solution.py:43
  129.8 22.4 %collective-permute-start.30 = (bf16[80,4096]{1,0:T(8,128)(2,1)S(1)}, bf16[80,4096]{1,0:T(8,128)(2,1)S(1)}, u32[]{:S(2)}, u32[]{:S(2)}) collective-permute-start(bf16[80,4096]{1,0:T(8,128)(2,1)S(1)} %finish.3), channel_id=1, source_target_pairs={{0,0},{1,64},{64,1},{65,65},{2,2},{3,66},{66,3},{67,67},{4,4},{5,6... | collective-permute-start | bytes 1966088 | tf_op jit(solution)/shard_map/ppermute | solution.py:31
  137.7 14.6 %collective-permute-start.29 = (bf16[80,4096]{1,0:T(8,128)(2,1)S(1)}, bf16[80,4096]{1,0:T(8,128)(2,1)S(1)}, u32[]{:S(2)}, u32[]{:S(2)}) collective-permute-start(bf16[80,4096]{1,0:T(8,128)(2,1)S(1)} %finish.2), channel_id=1, source_target_pairs={{0,0},{1,64},{64,1},{65,65},{2,2},{3,66},{66,3},{67,67},{4,4},{5,6... | collective-permute-start | bytes 1966088 | tf_op jit(solution)/shard_map/ppermute | solution.py:31
  139.6 12.6 %collective-permute-start.31 = (f32[1,128]{1,0:T(1,128)S(1)}, f32[1,128]{1,0:T(1,128)S(1)}, u32[]{:S(2)}, u32[]{:S(2)}) collective-permute-start(f32[1,128]{1,0:T(1,128)S(1)} %get-tuple-element.119), channel_id=1, source_target_pairs={{0,0},{1,64},{64,1},{65,65},{2,2},{3,66},{66,3},{67,67},{4,4},{5,6... | collective-permute-start | bytes 1544 | tf_op jit(solution)/shard_map/ppermute | solution.py:31
  143.2 8.9 %collective-permute-start.32 = (f32[1,128]{1,0:T(1,128)S(1)}, f32[1,128]{1,0:T(1,128)S(1)}, u32[]{:S(2)}, u32[]{:S(2)}) collective-permute-start(f32[1,128]{1,0:T(1,128)S(1)} %get-tuple-element.119), channel_id=1, source_target_pairs={{1,0},{65,1},{0,64},{64,65},{3,2},{67,3},{2,66},{66,67},{5,4},{69,... | collective-permute-start | bytes 1544 | tf_op jit(solution)/shard_map/ppermute | solution.py:452
  (9 other events, 43.4 us)

commit v8 on v7

--- a/solution.py
+++ b/solution.py
@@ -399,12 +399,12 @@
         ),
         flops=flops,
     )
-    last_other = other_core(after(last, to))
     far, rstat, cstat = call(
         tail_kernel, "tail", (logit_scale, a, bo, to, tile2, known2, mates, cols, rstat, cstat),
         (shape(side, side), shape(8, side), shape(8, 2 * side)),
         flops=flops,
     )
+    last_other = other_core(after(last, cstat))
     cstat_other = other_core(cstat)
     rstats = gather_small(rstat, "z")
     merged, lse_r = call(merge_kernel, "merge", (cstat, cstat_other, *rstats), (cstat, rstat))

time: 155 us -> 155 us (level)
  transfers between devices with their start and end apart: 33 -> 33, of which waited for: 10 -> 10; matrix products, arithmetic and copies ran while one was open for 0% -> 0% of each run, Pallas kernels for 18% -> 16%
where the time goes in v8:
time: 155 us; the launch traced here: 154 us
  waiting for transfers between devices  65.6 us (42%)
  starting transfers between devices  54.4 us (35%)
  Pallas kernels  30.2 us (19%)
  between operations  2.76 us (2%)
    ppermute x8, waiting for transfers between devices, up(): return lax.ppermute(v, axis, ring(4, 1))  35.3 us
    pallas_call x17, Pallas kernels, call(): pl.pallas_call(kernel, name=name, out_shape=tuple((jax.ShapeDtypeStruct(o...  30.2 us
    ppermute x5, waiting for transfers between devices, swap(): return lax.ppermute(v, ('yl', 'c'), SWAP)  22.6 us
    ppermute x5, starting transfers between devices, swap(): return lax.ppermute(v, ('yl', 'c'), SWAP)  19.1 us
    ppermute x8, starting transfers between devices, down(): return lax.ppermute(v, axis, ring(4, -1))  17.6 us
    ppermute x6, waiting for transfers between devices, gather_small(): return [v] + [lax.ppermute(v, axis, ring(4, -k)) for k in ORDER[1:]]  7.08 us
    ppermute x5, starting transfers between devices, other_core(): return lax.ppermute(v, 'c', ring(2, 1))  6.2 us
    ppermute x6, starting transfers between devices, gather_small(): return [v] + [lax.ppermute(v, axis, ring(4, -k)) for k in ORDER[1:]]  5.76 us
  transfers between devices with their start and end apart: 33, of which 10 were waited for; matrix products, arithmetic and copies ran while one was open for 0% of the time, Pallas kernels for 16%

profile of v8, /device:TPU:1, one launch (start us, length us, event | category | flops | bytes accessed | tf_op | source)
XLA Modules:
  0.0 154.5 jit_solution(5069956144585834612)
XLA Ops:
  0.6 4.6 %collective-permute-start = (bf16[160,4096]{1,0:T(8,128)(2,1)}, bf16[160,4096]{1,0:T(8,128)(2,1)S(1)}, u32[]{:S(2)}, u32[]{:S(2)}) collective-permute-start(bf16[160,4096]{1,0:T(8,128)(2,1)} %param.3), channel_id=1, source_target_pairs={{0,0},{1,64},{64,1},{65,65},{2,2},{3,66},{66,3},{67,67},{4,4},{5,6... | collective-permute-start | bytes 3932168 | tf_op jit(solution)/shard_map/ppermute | solution.py:31
  5.2 1.9 %collective-permute-start.1 = (s32[1,160]{1,0:T(1,128)}, s32[1,160]{1,0:T(1,128)S(1)}, u32[]{:S(2)}, u32[]{:S(2)}) collective-permute-start(s32[1,160]{1,0:T(1,128)} %bitcast.5), channel_id=1, source_target_pairs={{0,0},{1,64},{64,1},{65,65},{2,2},{3,66},{66,3},{67,67},{4,4},{5,6... | collective-permute-start | bytes 1928 | tf_op jit(solution)/shard_map/ppermute | solution.py:31
  7.2 13.8 %collective-permute-done.1 = s32[1,160]{1,0:T(1,128)S(1)} collective-permute-done((s32[1,160]{1,0:T(1,128)}, s32[1,160]{1,0:T(1,128)S(1)}, u32[]{:S(2)}, u32[]{:S(2)}) %collective-permute-start.1) | collective-permute-done | bytes 672 | tf_op jit(solution)/shard_map/ppermute | solution.py:31
  23.7 2.2 %collective-permute-start.3 = (bf16[160,4224]{1,0:T(8,128)(2,1)S(1)}, bf16[160,4224]{1,0:T(8,128)(2,1)S(1)}, u32[]{:S(2)}, u32[]{:S(2)}) collective-permute-start(bf16[160,4224]{1,0:T(8,128)(2,1)S(1)} %get-tuple-element.61.v), channel_id=1, source_target_pairs={{0,12},{4,0},{8,4},{12,8},{1,13},{5,1},{9,5},{13,9},{2,14},{6,2},{... | collective-permute-start | bytes 4055048 | tf_op jit(solution)/shard_map/ppermute | solution.py:43
  28.5 15.0 %collective-permute-done.4.xu.refs_2_ = bf16[160,4096]{1,0:T(8,128)(2,1)S(1)} collective-permute-done((bf16[160,4096]{1,0:T(8,128)(2,1)S(1)}, bf16[160,4096]{1,0:T(8,128)(2,1)S(1)}, u32[]{:S(2)}, u32[]{:S(2)}) %collective-permute-start.4) | collective-permute-done | bytes 1310752 | tf_op jit(solution)/shard_map/ppermute | solution.py:39
  44.2 2.7 %collective-permute-start.9 = (bf16[80,4224]{1,0:T(8,128)(2,1)S(1)}, bf16[80,4224]{1,0:T(8,128)(2,1)S(1)}, u32[]{:S(2)}, u32[]{:S(2)}) collective-permute-start(bf16[80,4224]{1,0:T(8,128)(2,1)S(1)} %get-tuple-element.70), channel_id=1, source_target_pairs={{0,12},{4,0},{8,4},{12,8},{1,13},{5,1},{9,5},{13,9},{2,14},{6,2},{... | collective-permute-start | bytes 2027528 | tf_op jit(solution)/shard_map/ppermute | solution.py:43
  50.7 5.3 %near.1 = (f32[480,480]{1,0:T(8,128)S(1)}, f32[480,480]{1,0:T(8,128)S(1)}, f32[8,480]{1,0:T(8,128)S(1)}, f32[8,480]{1,0:T(8,128)S(1)}) custom-call(f32[1]{0:T(128)S(6)} %copy.9.mult, bf16[160,4224]{1,0:T(8,128)(2,1)S(1)} %get-tuple-element.61.v, bf16[160,4224]{1,0:T(8,128)(2,1)S(1)} %collective-permute-done.3.zd, ...), custom_call_target="tpu_custom_call" | custom-call | flops 3774873600 | bytes 13798404 | tf_op jit(solution)/shard_map/near/pallas_call | solution.py:66
  55.9 7.3 %collective-permute-done.6.refs_0_ = bf16[80,4096]{1,0:T(8,128)(2,1)S(1)} collective-permute-done((bf16[80,4096]{1,0:T(8,128)(2,1)S(1)}, bf16[80,4096]{1,0:T(8,128)(2,1)S(1)}, u32[]{:S(2)}, u32[]{:S(2)}) %collective-permute-start.6) | collective-permute-done | bytes 655392 | tf_op jit(solution)/shard_map/ppermute | solution.py:39
  63.3 2.2 %collective-permute-start.11 = (bf16[160,4096]{1,0:T(8,128)(2,1)S(1)}, bf16[160,4096]{1,0:T(8,128)(2,1)S(1)}, u32[]{:S(2)}, u32[]{:S(2)}) collective-permute-start(bf16[160,4096]{1,0:T(8,128)(2,1)S(1)} %stack_t.1.t), channel_id=1, source_target_pairs={{0,1},{1,0},{2,3},{3,2},{4,5},{5,4},{6,7},{7,6},{8,9},{9,8},{10,11... | collective-permute-start | bytes 3932168 | tf_op jit(solution)/shard_map/ppermute | solution.py:35
  65.6 4.3 %early.1 = (bf16[640,4096]{1,0:T(8,128)(2,1)S(1)}, bf16[640,1792]{1,0:T(8,128)(2,1)S(1)}, f32[640,128]{1,0:T(8,128)S(1)}, f32[640,640]{1,0:T(8,128)S(1)}, f32[8,640]{1,0:T(8,128)S(1)}, /*index=5*/f32[8,640]{1,0:T(8,128)S(1)}) custom-call(f32[1]{0:T(128)S(6)} %copy.9.mult, bf16[160,4224]{1,0:T(8,128)(2,1)S(1)} %get-tuple-element.61.v, ...), custom_call_target="tpu_custom_call" | custom-call | flops 3355443200 | bytes 21135364 | tf_op jit(solution)/shard_map/early/pallas_call | solution.py:66
  69.8 4.3 %tail.1 = (f32[640,640]{1,0:T(8,128)S(1)}, f32[8,640]{1,0:T(8,128)S(1)}, f32[8,1280]{1,0:T(8,128)S(1)}) custom-call(f32[1]{0:T(128)S(6)} %copy.9.mult, bf16[640,4096]{1,0:T(8,128)(2,1)S(1)} %get-tuple-element.81.a, bf16[480,4096]{1,0:T(8,128)(2,1)S(1)} %collective-permute-done.10.bo.b, bf16[160,4096]{1,0:T(8,128)(2,1)S(1)} %collective-permute-done.11.t.to, ...), custom_call_target="tpu_custom_call" | custom-call | flops 3355443200 | bytes 13496324 | tf_op jit(solution)/shard_map/tail/pallas_call | solution.py:66
  80.6 2.7 %collective-permute-start.16 = (f32[8,1280]{1,0:T(8,128)S(1)}, f32[8,1280]{1,0:T(8,128)S(1)}, u32[]{:S(2)}, u32[]{:S(2)}) collective-permute-start(f32[8,1280]{1,0:T(8,128)S(1)} %get-tuple-element.91.c0), channel_id=1, source_target_pairs={{0,48},{16,0},{32,16},{48,32},{1,49},{17,1},{33,17},{49,33},{2,50}... | collective-permute-start | bytes 122888 | tf_op jit(solution)/shard_map/ppermute | solution.py:51
  84.7 3.1 %collective-permute-done.17.c2 = f32[8,1280]{1,0:T(8,128)S(1)} collective-permute-done((f32[8,1280]{1,0:T(8,128)S(1)}, f32[8,1280]{1,0:T(8,128)S(1)}, u32[]{:S(2)}, u32[]{:S(2)}) %collective-permute-start.17) | collective-permute-done | bytes 40992 | tf_op jit(solution)/shard_map/ppermute | solution.py:51
  89.5 3.3 %collective-permute-start.19 = (bf16[640,640]{1,0:T(8,128)(2,1)S(1)}, bf16[640,640]{1,0:T(8,128)(2,1)S(1)}, u32[]{:S(2)}, u32[]{:S(2)}) collective-permute-start(bf16[640,640]{1,0:T(8,128)(2,1)S(1)} %get-tuple-element.93.far), channel_id=1, source_target_pairs={{0,1},{1,0},{2,3},{3,2},{4,5},{5,4},{6,7},{7,6},{8,9},{9,8},{10,11... | collective-permute-start | bytes 2457608 | tf_op jit(solution)/shard_map/ppermute | solution.py:35
  94.7 2.7 %collective-permute-start.22 = (s16[80,2432]{1,0:T(8,128)(2,1)S(1)}, s16[80,2432]{1,0:T(8,128)(2,1)S(1)}, u32[]{:S(2)}, u32[]{:S(2)}) collective-permute-start(s16[80,2432]{1,0:T(8,128)(2,1)S(1)} %get-tuple-element.100), channel_id=1, source_target_pairs={{0,12},{4,0},{8,4},{12,8},{1,13},{5,1},{9,5},{13,9},{2,14},{6,2},{... | collective-permute-start | bytes 1167368 | tf_op jit(solution)/shard_map/ppermute | solution.py:43
  99.1 4.1 %rest_z.1 = (s16[80,2432]{1,0:T(8,128)(2,1)S(1)}, s16[80,2432]{1,0:T(8,128)(2,1)S(1)}, f32[80,2304]{1,0:T(8,128)S(1)}, f32[80,2304]{1,0:T(8,128)S(1)}, f32[160,2304]{1,0:T(8,128)S(1)}) custom-call(bf16[640,640]{1,0:T(8,128)(2,1)S(1)} %get-tuple-element.101.near, bf16[640,640]{1,0:T(8,128)(2,1)S(1)} %get-tuple-element.93.far, ...), custom_call_target="tpu_custom_call" | custom-call | flops 2831155200 | bytes 15851520 | tf_op jit(solution)/shard_map/rest_z/pallas_call | solution.py:66
  103.2 2.8 %collective-permute-start.26 = (s16[80,1920]{1,0:T(8,128)(2,1)S(1)}, s16[80,1920]{1,0:T(8,128)(2,1)S(1)}, u32[]{:S(2)}, u32[]{:S(2)}) collective-permute-start(s16[80,1920]{1,0:T(8,128)(2,1)S(1)} %get-tuple-element.111), channel_id=1, source_target_pairs={{0,48},{16,0},{32,16},{48,32},{1,49},{17,1},{33,17},{49,33},{2,50}... | collective-permute-start | bytes 921608 | tf_op jit(solution)/shard_map/ppermute | solution.py:43
  105.9 3.2 %rest_x.1 = (s16[80,1920]{1,0:T(8,128)(2,1)S(1)}, s16[80,1920]{1,0:T(8,128)(2,1)S(1)}, f32[80,1792]{1,0:T(8,128)S(1)}, f32[80,1792]{1,0:T(8,128)S(1)}, f32[160,1792]{1,0:T(8,128)S(1)}) custom-call(bf16[640,640]{1,0:T(8,128)(2,1)S(1)} %get-tuple-element.101.near, bf16[640,640]{1,0:T(8,128)(2,1)S(1)} %collective-permute-done.19.far, ...), custom_call_target="tpu_custom_call" | custom-call | flops 2202009600 | bytes 12083200 | tf_op jit(solution)/shard_map/rest_x/pallas_call | solution.py:66
  109.9 2.7 %collective-permute-start.24 = (s16[160,2432]{1,0:T(8,128)(2,1)S(1)}, s16[160,2432]{1,0:T(8,128)(2,1)S(1)}, u32[]{:S(2)}, u32[]{:S(2)}) collective-permute-start(s16[160,2432]{1,0:T(8,128)(2,1)S(1)} %get-tuple-element.110), channel_id=1, source_target_pairs={{0,12},{4,0},{8,4},{12,8},{1,13},{5,1},{9,5},{13,9},{2,14},{6,2},{... | collective-permute-start | bytes 2334728 | tf_op jit(solution)/shard_map/ppermute | solution.py:43
  115.9 13.0 %collective-permute-done.23.uz = s16[160,2432]{1,0:T(8,128)(2,1)S(1)} collective-permute-done((s16[160,2432]{1,0:T(8,128)(2,1)S(1)}, s16[160,2432]{1,0:T(8,128)(2,1)S(1)}, u32[]{:S(2)}, u32[]{:S(2)}) %collective-permute-start.23) | collective-permute-done | bytes 778272 | tf_op jit(solution)/shard_map/ppermute | solution.py:39
  129.8 7.0 %collective-permute-start.30 = (bf16[80,4096]{1,0:T(8,128)(2,1)S(1)}, bf16[80,4096]{1,0:T(8,128)(2,1)S(1)}, u32[]{:S(2)}, u32[]{:S(2)}) collective-permute-start(bf16[80,4096]{1,0:T(8,128)(2,1)S(1)} %finish.3), channel_id=1, source_target_pairs={{0,0},{1,64},{64,1},{65,65},{2,2},{3,66},{66,3},{67,67},{4,4},{5,6... | collective-permute-start | bytes 1966088 | tf_op jit(solution)/shard_map/ppermute | solution.py:31
  137.6 1.9 %collective-permute-start.29 = (bf16[80,4096]{1,0:T(8,128)(2,1)S(1)}, bf16[80,4096]{1,0:T(8,128)(2,1)S(1)}, u32[]{:S(2)}, u32[]{:S(2)}) collective-permute-start(bf16[80,4096]{1,0:T(8,128)(2,1)S(1)} %finish.2), channel_id=1, source_target_pairs={{0,0},{1,64},{64,1},{65,65},{2,2},{3,66},{66,3},{67,67},{4,4},{5,6... | collective-permute-start | bytes 1966088 | tf_op jit(solution)/shard_map/ppermute | solution.py:31
  139.5 3.6 %collective-permute-start.31 = (f32[1,128]{1,0:T(1,128)S(1)}, f32[1,128]{1,0:T(1,128)S(1)}, u32[]{:S(2)}, u32[]{:S(2)}) collective-permute-start(f32[1,128]{1,0:T(1,128)S(1)} %get-tuple-element.119), channel_id=1, source_target_pairs={{0,0},{1,64},{64,1},{65,65},{2,2},{3,66},{66,3},{67,67},{4,4},{5,6... | collective-permute-start | bytes 1544 | tf_op jit(solution)/shard_map/ppermute | solution.py:31
  143.3 8.8 %collective-permute-done.31 = f32[1,128]{1,0:T(1,128)S(1)} collective-permute-done((f32[1,128]{1,0:T(1,128)S(1)}, f32[1,128]{1,0:T(1,128)S(1)}, u32[]{:S(2)}, u32[]{:S(2)}) %collective-permute-start.31) | collective-permute-done | bytes 544 | tf_op jit(solution)/shard_map/ppermute | solution.py:31
  (66 shorter events, 29.5 us)
Async XLA Ops:
  0.6 20.7 %collective-permute-start = (bf16[160,4096]{1,0:T(8,128)(2,1)}, bf16[160,4096]{1,0:T(8,128)(2,1)S(1)}, u32[]{:S(2)}, u32[]{:S(2)}) collective-permute-start(bf16[160,4096]{1,0:T(8,128)(2,1)} %param.3), channel_id=1, source_target_pairs={{0,0},{1,64},{64,1},{65,65},{2,2},{3,66},{66,3},{67,67},{4,4},{5,6... | collective-permute-start | bytes 3932168 | tf_op jit(solution)/shard_map/ppermute | solution.py:31
  5.2 15.8 %collective-permute-start.1 = (s32[1,160]{1,0:T(1,128)}, s32[1,160]{1,0:T(1,128)S(1)}, u32[]{:S(2)}, u32[]{:S(2)}) collective-permute-start(s32[1,160]{1,0:T(1,128)} %bitcast.5), channel_id=1, source_target_pairs={{0,0},{1,64},{64,1},{65,65},{2,2},{3,66},{66,3},{67,67},{4,4},{5,6... | collective-permute-start | bytes 1928 | tf_op jit(solution)/shard_map/ppermute | solution.py:31
  22.0 21.6 %collective-permute-start.2 = (bf16[160,4224]{1,0:T(8,128)(2,1)S(1)}, bf16[160,4224]{1,0:T(8,128)(2,1)S(1)}, u32[]{:S(2)}, u32[]{:S(2)}) collective-permute-start(bf16[160,4224]{1,0:T(8,128)(2,1)S(1)} %get-tuple-element.61.v), channel_id=1, source_target_pairs={{0,4},{4,8},{8,12},{12,0},{1,5},{5,9},{9,13},{13,1},{2,6},{6,10},{... | collective-permute-start | bytes 4055048 | tf_op jit(solution)/shard_map/ppermute | solution.py:39
  23.7 19.9 %collective-permute-start.3 = (bf16[160,4224]{1,0:T(8,128)(2,1)S(1)}, bf16[160,4224]{1,0:T(8,128)(2,1)S(1)}, u32[]{:S(2)}, u32[]{:S(2)}) collective-permute-start(bf16[160,4224]{1,0:T(8,128)(2,1)S(1)} %get-tuple-element.61.v), channel_id=1, source_target_pairs={{0,12},{4,0},{8,4},{12,8},{1,13},{5,1},{9,5},{13,9},{2,14},{6,2},{... | collective-permute-start | bytes 4055048 | tf_op jit(solution)/shard_map/ppermute | solution.py:43
  25.9 17.7 %collective-permute-start.4 = (bf16[160,4096]{1,0:T(8,128)(2,1)S(1)}, bf16[160,4096]{1,0:T(8,128)(2,1)S(1)}, u32[]{:S(2)}, u32[]{:S(2)}) collective-permute-start(bf16[160,4096]{1,0:T(8,128)(2,1)S(1)} %get-tuple-element.62.refs_0_), channel_id=1, source_target_pairs={{0,16},{16,32},{32,48},{48,0},{1,17},{17,33},{33,49},{49,1},{2,18}... | collective-permute-start | bytes 3932168 | tf_op jit(solution)/shard_map/ppermute | solution.py:39
  27.1 16.5 %collective-permute-start.5 = (bf16[160,4096]{1,0:T(8,128)(2,1)S(1)}, bf16[160,4096]{1,0:T(8,128)(2,1)S(1)}, u32[]{:S(2)}, u32[]{:S(2)}) collective-permute-start(bf16[160,4096]{1,0:T(8,128)(2,1)S(1)} %get-tuple-element.62.refs_0_), channel_id=1, source_target_pairs={{0,48},{16,0},{32,16},{48,32},{1,49},{17,1},{33,17},{49,33},{2,50}... | collective-permute-start | bytes 3932168 | tf_op jit(solution)/shard_map/ppermute | solution.py:43
  44.1 19.1 %collective-permute-start.8 = (bf16[80,4224]{1,0:T(8,128)(2,1)S(1)}, bf16[80,4224]{1,0:T(8,128)(2,1)S(1)}, u32[]{:S(2)}, u32[]{:S(2)}) collective-permute-start(bf16[80,4224]{1,0:T(8,128)(2,1)S(1)} %get-tuple-element.69), channel_id=1, source_target_pairs={{0,4},{4,8},{8,12},{12,0},{1,5},{5,9},{9,13},{13,1},{2,6},{6,10},{... | collective-permute-start | bytes 2027528 | tf_op jit(solution)/shard_map/ppermute | solution.py:39
  44.2 19.1 %collective-permute-start.9 = (bf16[80,4224]{1,0:T(8,128)(2,1)S(1)}, bf16[80,4224]{1,0:T(8,128)(2,1)S(1)}, u32[]{:S(2)}, u32[]{:S(2)}) collective-permute-start(bf16[80,4224]{1,0:T(8,128)(2,1)S(1)} %get-tuple-element.70), channel_id=1, source_target_pairs={{0,12},{4,0},{8,4},{12,8},{1,13},{5,1},{9,5},{13,9},{2,14},{6,2},{... | collective-permute-start | bytes 2027528 | tf_op jit(solution)/shard_map/ppermute | solution.py:43
  46.8 16.4 %collective-permute-start.6 = (bf16[80,4096]{1,0:T(8,128)(2,1)S(1)}, bf16[80,4096]{1,0:T(8,128)(2,1)S(1)}, u32[]{:S(2)}, u32[]{:S(2)}) collective-permute-start(bf16[80,4096]{1,0:T(8,128)(2,1)S(1)} %get-tuple-element.67), channel_id=1, source_target_pairs={{0,16},{16,32},{32,48},{48,0},{1,17},{17,33},{33,49},{49,1},{2,18}... | collective-permute-start | bytes 1966088 | tf_op jit(solution)/shard_map/ppermute | solution.py:39
  48.0 15.2 %collective-permute-start.7 = (bf16[80,4096]{1,0:T(8,128)(2,1)S(1)}, bf16[80,4096]{1,0:T(8,128)(2,1)S(1)}, u32[]{:S(2)}, u32[]{:S(2)}) collective-permute-start(bf16[80,4096]{1,0:T(8,128)(2,1)S(1)} %get-tuple-element.68), channel_id=1, source_target_pairs={{0,48},{16,0},{32,16},{48,32},{1,49},{17,1},{33,17},{49,33},{2,50}... | collective-permute-start | bytes 1966088 | tf_op jit(solution)/shard_map/ppermute | solution.py:43
  74.1 23.2 %collective-permute-start.20 = (bf16[640,1792]{1,0:T(8,128)(2,1)S(1)}, bf16[640,1792]{1,0:T(8,128)(2,1)S(1)}, u32[]{:S(2)}, u32[]{:S(2)}) collective-permute-start(bf16[640,1792]{1,0:T(8,128)(2,1)S(1)} %get-tuple-element.95), channel_id=1, source_target_pairs={{0,1},{1,0},{2,3},{3,2},{4,5},{5,4},{6,7},{7,6},{8,9},{9,8},{10,11... | collective-permute-start | bytes 6881288 | tf_op jit(solution)/shard_map/ppermute | solution.py:35
  89.5 7.8 %collective-permute-start.19 = (bf16[640,640]{1,0:T(8,128)(2,1)S(1)}, bf16[640,640]{1,0:T(8,128)(2,1)S(1)}, u32[]{:S(2)}, u32[]{:S(2)}) collective-permute-start(bf16[640,640]{1,0:T(8,128)(2,1)S(1)} %get-tuple-element.93.far), channel_id=1, source_target_pairs={{0,1},{1,0},{2,3},{3,2},{4,5},{5,4},{6,7},{7,6},{8,9},{9,8},{10,11... | collective-permute-start | bytes 2457608 | tf_op jit(solution)/shard_map/ppermute | solution.py:35
  94.6 14.6 %collective-permute-start.21 = (s16[80,2432]{1,0:T(8,128)(2,1)S(1)}, s16[80,2432]{1,0:T(8,128)(2,1)S(1)}, u32[]{:S(2)}, u32[]{:S(2)}) collective-permute-start(s16[80,2432]{1,0:T(8,128)(2,1)S(1)} %get-tuple-element.99), channel_id=1, source_target_pairs={{0,4},{4,8},{8,12},{12,0},{1,5},{5,9},{9,13},{13,1},{2,6},{6,10},{... | collective-permute-start | bytes 1167368 | tf_op jit(solution)/shard_map/ppermute | solution.py:39
  94.7 14.5 %collective-permute-start.22 = (s16[80,2432]{1,0:T(8,128)(2,1)S(1)}, s16[80,2432]{1,0:T(8,128)(2,1)S(1)}, u32[]{:S(2)}, u32[]{:S(2)}) collective-permute-start(s16[80,2432]{1,0:T(8,128)(2,1)S(1)} %get-tuple-element.100), channel_id=1, source_target_pairs={{0,12},{4,0},{8,4},{12,8},{1,13},{5,1},{9,5},{13,9},{2,14},{6,2},{... | collective-permute-start | bytes 1167368 | tf_op jit(solution)/shard_map/ppermute | solution.py:43
  98.9 13.6 %collective-permute-start.25 = (s16[80,1920]{1,0:T(8,128)(2,1)S(1)}, s16[80,1920]{1,0:T(8,128)(2,1)S(1)}, u32[]{:S(2)}, u32[]{:S(2)}) collective-permute-start(s16[80,1920]{1,0:T(8,128)(2,1)S(1)} %get-tuple-element.96), channel_id=1, source_target_pairs={{0,16},{16,32},{32,48},{48,0},{1,17},{17,33},{33,49},{49,1},{2,18}... | collective-permute-start | bytes 921608 | tf_op jit(solution)/shard_map/ppermute | solution.py:39
  103.2 9.3 %collective-permute-start.26 = (s16[80,1920]{1,0:T(8,128)(2,1)S(1)}, s16[80,1920]{1,0:T(8,128)(2,1)S(1)}, u32[]{:S(2)}, u32[]{:S(2)}) collective-permute-start(s16[80,1920]{1,0:T(8,128)(2,1)S(1)} %get-tuple-element.111), channel_id=1, source_target_pairs={{0,48},{16,0},{32,16},{48,32},{1,49},{17,1},{33,17},{49,33},{2,50}... | collective-permute-start | bytes 921608 | tf_op jit(solution)/shard_map/ppermute | solution.py:43
  109.8 19.2 %collective-permute-start.23 = (s16[160,2432]{1,0:T(8,128)(2,1)S(1)}, s16[160,2432]{1,0:T(8,128)(2,1)S(1)}, u32[]{:S(2)}, u32[]{:S(2)}) collective-permute-start(s16[160,2432]{1,0:T(8,128)(2,1)S(1)} %get-tuple-element.109), channel_id=1, source_target_pairs={{0,4},{4,8},{8,12},{12,0},{1,5},{5,9},{9,13},{13,1},{2,6},{6,10},{... | collective-permute-start | bytes 2334728 | tf_op jit(solution)/shard_map/ppermute | solution.py:39
  109.9 19.1 %collective-permute-start.24 = (s16[160,2432]{1,0:T(8,128)(2,1)S(1)}, s16[160,2432]{1,0:T(8,128)(2,1)S(1)}, u32[]{:S(2)}, u32[]{:S(2)}) collective-permute-start(s16[160,2432]{1,0:T(8,128)(2,1)S(1)} %get-tuple-element.110), channel_id=1, source_target_pairs={{0,12},{4,0},{8,4},{12,8},{1,13},{5,1},{9,5},{13,9},{2,14},{6,2},{... | collective-permute-start | bytes 2334728 | tf_op jit(solution)/shard_map/ppermute | solution.py:43
  113.1 15.9 %collective-permute-start.27 = (s16[160,1920]{1,0:T(8,128)(2,1)S(1)}, s16[160,1920]{1,0:T(8,128)(2,1)S(1)}, u32[]{:S(2)}, u32[]{:S(2)}) collective-permute-start(s16[160,1920]{1,0:T(8,128)(2,1)S(1)} %get-tuple-element.116), channel_id=1, source_target_pairs={{0,16},{16,32},{32,48},{48,0},{1,17},{17,33},{33,49},{49,1},{2,18}... | collective-permute-start | bytes 1843208 | tf_op jit(solution)/shard_map/ppermute | solution.py:39
  114.2 14.8 %collective-permute-start.28 = (s16[160,1920]{1,0:T(8,128)(2,1)S(1)}, s16[160,1920]{1,0:T(8,128)(2,1)S(1)}, u32[]{:S(2)}, u32[]{:S(2)}) collective-permute-start(s16[160,1920]{1,0:T(8,128)(2,1)S(1)} %get-tuple-element.117), channel_id=1, source_target_pairs={{0,48},{16,0},{32,16},{48,32},{1,49},{17,1},{33,17},{49,33},{2,50}... | collective-permute-start | bytes 1843208 | tf_op jit(solution)/shard_map/ppermute | solution.py:43
  129.8 22.4 %collective-permute-start.30 = (bf16[80,4096]{1,0:T(8,128)(2,1)S(1)}, bf16[80,4096]{1,0:T(8,128)(2,1)S(1)}, u32[]{:S(2)}, u32[]{:S(2)}) collective-permute-start(bf16[80,4096]{1,0:T(8,128)(2,1)S(1)} %finish.3), channel_id=1, source_target_pairs={{0,0},{1,64},{64,1},{65,65},{2,2},{3,66},{66,3},{67,67},{4,4},{5,6... | collective-permute-start | bytes 1966088 | tf_op jit(solution)/shard_map/ppermute | solution.py:31
  137.6 14.6 %collective-permute-start.29 = (bf16[80,4096]{1,0:T(8,128)(2,1)S(1)}, bf16[80,4096]{1,0:T(8,128)(2,1)S(1)}, u32[]{:S(2)}, u32[]{:S(2)}) collective-permute-start(bf16[80,4096]{1,0:T(8,128)(2,1)S(1)} %finish.2), channel_id=1, source_target_pairs={{0,0},{1,64},{64,1},{65,65},{2,2},{3,66},{66,3},{67,67},{4,4},{5,6... | collective-permute-start | bytes 1966088 | tf_op jit(solution)/shard_map/ppermute | solution.py:31
  139.5 12.6 %collective-permute-start.31 = (f32[1,128]{1,0:T(1,128)S(1)}, f32[1,128]{1,0:T(1,128)S(1)}, u32[]{:S(2)}, u32[]{:S(2)}) collective-permute-start(f32[1,128]{1,0:T(1,128)S(1)} %get-tuple-element.119), channel_id=1, source_target_pairs={{0,0},{1,64},{64,1},{65,65},{2,2},{3,66},{66,3},{67,67},{4,4},{5,6... | collective-permute-start | bytes 1544 | tf_op jit(solution)/shard_map/ppermute | solution.py:31
  143.2 8.9 %collective-permute-start.32 = (f32[1,128]{1,0:T(1,128)S(1)}, f32[1,128]{1,0:T(1,128)S(1)}, u32[]{:S(2)}, u32[]{:S(2)}) collective-permute-start(f32[1,128]{1,0:T(1,128)S(1)} %get-tuple-element.119), channel_id=1, source_target_pairs={{1,0},{65,1},{0,64},{64,65},{3,2},{67,3},{2,66},{66,67},{5,4},{69,... | collective-permute-start | bytes 1544 | tf_op jit(solution)/shard_map/ppermute | solution.py:452
  (9 other events, 43.3 us)

commit v9 on v7

--- a/solution.py
+++ b/solution.py
@@ -450,7 +450,10 @@
     ]
     part = after(part, *grads)
     both = swap(part) + lax.ppermute(part, ("yl", "c"), SWAP_OTHER)
-    return jnp.concatenate([swap(g) for g in grads], 0), (both[0, :1] / total)
+    grad = embeddings
+    for h, g in enumerate(grads):
+        grad = lax.dynamic_update_slice(grad, swap(g), (h * cut, 0))
+    return grad, (both[0, :1] / total)
 
 
 def solution(mesh):

time: 155 us -> 156 us (level)
  local copies, waits for them, and re-layouts: 0.19 us -> 2.65 us
    unnamed x0 -> x5, local copies, waits for them, and re-layouts: none -> 2.38 us
where the time goes in v9:
time: 156 us
  waiting for transfers between devices  65.3 us (42%)
  starting transfers between devices  54.5 us (35%)
  Pallas kernels  30.2 us (19%)
  between operations  2.8 us (2%)
  local copies, waits for them, and re-layouts  2.65 us (2%)
    ppermute x8, waiting for transfers between devices, up(): return lax.ppermute(v, axis, ring(4, 1))  35.3 us
    pallas_call x17, Pallas kernels, call(): pl.pallas_call(kernel, name=name, out_shape=tuple((jax.ShapeDtypeStruct(o...  30.2 us
    ppermute x5, waiting for transfers between devices, swap(): return lax.ppermute(v, ('yl', 'c'), SWAP)  22.4 us
    ppermute x5, starting transfers between devices, swap(): return lax.ppermute(v, ('yl', 'c'), SWAP)  19.1 us
    ppermute x8, starting transfers between devices, down(): return lax.ppermute(v, axis, ring(4, -1))  17.6 us
    ppermute x6, waiting for transfers between devices, gather_small(): return [v] + [lax.ppermute(v, axis, ring(4, -k)) for k in ORDER[1:]]  7.09 us
    ppermute x5, starting transfers between devices, other_core(): return lax.ppermute(v, 'c', ring(2, 1))  6.27 us
    ppermute x6, starting transfers between devices, gather_small(): return [v] + [lax.ppermute(v, axis, ring(4, -k)) for k in ORDER[1:]]  5.76 us
  transfers between devices with their start and end apart: 33, of which 10 were waited for; matrix products, arithmetic and copies ran while one was open for 0% of the time, Pallas kernels for 18%

profile of v9, /device:TPU:1, one launch (start us, length us, event | category | flops | bytes accessed | tf_op | source)
XLA Modules:
  0.0 155.7 jit_solution(2422414107633058373)
XLA Ops:
  2.0 4.6 %collective-permute-start = (bf16[160,4096]{1,0:T(8,128)(2,1)S(1)}, bf16[160,4096]{1,0:T(8,128)(2,1)S(1)}, u32[]{:S(2)}, u32[]{:S(2)}) collective-permute-start(bf16[160,4096]{1,0:T(8,128)(2,1)S(1)} %copy.13), channel_id=1, source_target_pairs={{0,0},{1,64},{64,1},{65,65},{2,2},{3,66},{66,3},{67,67},{4,4},{5,6... | collective-permute-start | bytes 3932168 | tf_op jit(solution)/shard_map/ppermute | solution.py:31
  6.6 1.9 %collective-permute-start.1 = (s32[1,160]{1,0:T(1,128)S(1)}, s32[1,160]{1,0:T(1,128)S(1)}, u32[]{:S(2)}, u32[]{:S(2)}) collective-permute-start(s32[1,160]{1,0:T(1,128)S(1)} %bitcast.5), channel_id=1, source_target_pairs={{0,0},{1,64},{64,1},{65,65},{2,2},{3,66},{66,3},{67,67},{4,4},{5,6... | collective-permute-start | bytes 1928 | tf_op jit(solution)/shard_map/ppermute | solution.py:31
  8.6 13.6 %collective-permute-done.1 = s32[1,160]{1,0:T(1,128)S(1)} collective-permute-done((s32[1,160]{1,0:T(1,128)S(1)}, s32[1,160]{1,0:T(1,128)S(1)}, u32[]{:S(2)}, u32[]{:S(2)}) %collective-permute-start.1) | collective-permute-done | bytes 672 | tf_op jit(solution)/shard_map/ppermute | solution.py:31
  24.8 2.2 %collective-permute-start.3 = (bf16[160,4224]{1,0:T(8,128)(2,1)S(1)}, bf16[160,4224]{1,0:T(8,128)(2,1)S(1)}, u32[]{:S(2)}, u32[]{:S(2)}) collective-permute-start(bf16[160,4224]{1,0:T(8,128)(2,1)S(1)} %get-tuple-element.61.v), channel_id=1, source_target_pairs={{0,12},{4,0},{8,4},{12,8},{1,13},{5,1},{9,5},{13,9},{2,14},{6,2},{... | collective-permute-start | bytes 4055048 | tf_op jit(solution)/shard_map/ppermute | solution.py:43
  29.7 15.0 %collective-permute-done.4.xu.refs_2_ = bf16[160,4096]{1,0:T(8,128)(2,1)S(1)} collective-permute-done((bf16[160,4096]{1,0:T(8,128)(2,1)S(1)}, bf16[160,4096]{1,0:T(8,128)(2,1)S(1)}, u32[]{:S(2)}, u32[]{:S(2)}) %collective-permute-start.4) | collective-permute-done | bytes 1310752 | tf_op jit(solution)/shard_map/ppermute | solution.py:39
  45.3 2.7 %collective-permute-start.9 = (bf16[80,4224]{1,0:T(8,128)(2,1)S(1)}, bf16[80,4224]{1,0:T(8,128)(2,1)S(1)}, u32[]{:S(2)}, u32[]{:S(2)}) collective-permute-start(bf16[80,4224]{1,0:T(8,128)(2,1)S(1)} %get-tuple-element.70), channel_id=1, source_target_pairs={{0,12},{4,0},{8,4},{12,8},{1,13},{5,1},{9,5},{13,9},{2,14},{6,2},{... | collective-permute-start | bytes 2027528 | tf_op jit(solution)/shard_map/ppermute | solution.py:43
  51.8 5.3 %near.1 = (f32[480,480]{1,0:T(8,128)S(1)}, f32[480,480]{1,0:T(8,128)S(1)}, f32[8,480]{1,0:T(8,128)S(1)}, f32[8,480]{1,0:T(8,128)S(1)}) custom-call(f32[1]{0:T(128)S(6)} %copy.12.mult, bf16[160,4224]{1,0:T(8,128)(2,1)S(1)} %get-tuple-element.61.v, bf16[160,4224]{1,0:T(8,128)(2,1)S(1)} %collective-permute-done.3.zd, ...), custom_call_target="tpu_custom_call" | custom-call | flops 3774873600 | bytes 13798404 | tf_op jit(solution)/shard_map/near/pallas_call | solution.py:66
  57.0 7.3 %collective-permute-done.6.refs_0_ = bf16[80,4096]{1,0:T(8,128)(2,1)S(1)} collective-permute-done((bf16[80,4096]{1,0:T(8,128)(2,1)S(1)}, bf16[80,4096]{1,0:T(8,128)(2,1)S(1)}, u32[]{:S(2)}, u32[]{:S(2)}) %collective-permute-start.6) | collective-permute-done | bytes 655392 | tf_op jit(solution)/shard_map/ppermute | solution.py:39
  64.4 2.2 %collective-permute-start.11 = (bf16[160,4096]{1,0:T(8,128)(2,1)S(1)}, bf16[160,4096]{1,0:T(8,128)(2,1)S(1)}, u32[]{:S(2)}, u32[]{:S(2)}) collective-permute-start(bf16[160,4096]{1,0:T(8,128)(2,1)S(1)} %stack_t.1.t), channel_id=1, source_target_pairs={{0,1},{1,0},{2,3},{3,2},{4,5},{5,4},{6,7},{7,6},{8,9},{9,8},{10,11... | collective-permute-start | bytes 3932168 | tf_op jit(solution)/shard_map/ppermute | solution.py:35
  66.7 4.3 %early.1 = (bf16[640,4096]{1,0:T(8,128)(2,1)S(1)}, bf16[640,1792]{1,0:T(8,128)(2,1)S(1)}, f32[640,128]{1,0:T(8,128)S(1)}, f32[640,640]{1,0:T(8,128)S(1)}, f32[8,640]{1,0:T(8,128)S(1)}, /*index=5*/f32[8,640]{1,0:T(8,128)S(1)}) custom-call(f32[1]{0:T(128)S(6)} %copy.12.mult, bf16[160,4224]{1,0:T(8,128)(2,1)S(1)} %get-tuple-element.61.v, ...), custom_call_target="tpu_custom_call" | custom-call | flops 3355443200 | bytes 21135364 | tf_op jit(solution)/shard_map/early/pallas_call | solution.py:66
  71.1 4.3 %tail.1 = (f32[640,640]{1,0:T(8,128)S(1)}, f32[8,640]{1,0:T(8,128)S(1)}, f32[8,1280]{1,0:T(8,128)S(1)}) custom-call(f32[1]{0:T(128)S(6)} %copy.12.mult, bf16[640,4096]{1,0:T(8,128)(2,1)S(1)} %get-tuple-element.81.a, bf16[480,4096]{1,0:T(8,128)(2,1)S(1)} %collective-permute-done.10.bo.b, bf16[160,4096]{1,0:T(8,128)(2,1)S(1)} %collective-permute-done.11.t.to, ...), custom_call_target="tpu_custom_call" | custom-call | flops 3355443200 | bytes 13496324 | tf_op jit(solution)/shard_map/tail/pallas_call | solution.py:66
  81.8 2.7 %collective-permute-start.16 = (f32[8,1280]{1,0:T(8,128)S(1)}, f32[8,1280]{1,0:T(8,128)S(1)}, u32[]{:S(2)}, u32[]{:S(2)}) collective-permute-start(f32[8,1280]{1,0:T(8,128)S(1)} %get-tuple-element.91.c0), channel_id=1, source_target_pairs={{0,48},{16,0},{32,16},{48,32},{1,49},{17,1},{33,17},{49,33},{2,50}... | collective-permute-start | bytes 122888 | tf_op jit(solution)/shard_map/ppermute | solution.py:51
  85.9 3.1 %collective-permute-done.17.c2 = f32[8,1280]{1,0:T(8,128)S(1)} collective-permute-done((f32[8,1280]{1,0:T(8,128)S(1)}, f32[8,1280]{1,0:T(8,128)S(1)}, u32[]{:S(2)}, u32[]{:S(2)}) %collective-permute-start.17) | collective-permute-done | bytes 40992 | tf_op jit(solution)/shard_map/ppermute | solution.py:51
  90.7 3.3 %collective-permute-start.19 = (bf16[640,640]{1,0:T(8,128)(2,1)S(1)}, bf16[640,640]{1,0:T(8,128)(2,1)S(1)}, u32[]{:S(2)}, u32[]{:S(2)}) collective-permute-start(bf16[640,640]{1,0:T(8,128)(2,1)S(1)} %get-tuple-element.93.far), channel_id=1, source_target_pairs={{0,1},{1,0},{2,3},{3,2},{4,5},{5,4},{6,7},{7,6},{8,9},{9,8},{10,11... | collective-permute-start | bytes 2457608 | tf_op jit(solution)/shard_map/ppermute | solution.py:35
  95.8 2.7 %collective-permute-start.22 = (s16[80,2432]{1,0:T(8,128)(2,1)S(1)}, s16[80,2432]{1,0:T(8,128)(2,1)S(1)}, u32[]{:S(2)}, u32[]{:S(2)}) collective-permute-start(s16[80,2432]{1,0:T(8,128)(2,1)S(1)} %get-tuple-element.100), channel_id=1, source_target_pairs={{0,12},{4,0},{8,4},{12,8},{1,13},{5,1},{9,5},{13,9},{2,14},{6,2},{... | collective-permute-start | bytes 1167368 | tf_op jit(solution)/shard_map/ppermute | solution.py:43
  100.3 4.1 %rest_z.1 = (s16[80,2432]{1,0:T(8,128)(2,1)S(1)}, s16[80,2432]{1,0:T(8,128)(2,1)S(1)}, f32[80,2304]{1,0:T(8,128)S(1)}, f32[80,2304]{1,0:T(8,128)S(1)}, f32[160,2304]{1,0:T(8,128)S(1)}) custom-call(bf16[640,640]{1,0:T(8,128)(2,1)S(1)} %get-tuple-element.101.near, bf16[640,640]{1,0:T(8,128)(2,1)S(1)} %get-tuple-element.93.far, ...), custom_call_target="tpu_custom_call" | custom-call | flops 2831155200 | bytes 15851520 | tf_op jit(solution)/shard_map/rest_z/pallas_call | solution.py:66
  104.4 2.8 %collective-permute-start.26 = (s16[80,1920]{1,0:T(8,128)(2,1)S(1)}, s16[80,1920]{1,0:T(8,128)(2,1)S(1)}, u32[]{:S(2)}, u32[]{:S(2)}) collective-permute-start(s16[80,1920]{1,0:T(8,128)(2,1)S(1)} %get-tuple-element.111), channel_id=1, source_target_pairs={{0,48},{16,0},{32,16},{48,32},{1,49},{17,1},{33,17},{49,33},{2,50}... | collective-permute-start | bytes 921608 | tf_op jit(solution)/shard_map/ppermute | solution.py:43
  107.1 3.2 %rest_x.1 = (s16[80,1920]{1,0:T(8,128)(2,1)S(1)}, s16[80,1920]{1,0:T(8,128)(2,1)S(1)}, f32[80,1792]{1,0:T(8,128)S(1)}, f32[80,1792]{1,0:T(8,128)S(1)}, f32[160,1792]{1,0:T(8,128)S(1)}) custom-call(bf16[640,640]{1,0:T(8,128)(2,1)S(1)} %get-tuple-element.101.near, bf16[640,640]{1,0:T(8,128)(2,1)S(1)} %collective-permute-done.19.far, ...), custom_call_target="tpu_custom_call" | custom-call | flops 2202009600 | bytes 12083200 | tf_op jit(solution)/shard_map/rest_x/pallas_call | solution.py:66
  111.0 2.7 %collective-permute-start.24 = (s16[160,2432]{1,0:T(8,128)(2,1)S(1)}, s16[160,2432]{1,0:T(8,128)(2,1)S(1)}, u32[]{:S(2)}, u32[]{:S(2)}) collective-permute-start(s16[160,2432]{1,0:T(8,128)(2,1)S(1)} %get-tuple-element.110), channel_id=1, source_target_pairs={{0,12},{4,0},{8,4},{12,8},{1,13},{5,1},{9,5},{13,9},{2,14},{6,2},{... | collective-permute-start | bytes 2334728 | tf_op jit(solution)/shard_map/ppermute | solution.py:43
  117.1 13.0 %collective-permute-done.23.uz = s16[160,2432]{1,0:T(8,128)(2,1)S(1)} collective-permute-done((s16[160,2432]{1,0:T(8,128)(2,1)S(1)}, s16[160,2432]{1,0:T(8,128)(2,1)S(1)}, u32[]{:S(2)}, u32[]{:S(2)}) %collective-permute-start.23) | collective-permute-done | bytes 778272 | tf_op jit(solution)/shard_map/ppermute | solution.py:39
  130.9 7.0 %collective-permute-start.29 = (bf16[80,4096]{1,0:T(8,128)(2,1)S(1)}, bf16[80,4096]{1,0:T(8,128)(2,1)S(1)}, u32[]{:S(2)}, u32[]{:S(2)}) collective-permute-start(bf16[80,4096]{1,0:T(8,128)(2,1)S(1)} %finish.2), channel_id=1, source_target_pairs={{0,0},{1,64},{64,1},{65,65},{2,2},{3,66},{66,3},{67,67},{4,4},{5,6... | collective-permute-start | bytes 1966088 | tf_op jit(solution)/shard_map/ppermute | solution.py:31
  138.8 1.9 %collective-permute-start.30 = (bf16[80,4096]{1,0:T(8,128)(2,1)S(1)}, bf16[80,4096]{1,0:T(8,128)(2,1)S(1)}, u32[]{:S(2)}, u32[]{:S(2)}) collective-permute-start(bf16[80,4096]{1,0:T(8,128)(2,1)S(1)} %finish.3), channel_id=1, source_target_pairs={{0,0},{1,64},{64,1},{65,65},{2,2},{3,66},{66,3},{67,67},{4,4},{5,6... | collective-permute-start | bytes 1966088 | tf_op jit(solution)/shard_map/ppermute | solution.py:31
  140.7 3.6 %collective-permute-start.31 = (f32[1,128]{1,0:T(1,128)S(1)}, f32[1,128]{1,0:T(1,128)S(1)}, u32[]{:S(2)}, u32[]{:S(2)}) collective-permute-start(f32[1,128]{1,0:T(1,128)S(1)} %get-tuple-element.119), channel_id=1, source_target_pairs={{0,0},{1,64},{64,1},{65,65},{2,2},{3,66},{66,3},{67,67},{4,4},{5,6... | collective-permute-start | bytes 1544 | tf_op jit(solution)/shard_map/ppermute | solution.py:31
  144.4 8.9 %collective-permute-done.31 = f32[1,128]{1,0:T(1,128)S(1)} collective-permute-done((f32[1,128]{1,0:T(1,128)S(1)}, f32[1,128]{1,0:T(1,128)S(1)}, u32[]{:S(2)}, u32[]{:S(2)}) %collective-permute-start.31) | collective-permute-done | bytes 544 | tf_op jit(solution)/shard_map/ppermute | solution.py:31
  (72 shorter events, 30.8 us)
Async XLA Ops:
  2.0 20.5 %collective-permute-start = (bf16[160,4096]{1,0:T(8,128)(2,1)S(1)}, bf16[160,4096]{1,0:T(8,128)(2,1)S(1)}, u32[]{:S(2)}, u32[]{:S(2)}) collective-permute-start(bf16[160,4096]{1,0:T(8,128)(2,1)S(1)} %copy.13), channel_id=1, source_target_pairs={{0,0},{1,64},{64,1},{65,65},{2,2},{3,66},{66,3},{67,67},{4,4},{5,6... | collective-permute-start | bytes 3932168 | tf_op jit(solution)/shard_map/ppermute | solution.py:31
  6.6 15.6 %collective-permute-start.1 = (s32[1,160]{1,0:T(1,128)S(1)}, s32[1,160]{1,0:T(1,128)S(1)}, u32[]{:S(2)}, u32[]{:S(2)}) collective-permute-start(s32[1,160]{1,0:T(1,128)S(1)} %bitcast.5), channel_id=1, source_target_pairs={{0,0},{1,64},{64,1},{65,65},{2,2},{3,66},{66,3},{67,67},{4,4},{5,6... | collective-permute-start | bytes 1928 | tf_op jit(solution)/shard_map/ppermute | solution.py:31
  23.1 21.6 %collective-permute-start.2 = (bf16[160,4224]{1,0:T(8,128)(2,1)S(1)}, bf16[160,4224]{1,0:T(8,128)(2,1)S(1)}, u32[]{:S(2)}, u32[]{:S(2)}) collective-permute-start(bf16[160,4224]{1,0:T(8,128)(2,1)S(1)} %get-tuple-element.61.v), channel_id=1, source_target_pairs={{0,4},{4,8},{8,12},{12,0},{1,5},{5,9},{9,13},{13,1},{2,6},{6,10},{... | collective-permute-start | bytes 4055048 | tf_op jit(solution)/shard_map/ppermute | solution.py:39
  24.8 19.9 %collective-permute-start.3 = (bf16[160,4224]{1,0:T(8,128)(2,1)S(1)}, bf16[160,4224]{1,0:T(8,128)(2,1)S(1)}, u32[]{:S(2)}, u32[]{:S(2)}) collective-permute-start(bf16[160,4224]{1,0:T(8,128)(2,1)S(1)} %get-tuple-element.61.v), channel_id=1, source_target_pairs={{0,12},{4,0},{8,4},{12,8},{1,13},{5,1},{9,5},{13,9},{2,14},{6,2},{... | collective-permute-start | bytes 4055048 | tf_op jit(solution)/shard_map/ppermute | solution.py:43
  27.0 17.7 %collective-permute-start.4 = (bf16[160,4096]{1,0:T(8,128)(2,1)S(1)}, bf16[160,4096]{1,0:T(8,128)(2,1)S(1)}, u32[]{:S(2)}, u32[]{:S(2)}) collective-permute-start(bf16[160,4096]{1,0:T(8,128)(2,1)S(1)} %get-tuple-element.62.refs_0_), channel_id=1, source_target_pairs={{0,16},{16,32},{32,48},{48,0},{1,17},{17,33},{33,49},{49,1},{2,18}... | collective-permute-start | bytes 3932168 | tf_op jit(solution)/shard_map/ppermute | solution.py:39
  28.2 16.5 %collective-permute-start.5 = (bf16[160,4096]{1,0:T(8,128)(2,1)S(1)}, bf16[160,4096]{1,0:T(8,128)(2,1)S(1)}, u32[]{:S(2)}, u32[]{:S(2)}) collective-permute-start(bf16[160,4096]{1,0:T(8,128)(2,1)S(1)} %get-tuple-element.62.refs_0_), channel_id=1, source_target_pairs={{0,48},{16,0},{32,16},{48,32},{1,49},{17,1},{33,17},{49,33},{2,50}... | collective-permute-start | bytes 3932168 | tf_op jit(solution)/shard_map/ppermute | solution.py:43
  45.2 19.1 %collective-permute-start.8 = (bf16[80,4224]{1,0:T(8,128)(2,1)S(1)}, bf16[80,4224]{1,0:T(8,128)(2,1)S(1)}, u32[]{:S(2)}, u32[]{:S(2)}) collective-permute-start(bf16[80,4224]{1,0:T(8,128)(2,1)S(1)} %get-tuple-element.69), channel_id=1, source_target_pairs={{0,4},{4,8},{8,12},{12,0},{1,5},{5,9},{9,13},{13,1},{2,6},{6,10},{... | collective-permute-start | bytes 2027528 | tf_op jit(solution)/shard_map/ppermute | solution.py:39
  45.3 19.1 %collective-permute-start.9 = (bf16[80,4224]{1,0:T(8,128)(2,1)S(1)}, bf16[80,4224]{1,0:T(8,128)(2,1)S(1)}, u32[]{:S(2)}, u32[]{:S(2)}) collective-permute-start(bf16[80,4224]{1,0:T(8,128)(2,1)S(1)} %get-tuple-element.70), channel_id=1, source_target_pairs={{0,12},{4,0},{8,4},{12,8},{1,13},{5,1},{9,5},{13,9},{2,14},{6,2},{... | collective-permute-start | bytes 2027528 | tf_op jit(solution)/shard_map/ppermute | solution.py:43
  47.9 16.4 %collective-permute-start.6 = (bf16[80,4096]{1,0:T(8,128)(2,1)S(1)}, bf16[80,4096]{1,0:T(8,128)(2,1)S(1)}, u32[]{:S(2)}, u32[]{:S(2)}) collective-permute-start(bf16[80,4096]{1,0:T(8,128)(2,1)S(1)} %get-tuple-element.67), channel_id=1, source_target_pairs={{0,16},{16,32},{32,48},{48,0},{1,17},{17,33},{33,49},{49,1},{2,18}... | collective-permute-start | bytes 1966088 | tf_op jit(solution)/shard_map/ppermute | solution.py:39
  49.1 15.2 %collective-permute-start.7 = (bf16[80,4096]{1,0:T(8,128)(2,1)S(1)}, bf16[80,4096]{1,0:T(8,128)(2,1)S(1)}, u32[]{:S(2)}, u32[]{:S(2)}) collective-permute-start(bf16[80,4096]{1,0:T(8,128)(2,1)S(1)} %get-tuple-element.68), channel_id=1, source_target_pairs={{0,48},{16,0},{32,16},{48,32},{1,49},{17,1},{33,17},{49,33},{2,50}... | collective-permute-start | bytes 1966088 | tf_op jit(solution)/shard_map/ppermute | solution.py:43
  71.0 27.5 %collective-permute-start.20 = (bf16[640,1792]{1,0:T(8,128)(2,1)S(1)}, bf16[640,1792]{1,0:T(8,128)(2,1)S(1)}, u32[]{:S(2)}, u32[]{:S(2)}) collective-permute-start(bf16[640,1792]{1,0:T(8,128)(2,1)S(1)} %get-tuple-element.95), channel_id=1, source_target_pairs={{0,1},{1,0},{2,3},{3,2},{4,5},{5,4},{6,7},{7,6},{8,9},{9,8},{10,11... | collective-permute-start | bytes 6881288 | tf_op jit(solution)/shard_map/ppermute | solution.py:35
  90.7 7.8 %collective-permute-start.19 = (bf16[640,640]{1,0:T(8,128)(2,1)S(1)}, bf16[640,640]{1,0:T(8,128)(2,1)S(1)}, u32[]{:S(2)}, u32[]{:S(2)}) collective-permute-start(bf16[640,640]{1,0:T(8,128)(2,1)S(1)} %get-tuple-element.93.far), channel_id=1, source_target_pairs={{0,1},{1,0},{2,3},{3,2},{4,5},{5,4},{6,7},{7,6},{8,9},{9,8},{10,11... | collective-permute-start | bytes 2457608 | tf_op jit(solution)/shard_map/ppermute | solution.py:35
  95.7 14.5 %collective-permute-start.21 = (s16[80,2432]{1,0:T(8,128)(2,1)S(1)}, s16[80,2432]{1,0:T(8,128)(2,1)S(1)}, u32[]{:S(2)}, u32[]{:S(2)}) collective-permute-start(s16[80,2432]{1,0:T(8,128)(2,1)S(1)} %get-tuple-element.99), channel_id=1, source_target_pairs={{0,4},{4,8},{8,12},{12,0},{1,5},{5,9},{9,13},{13,1},{2,6},{6,10},{... | collective-permute-start | bytes 1167368 | tf_op jit(solution)/shard_map/ppermute | solution.py:39
  95.8 14.5 %collective-permute-start.22 = (s16[80,2432]{1,0:T(8,128)(2,1)S(1)}, s16[80,2432]{1,0:T(8,128)(2,1)S(1)}, u32[]{:S(2)}, u32[]{:S(2)}) collective-permute-start(s16[80,2432]{1,0:T(8,128)(2,1)S(1)} %get-tuple-element.100), channel_id=1, source_target_pairs={{0,12},{4,0},{8,4},{12,8},{1,13},{5,1},{9,5},{13,9},{2,14},{6,2},{... | collective-permute-start | bytes 1167368 | tf_op jit(solution)/shard_map/ppermute | solution.py:43
  100.1 13.6 %collective-permute-start.25 = (s16[80,1920]{1,0:T(8,128)(2,1)S(1)}, s16[80,1920]{1,0:T(8,128)(2,1)S(1)}, u32[]{:S(2)}, u32[]{:S(2)}) collective-permute-start(s16[80,1920]{1,0:T(8,128)(2,1)S(1)} %get-tuple-element.96), channel_id=1, source_target_pairs={{0,16},{16,32},{32,48},{48,0},{1,17},{17,33},{33,49},{49,1},{2,18}... | collective-permute-start | bytes 921608 | tf_op jit(solution)/shard_map/ppermute | solution.py:39
  104.4 9.3 %collective-permute-start.26 = (s16[80,1920]{1,0:T(8,128)(2,1)S(1)}, s16[80,1920]{1,0:T(8,128)(2,1)S(1)}, u32[]{:S(2)}, u32[]{:S(2)}) collective-permute-start(s16[80,1920]{1,0:T(8,128)(2,1)S(1)} %get-tuple-element.111), channel_id=1, source_target_pairs={{0,48},{16,0},{32,16},{48,32},{1,49},{17,1},{33,17},{49,33},{2,50}... | collective-permute-start | bytes 921608 | tf_op jit(solution)/shard_map/ppermute | solution.py:43
  111.0 19.1 %collective-permute-start.23 = (s16[160,2432]{1,0:T(8,128)(2,1)S(1)}, s16[160,2432]{1,0:T(8,128)(2,1)S(1)}, u32[]{:S(2)}, u32[]{:S(2)}) collective-permute-start(s16[160,2432]{1,0:T(8,128)(2,1)S(1)} %get-tuple-element.109), channel_id=1, source_target_pairs={{0,4},{4,8},{8,12},{12,0},{1,5},{5,9},{9,13},{13,1},{2,6},{6,10},{... | collective-permute-start | bytes 2334728 | tf_op jit(solution)/shard_map/ppermute | solution.py:39
  111.0 19.1 %collective-permute-start.24 = (s16[160,2432]{1,0:T(8,128)(2,1)S(1)}, s16[160,2432]{1,0:T(8,128)(2,1)S(1)}, u32[]{:S(2)}, u32[]{:S(2)}) collective-permute-start(s16[160,2432]{1,0:T(8,128)(2,1)S(1)} %get-tuple-element.110), channel_id=1, source_target_pairs={{0,12},{4,0},{8,4},{12,8},{1,13},{5,1},{9,5},{13,9},{2,14},{6,2},{... | collective-permute-start | bytes 2334728 | tf_op jit(solution)/shard_map/ppermute | solution.py:43
  114.2 15.9 %collective-permute-start.27 = (s16[160,1920]{1,0:T(8,128)(2,1)S(1)}, s16[160,1920]{1,0:T(8,128)(2,1)S(1)}, u32[]{:S(2)}, u32[]{:S(2)}) collective-permute-start(s16[160,1920]{1,0:T(8,128)(2,1)S(1)} %get-tuple-element.116), channel_id=1, source_target_pairs={{0,16},{16,32},{32,48},{48,0},{1,17},{17,33},{33,49},{49,1},{2,18}... | collective-permute-start | bytes 1843208 | tf_op jit(solution)/shard_map/ppermute | solution.py:39
  115.3 14.8 %collective-permute-start.28 = (s16[160,1920]{1,0:T(8,128)(2,1)S(1)}, s16[160,1920]{1,0:T(8,128)(2,1)S(1)}, u32[]{:S(2)}, u32[]{:S(2)}) collective-permute-start(s16[160,1920]{1,0:T(8,128)(2,1)S(1)} %get-tuple-element.117), channel_id=1, source_target_pairs={{0,48},{16,0},{32,16},{48,32},{1,49},{17,1},{33,17},{49,33},{2,50}... | collective-permute-start | bytes 1843208 | tf_op jit(solution)/shard_map/ppermute | solution.py:43
  130.9 22.4 %collective-permute-start.29 = (bf16[80,4096]{1,0:T(8,128)(2,1)S(1)}, bf16[80,4096]{1,0:T(8,128)(2,1)S(1)}, u32[]{:S(2)}, u32[]{:S(2)}) collective-permute-start(bf16[80,4096]{1,0:T(8,128)(2,1)S(1)} %finish.2), channel_id=1, source_target_pairs={{0,0},{1,64},{64,1},{65,65},{2,2},{3,66},{66,3},{67,67},{4,4},{5,6... | collective-permute-start | bytes 1966088 | tf_op jit(solution)/shard_map/ppermute | solution.py:31
  138.8 14.6 %collective-permute-start.30 = (bf16[80,4096]{1,0:T(8,128)(2,1)S(1)}, bf16[80,4096]{1,0:T(8,128)(2,1)S(1)}, u32[]{:S(2)}, u32[]{:S(2)}) collective-permute-start(bf16[80,4096]{1,0:T(8,128)(2,1)S(1)} %finish.3), channel_id=1, source_target_pairs={{0,0},{1,64},{64,1},{65,65},{2,2},{3,66},{66,3},{67,67},{4,4},{5,6... | collective-permute-start | bytes 1966088 | tf_op jit(solution)/shard_map/ppermute | solution.py:31
  140.7 12.6 %collective-permute-start.31 = (f32[1,128]{1,0:T(1,128)S(1)}, f32[1,128]{1,0:T(1,128)S(1)}, u32[]{:S(2)}, u32[]{:S(2)}) collective-permute-start(f32[1,128]{1,0:T(1,128)S(1)} %get-tuple-element.119), channel_id=1, source_target_pairs={{0,0},{1,64},{64,1},{65,65},{2,2},{3,66},{66,3},{67,67},{4,4},{5,6... | collective-permute-start | bytes 1544 | tf_op jit(solution)/shard_map/ppermute | solution.py:31
  144.4 8.9 %collective-permute-start.32 = (f32[1,128]{1,0:T(1,128)S(1)}, f32[1,128]{1,0:T(1,128)S(1)}, u32[]{:S(2)}, u32[]{:S(2)}) collective-permute-start(f32[1,128]{1,0:T(1,128)S(1)} %get-tuple-element.119), channel_id=1, source_target_pairs={{1,0},{65,1},{0,64},{64,65},{3,2},{67,3},{2,66},{66,67},{5,4},{69,... | collective-permute-start | bytes 1544 | tf_op jit(solution)/shard_map/ppermute | solution.py:452
  (11 other events, 50.3 us)
